TPU v7x, 512 devices: a whole 4x8x8 slice. The times are simulated.
512 devices in a mesh: tm: 16 (over y, x_hi), space: 32 (over z, x_lo, core).
Axes of the slice: x: 4 (x_hi: 2, x_lo: 2; x = x_hi * 2 + x_lo), y: 8, z: 8, core: 2. Of those that a mesh axis runs over, the one named last changes fastest.
Arguments:
- states: float32 [16, 3, 2, 128, 128, 128], P('tm', None, None, 'space'), may hold values from 0 to 1
- first_start: float32 [2, 128, 128, 128], P(None, 'space'), may hold values from 0 to 1
Outputs:
- next_states: float32 [16, 3, 2, 128, 128, 128], P('tm', None, None, 'space')
All inputs are finite; a program needn't handle non-finite values.
Results may differ from a plain program's by a relative error of at most 0.00002.
Values sent between devices are 32-bit elements; how exact they have to be, the bound alone decides.
No kernel may reach another device: no remote copies, remote signals or barrier semaphores. Data moves between devices by JAX's collectives and lax.ppermute only.
A program may use at most 64 MiB of HBM per device.

v0:
```python
import jax
import jax.numpy as jnp
from jax import lax
from jax.sharding import PartitionSpec as P

step_time = 0.25
half_step = 0.125
diffuse_fast = 0.6
diffuse_slow = 0.3
feed_rate = 0.04
kill_rate = 0.06
sweep_weights = ((5.0 / 24.0, 1.0 / 3.0, -1.0 / 24.0), (-1.0 / 24.0, 1.0 / 3.0, 5.0 / 24.0))


def padded_2(cells, sides, width):
    for axis, dim in sides:
        count = lax.axis_size(axis)
        head = lax.slice_in_dim(cells, 0, width, axis=dim)
        tail = lax.slice_in_dim(cells, cells.shape[dim] - width, cells.shape[dim], axis=dim)
        cells = jnp.concatenate(
            [
                lax.ppermute(tail, axis, [(i, (i + 1) % count) for i in range(count)]),
                cells,
                lax.ppermute(head, axis, [((i + 1) % count, i) for i in range(count)]),
            ],
            axis=dim,
        )
    return cells


def passed_along(block, axis, distance):
    devices = range(lax.axis_size(axis))
    route = [(i - distance, i) for i in devices if i - distance in devices]
    return lax.ppermute(block, axis, route)


def laplace_padded(padded):
    middle = padded[..., 1:-1, :, :]
    total = padded[..., 2:, :, :] + padded[..., :-2, :, :]
    total = total + jnp.roll(middle, 1, -2) + jnp.roll(middle, -1, -2)
    total = total + jnp.roll(middle, 1, -1) + jnp.roll(middle, -1, -1)
    return total - 6.0 * middle


def reaction_rates(padded):
    middle = padded[..., 1:-1, :, :]
    substrate = middle[..., 0, :, :, :]
    catalyst = middle[..., 1, :, :, :]
    product = substrate * catalyst * catalyst
    rate_sub = (
        diffuse_fast * laplace_padded(padded[..., 0, :, :, :])
        - product
        + feed_rate * (1.0 - substrate)
    )
    rate_cat = (
        diffuse_slow * laplace_padded(padded[..., 1, :, :, :])
        + product
        - (feed_rate + kill_rate) * catalyst
    )
    return jnp.stack([rate_sub, rate_cat], axis=-4)


def local(states, first_start):
    current_slab = states[0]
    leading = lax.axis_index("tm") == 0
    trailing = lax.axis_index("tm") == lax.axis_size("tm") - 1
    padded_old = padded_2(current_slab, (("space", 2),), 1)
    previous = reaction_rates(padded_old)
    arrived = passed_along(current_slab[2], "tm", 1)
    slab_start = jnp.where(leading, first_start, arrived)
    fine_states = [slab_start]
    fine_rates = []
    current = slab_start
    for level_node in range(3):
        padded = padded_2(current, (("space", 1),), 1)
        node_rate = reaction_rates(padded)
        fine_rates.append(node_rate)
        if level_node < 2:
            weights = sweep_weights[level_node]
            current = (
                current
                + half_step * (node_rate - previous[level_node])
                + step_time
                * (weights[0] * previous[0] + weights[1] * previous[1] + weights[2] * previous[2])
            )
            fine_states.append(current)
    rate_zero, rate_one, rate_two = fine_rates
    offset = step_time * 0.5 * (rate_two - rate_zero) + step_time * (
        2.0 / 3.0 * rate_one - 1.0 / 3.0 * rate_zero - 1.0 / 3.0 * rate_two
    )
    coarse_end = slab_start + step_time * rate_zero + offset
    turns = lax.axis_size("tm") - 1

    def chain_turn(index, carry):
        coarse_start, coarse_last = carry
        passed = passed_along(coarse_last, "tm", 1)
        coarse_start = jnp.where(leading, first_start, passed)
        padded = padded_2(coarse_start, (("space", 1),), 1)
        return (coarse_start, coarse_start + step_time * reaction_rates(padded) + offset)

    coarse_start, coarse_end = lax.fori_loop(0, turns, chain_turn, (slab_start, coarse_end))
    middle = fine_states[1] + 0.5 * (coarse_start - fine_states[0] + (coarse_end - fine_states[2]))
    updated = jnp.stack([coarse_start, middle, coarse_end])
    moved = passed_along(updated, "tm", -1)
    replaced = jnp.stack([coarse_end, coarse_end, coarse_end])
    result = jnp.where(trailing, replaced, moved)
    return result[None]


def solution(mesh):
    return jax.shard_map(
        local,
        mesh=mesh,
        in_specs=(P("tm", None, None, "space", None, None), P(None, "space", None, None)),
        out_specs=P("tm", None, None, "space", None, None),
        check_vma=False,
    )
```

profile of v0, /device:TPU:220, one launch (start us, length us, event | category | flops | bytes accessed | tf_op | source)
XLA Modules:
  0.0 568.2 jit_solution(9031884752949474335)
XLA Ops:
  20.8 9.3 %collective-permute-done.3 = f32[2,4,128,128]{3,2,1,0:T(8,128)S(1)} collective-permute-done((f32[2,4,128,128]{3,2,1,0:T(8,128)S(1)}, f32[2,4,128,128]{3,2,1,0:T(8,128)S(1)}, u32[]{:S(2)}, u32[]{:S(2)}) %collective-permute-start.3) | collective-permute-done | bytes 524320 | tf_op jit(solution)/shard_map/ppermute | solution.py:34
  63.8 457.6 %while.12 = (s32[]{:T(128)}, f32[2,4,128,128]{3,2,1,0:T(8,128)}, f32[2,4,128,128]{3,2,1,0:T(8,128)}, pred[]{:T(512)}, f32[2,4,128,128]{3,2,1,0:T(8,128)S(1)}, /*index=5*/f32[2,4,128,128]{3,2,1,0:T(8,128)S(1)}, s32[]{:T(128)}) while((s32[]{:T(128)}, f32[2,4,128,128]{3,2,1,0:T(8,128)}, f32[2,4,128,128]{3,2,1,0:T(8,128)}, pred[]{:T(512)}, ...), condition=%wide.region_1.2_spmd, body=%wide.region_0.1_spmd.sunk | while | flops 3211266 | bytes 20717792 | solution.py:101
  70.8 10.7 %collective-permute-done = f32[2,4,128,128]{3,2,1,0:T(8,128)S(1)} collective-permute-done((f32[2,4,128,128]{3,2,1,0:T(8,128)}, f32[2,4,128,128]{3,2,1,0:T(8,128)S(1)}, u32[]{:S(2)}, u32[]{:S(2)}) %collective-permute-start) | collective-permute-done | bytes 524320 | tf_op jit(solution)/shard_map/while/body/eval_jaxpr/ppermute | solution.py:34
  100.7 11.5 %collective-permute-done = f32[2,4,128,128]{3,2,1,0:T(8,128)S(1)} collective-permute-done((f32[2,4,128,128]{3,2,1,0:T(8,128)}, f32[2,4,128,128]{3,2,1,0:T(8,128)S(1)}, u32[]{:S(2)}, u32[]{:S(2)}) %collective-permute-start) | collective-permute-done | bytes 524320 | tf_op jit(solution)/shard_map/while/body/eval_jaxpr/ppermute | solution.py:34
  123.5 7.9 %collective-permute-start = (f32[2,4,128,128]{3,2,1,0:T(8,128)}, f32[2,4,128,128]{3,2,1,0:T(8,128)S(1)}, u32[]{:S(2)}, u32[]{:S(2)}) collective-permute-start(f32[2,4,128,128]{3,2,1,0:T(8,128)} %get-tuple-element.245), channel_id=1, source_target_pairs={{0,32},{32,64},{64,96},{96,128},{128,160},{160,192},{192,224},{224... | collective-permute-start | bytes 1572872 | tf_op jit(solution)/shard_map/while/body/eval_jaxpr/ppermute | solution.py:34
  131.4 12.1 %collective-permute-done = f32[2,4,128,128]{3,2,1,0:T(8,128)S(1)} collective-permute-done((f32[2,4,128,128]{3,2,1,0:T(8,128)}, f32[2,4,128,128]{3,2,1,0:T(8,128)S(1)}, u32[]{:S(2)}, u32[]{:S(2)}) %collective-permute-start) | collective-permute-done | bytes 524320 | tf_op jit(solution)/shard_map/while/body/eval_jaxpr/ppermute | solution.py:34
  154.8 7.9 %collective-permute-start = (f32[2,4,128,128]{3,2,1,0:T(8,128)}, f32[2,4,128,128]{3,2,1,0:T(8,128)S(1)}, u32[]{:S(2)}, u32[]{:S(2)}) collective-permute-start(f32[2,4,128,128]{3,2,1,0:T(8,128)} %get-tuple-element.245), channel_id=1, source_target_pairs={{0,32},{32,64},{64,96},{96,128},{128,160},{160,192},{192,224},{224... | collective-permute-start | bytes 1572872 | tf_op jit(solution)/shard_map/while/body/eval_jaxpr/ppermute | solution.py:34
  162.7 11.1 %collective-permute-done = f32[2,4,128,128]{3,2,1,0:T(8,128)S(1)} collective-permute-done((f32[2,4,128,128]{3,2,1,0:T(8,128)}, f32[2,4,128,128]{3,2,1,0:T(8,128)S(1)}, u32[]{:S(2)}, u32[]{:S(2)}) %collective-permute-start) | collective-permute-done | bytes 524320 | tf_op jit(solution)/shard_map/while/body/eval_jaxpr/ppermute | solution.py:34
  192.9 11.1 %collective-permute-done = f32[2,4,128,128]{3,2,1,0:T(8,128)S(1)} collective-permute-done((f32[2,4,128,128]{3,2,1,0:T(8,128)}, f32[2,4,128,128]{3,2,1,0:T(8,128)S(1)}, u32[]{:S(2)}, u32[]{:S(2)}) %collective-permute-start) | collective-permute-done | bytes 524320 | tf_op jit(solution)/shard_map/while/body/eval_jaxpr/ppermute | solution.py:34
  215.3 7.9 %collective-permute-start = (f32[2,4,128,128]{3,2,1,0:T(8,128)}, f32[2,4,128,128]{3,2,1,0:T(8,128)S(1)}, u32[]{:S(2)}, u32[]{:S(2)}) collective-permute-start(f32[2,4,128,128]{3,2,1,0:T(8,128)} %get-tuple-element.245), channel_id=1, source_target_pairs={{0,32},{32,64},{64,96},{96,128},{128,160},{160,192},{192,224},{224... | collective-permute-start | bytes 1572872 | tf_op jit(solution)/shard_map/while/body/eval_jaxpr/ppermute | solution.py:34
  223.2 11.7 %collective-permute-done = f32[2,4,128,128]{3,2,1,0:T(8,128)S(1)} collective-permute-done((f32[2,4,128,128]{3,2,1,0:T(8,128)}, f32[2,4,128,128]{3,2,1,0:T(8,128)S(1)}, u32[]{:S(2)}, u32[]{:S(2)}) %collective-permute-start) | collective-permute-done | bytes 524320 | tf_op jit(solution)/shard_map/while/body/eval_jaxpr/ppermute | solution.py:34
  246.2 7.9 %collective-permute-start = (f32[2,4,128,128]{3,2,1,0:T(8,128)}, f32[2,4,128,128]{3,2,1,0:T(8,128)S(1)}, u32[]{:S(2)}, u32[]{:S(2)}) collective-permute-start(f32[2,4,128,128]{3,2,1,0:T(8,128)} %get-tuple-element.245), channel_id=1, source_target_pairs={{0,32},{32,64},{64,96},{96,128},{128,160},{160,192},{192,224},{224... | collective-permute-start | bytes 1572872 | tf_op jit(solution)/shard_map/while/body/eval_jaxpr/ppermute | solution.py:34
  254.1 12.3 %collective-permute-done = f32[2,4,128,128]{3,2,1,0:T(8,128)S(1)} collective-permute-done((f32[2,4,128,128]{3,2,1,0:T(8,128)}, f32[2,4,128,128]{3,2,1,0:T(8,128)S(1)}, u32[]{:S(2)}, u32[]{:S(2)}) %collective-permute-start) | collective-permute-done | bytes 524320 | tf_op jit(solution)/shard_map/while/body/eval_jaxpr/ppermute | solution.py:34
  285.6 12.0 %collective-permute-done = f32[2,4,128,128]{3,2,1,0:T(8,128)S(1)} collective-permute-done((f32[2,4,128,128]{3,2,1,0:T(8,128)}, f32[2,4,128,128]{3,2,1,0:T(8,128)S(1)}, u32[]{:S(2)}, u32[]{:S(2)}) %collective-permute-start) | collective-permute-done | bytes 524320 | tf_op jit(solution)/shard_map/while/body/eval_jaxpr/ppermute | solution.py:34
  316.8 11.1 %collective-permute-done = f32[2,4,128,128]{3,2,1,0:T(8,128)S(1)} collective-permute-done((f32[2,4,128,128]{3,2,1,0:T(8,128)}, f32[2,4,128,128]{3,2,1,0:T(8,128)S(1)}, u32[]{:S(2)}, u32[]{:S(2)}) %collective-permute-start) | collective-permute-done | bytes 524320 | tf_op jit(solution)/shard_map/while/body/eval_jaxpr/ppermute | solution.py:34
  347.1 11.1 %collective-permute-done = f32[2,4,128,128]{3,2,1,0:T(8,128)S(1)} collective-permute-done((f32[2,4,128,128]{3,2,1,0:T(8,128)}, f32[2,4,128,128]{3,2,1,0:T(8,128)S(1)}, u32[]{:S(2)}, u32[]{:S(2)}) %collective-permute-start) | collective-permute-done | bytes 524320 | tf_op jit(solution)/shard_map/while/body/eval_jaxpr/ppermute | solution.py:34
  369.5 7.9 %collective-permute-start = (f32[2,4,128,128]{3,2,1,0:T(8,128)}, f32[2,4,128,128]{3,2,1,0:T(8,128)S(1)}, u32[]{:S(2)}, u32[]{:S(2)}) collective-permute-start(f32[2,4,128,128]{3,2,1,0:T(8,128)} %get-tuple-element.245), channel_id=1, source_target_pairs={{0,32},{32,64},{64,96},{96,128},{128,160},{160,192},{192,224},{224... | collective-permute-start | bytes 1572872 | tf_op jit(solution)/shard_map/while/body/eval_jaxpr/ppermute | solution.py:34
  377.4 11.1 %collective-permute-done = f32[2,4,128,128]{3,2,1,0:T(8,128)S(1)} collective-permute-done((f32[2,4,128,128]{3,2,1,0:T(8,128)}, f32[2,4,128,128]{3,2,1,0:T(8,128)S(1)}, u32[]{:S(2)}, u32[]{:S(2)}) %collective-permute-start) | collective-permute-done | bytes 524320 | tf_op jit(solution)/shard_map/while/body/eval_jaxpr/ppermute | solution.py:34
  407.7 11.1 %collective-permute-done = f32[2,4,128,128]{3,2,1,0:T(8,128)S(1)} collective-permute-done((f32[2,4,128,128]{3,2,1,0:T(8,128)}, f32[2,4,128,128]{3,2,1,0:T(8,128)S(1)}, u32[]{:S(2)}, u32[]{:S(2)}) %collective-permute-start) | collective-permute-done | bytes 524320 | tf_op jit(solution)/shard_map/while/body/eval_jaxpr/ppermute | solution.py:34
  430.1 7.9 %collective-permute-start = (f32[2,4,128,128]{3,2,1,0:T(8,128)}, f32[2,4,128,128]{3,2,1,0:T(8,128)S(1)}, u32[]{:S(2)}, u32[]{:S(2)}) collective-permute-start(f32[2,4,128,128]{3,2,1,0:T(8,128)} %get-tuple-element.245), channel_id=1, source_target_pairs={{0,32},{32,64},{64,96},{96,128},{128,160},{160,192},{192,224},{224... | collective-permute-start | bytes 1572872 | tf_op jit(solution)/shard_map/while/body/eval_jaxpr/ppermute | solution.py:34
  438.0 11.1 %collective-permute-done = f32[2,4,128,128]{3,2,1,0:T(8,128)S(1)} collective-permute-done((f32[2,4,128,128]{3,2,1,0:T(8,128)}, f32[2,4,128,128]{3,2,1,0:T(8,128)S(1)}, u32[]{:S(2)}, u32[]{:S(2)}) %collective-permute-start) | collective-permute-done | bytes 524320 | tf_op jit(solution)/shard_map/while/body/eval_jaxpr/ppermute | solution.py:34
  468.3 11.1 %collective-permute-done = f32[2,4,128,128]{3,2,1,0:T(8,128)S(1)} collective-permute-done((f32[2,4,128,128]{3,2,1,0:T(8,128)}, f32[2,4,128,128]{3,2,1,0:T(8,128)S(1)}, u32[]{:S(2)}, u32[]{:S(2)}) %collective-permute-start) | collective-permute-done | bytes 524320 | tf_op jit(solution)/shard_map/while/body/eval_jaxpr/ppermute | solution.py:34
  498.6 11.6 %collective-permute-done = f32[2,4,128,128]{3,2,1,0:T(8,128)S(1)} collective-permute-done((f32[2,4,128,128]{3,2,1,0:T(8,128)}, f32[2,4,128,128]{3,2,1,0:T(8,128)S(1)}, u32[]{:S(2)}, u32[]{:S(2)}) %collective-permute-start) | collective-permute-done | bytes 524320 | tf_op jit(solution)/shard_map/while/body/eval_jaxpr/ppermute | solution.py:34
  525.1 40.4 %collective-permute-done.12 = f32[3,2,4,128,128]{4,3,2,1,0:T(8,128)} collective-permute-done((f32[3,2,4,128,128]{4,3,2,1,0:T(8,128)S(1)}, f32[3,2,4,128,128]{4,3,2,1,0:T(8,128)}, u32[]{:S(2)}, u32[]{:S(2)}) %collective-permute-start.12) | collective-permute-done | bytes 1572896 | tf_op jit(solution)/shard_map/ppermute | solution.py:34
  (388 shorter events, 298.3 us)
Async XLA Ops:
  2.5 12.2 %collective-permute-start.6 = (f32[3,2,1,128,128]{4,3,2,0,1:T(8,128)}, f32[3,2,1,128,128]{4,3,2,0,1:T(8,128)S(1)}, u32[]{:S(2)}, u32[]{:S(2)}) collective-permute-start(f32[3,2,1,128,128]{4,3,2,0,1:T(8,128)} %get-tuple-element.75), channel_id=1, source_target_pairs={{0,1},{1,2},{2,3},{3,4},{4,5},{5,6},{6,7},{7,8},{8,9},{9,10},{10,1... | collective-permute-start | bytes 1179656 | tf_op jit(solution)/shard_map/ppermute | solution.py:22
  4.4 12.9 %collective-permute-start.7 = (f32[3,2,1,128,128]{4,3,2,0,1:T(8,128)}, f32[3,2,1,128,128]{4,3,2,0,1:T(8,128)S(1)}, u32[]{:S(2)}, u32[]{:S(2)}) collective-permute-start(f32[3,2,1,128,128]{4,3,2,0,1:T(8,128)} %get-tuple-element.76), channel_id=1, source_target_pairs={{1,0},{2,1},{3,2},{4,3},{5,4},{6,5},{7,6},{8,7},{9,8},{10,9},{11,1... | collective-permute-start | bytes 1179656 | tf_op jit(solution)/shard_map/ppermute | solution.py:24
  10.0 20.1 %collective-permute-start.3 = (f32[2,4,128,128]{3,2,1,0:T(8,128)S(1)}, f32[2,4,128,128]{3,2,1,0:T(8,128)S(1)}, u32[]{:S(2)}, u32[]{:S(2)}) collective-permute-start(f32[2,4,128,128]{3,2,1,0:T(8,128)S(1)} %slice_bitcast_fusion.22), channel_id=1, source_target_pairs={{0,32},{32,64},{64,96},{96,128},{128,160},{160,192},{192,224},{224... | collective-permute-start | bytes 1572872 | tf_op jit(solution)/shard_map/ppermute | solution.py:34
  33.3 7.3 %collective-permute-start.5 = (f32[2,1,128,128]{3,2,1,0:T(8,128)S(1)}, f32[2,1,128,128]{3,2,1,0:T(8,128)S(1)}, u32[]{:S(2)}, u32[]{:S(2)}) collective-permute-start(f32[2,1,128,128]{3,2,1,0:T(8,128)S(1)} %get-tuple-element.104), channel_id=1, source_target_pairs={{0,1},{1,2},{2,3},{3,4},{4,5},{5,6},{6,7},{7,8},{8,9},{9,10},{10,1... | collective-permute-start | bytes 393224 | tf_op jit(solution)/shard_map/ppermute | solution.py:22
  63.8 17.6 %collective-permute-start = (f32[2,4,128,128]{3,2,1,0:T(8,128)}, f32[2,4,128,128]{3,2,1,0:T(8,128)S(1)}, u32[]{:S(2)}, u32[]{:S(2)}) collective-permute-start(f32[2,4,128,128]{3,2,1,0:T(8,128)} %get-tuple-element.245), channel_id=1, source_target_pairs={{0,32},{32,64},{64,96},{96,128},{128,160},{160,192},{192,224},{224... | collective-permute-start | bytes 1572872 | tf_op jit(solution)/shard_map/while/body/eval_jaxpr/ppermute | solution.py:34
  92.8 19.4 %collective-permute-start = (f32[2,4,128,128]{3,2,1,0:T(8,128)}, f32[2,4,128,128]{3,2,1,0:T(8,128)S(1)}, u32[]{:S(2)}, u32[]{:S(2)}) collective-permute-start(f32[2,4,128,128]{3,2,1,0:T(8,128)} %get-tuple-element.245), channel_id=1, source_target_pairs={{0,32},{32,64},{64,96},{96,128},{128,160},{160,192},{192,224},{224... | collective-permute-start | bytes 1572872 | tf_op jit(solution)/shard_map/while/body/eval_jaxpr/ppermute | solution.py:34
  123.5 20.0 %collective-permute-start = (f32[2,4,128,128]{3,2,1,0:T(8,128)}, f32[2,4,128,128]{3,2,1,0:T(8,128)S(1)}, u32[]{:S(2)}, u32[]{:S(2)}) collective-permute-start(f32[2,4,128,128]{3,2,1,0:T(8,128)} %get-tuple-element.245), channel_id=1, source_target_pairs={{0,32},{32,64},{64,96},{96,128},{128,160},{160,192},{192,224},{224... | collective-permute-start | bytes 1572872 | tf_op jit(solution)/shard_map/while/body/eval_jaxpr/ppermute | solution.py:34
  143.9 7.2 %collective-permute-start.1 = (f32[2,1,128,128]{3,2,1,0:T(8,128)S(1)}, f32[2,1,128,128]{3,2,1,0:T(8,128)S(1)}, u32[]{:S(2)}, u32[]{:S(2)}) collective-permute-start(f32[2,1,128,128]{3,2,1,0:T(8,128)S(1)} %get-tuple-element.216), channel_id=1, source_target_pairs={{0,1},{1,2},{2,3},{3,4},{4,5},{5,6},{6,7},{7,8},{8,9},{9,10},{10,1... | collective-permute-start | bytes 393224 | tf_op jit(solution)/shard_map/while/body/eval_jaxpr/ppermute | solution.py:22
  154.8 19.0 %collective-permute-start = (f32[2,4,128,128]{3,2,1,0:T(8,128)}, f32[2,4,128,128]{3,2,1,0:T(8,128)S(1)}, u32[]{:S(2)}, u32[]{:S(2)}) collective-permute-start(f32[2,4,128,128]{3,2,1,0:T(8,128)} %get-tuple-element.245), channel_id=1, source_target_pairs={{0,32},{32,64},{64,96},{96,128},{128,160},{160,192},{192,224},{224... | collective-permute-start | bytes 1572872 | tf_op jit(solution)/shard_map/while/body/eval_jaxpr/ppermute | solution.py:34
  185.0 19.0 %collective-permute-start = (f32[2,4,128,128]{3,2,1,0:T(8,128)}, f32[2,4,128,128]{3,2,1,0:T(8,128)S(1)}, u32[]{:S(2)}, u32[]{:S(2)}) collective-permute-start(f32[2,4,128,128]{3,2,1,0:T(8,128)} %get-tuple-element.245), channel_id=1, source_target_pairs={{0,32},{32,64},{64,96},{96,128},{128,160},{160,192},{192,224},{224... | collective-permute-start | bytes 1572872 | tf_op jit(solution)/shard_map/while/body/eval_jaxpr/ppermute | solution.py:34
  215.3 19.6 %collective-permute-start = (f32[2,4,128,128]{3,2,1,0:T(8,128)}, f32[2,4,128,128]{3,2,1,0:T(8,128)S(1)}, u32[]{:S(2)}, u32[]{:S(2)}) collective-permute-start(f32[2,4,128,128]{3,2,1,0:T(8,128)} %get-tuple-element.245), channel_id=1, source_target_pairs={{0,32},{32,64},{64,96},{96,128},{128,160},{160,192},{192,224},{224... | collective-permute-start | bytes 1572872 | tf_op jit(solution)/shard_map/while/body/eval_jaxpr/ppermute | solution.py:34
  246.2 20.2 %collective-permute-start = (f32[2,4,128,128]{3,2,1,0:T(8,128)}, f32[2,4,128,128]{3,2,1,0:T(8,128)S(1)}, u32[]{:S(2)}, u32[]{:S(2)}) collective-permute-start(f32[2,4,128,128]{3,2,1,0:T(8,128)} %get-tuple-element.245), channel_id=1, source_target_pairs={{0,32},{32,64},{64,96},{96,128},{128,160},{160,192},{192,224},{224... | collective-permute-start | bytes 1572872 | tf_op jit(solution)/shard_map/while/body/eval_jaxpr/ppermute | solution.py:34
  268.8 7.4 %collective-permute-start.2 = (f32[2,1,128,128]{3,2,1,0:T(8,128)S(1)}, f32[2,1,128,128]{3,2,1,0:T(8,128)S(1)}, u32[]{:S(2)}, u32[]{:S(2)}) collective-permute-start(f32[2,1,128,128]{3,2,1,0:T(8,128)S(1)} %get-tuple-element.217), channel_id=1, source_target_pairs={{1,0},{2,1},{3,2},{4,3},{5,4},{6,5},{7,6},{8,7},{9,8},{10,9},{11,1... | collective-permute-start | bytes 393224 | tf_op jit(solution)/shard_map/while/body/eval_jaxpr/ppermute | solution.py:24
  278.1 19.5 %collective-permute-start = (f32[2,4,128,128]{3,2,1,0:T(8,128)}, f32[2,4,128,128]{3,2,1,0:T(8,128)S(1)}, u32[]{:S(2)}, u32[]{:S(2)}) collective-permute-start(f32[2,4,128,128]{3,2,1,0:T(8,128)} %get-tuple-element.245), channel_id=1, source_target_pairs={{0,32},{32,64},{64,96},{96,128},{128,160},{160,192},{192,224},{224... | collective-permute-start | bytes 1572872 | tf_op jit(solution)/shard_map/while/body/eval_jaxpr/ppermute | solution.py:34
  298.1 7.2 %collective-permute-start.1 = (f32[2,1,128,128]{3,2,1,0:T(8,128)S(1)}, f32[2,1,128,128]{3,2,1,0:T(8,128)S(1)}, u32[]{:S(2)}, u32[]{:S(2)}) collective-permute-start(f32[2,1,128,128]{3,2,1,0:T(8,128)S(1)} %get-tuple-element.216), channel_id=1, source_target_pairs={{0,1},{1,2},{2,3},{3,4},{4,5},{5,6},{6,7},{7,8},{8,9},{9,10},{10,1... | collective-permute-start | bytes 393224 | tf_op jit(solution)/shard_map/while/body/eval_jaxpr/ppermute | solution.py:22
  300.0 7.4 %collective-permute-start.2 = (f32[2,1,128,128]{3,2,1,0:T(8,128)S(1)}, f32[2,1,128,128]{3,2,1,0:T(8,128)S(1)}, u32[]{:S(2)}, u32[]{:S(2)}) collective-permute-start(f32[2,1,128,128]{3,2,1,0:T(8,128)S(1)} %get-tuple-element.217), channel_id=1, source_target_pairs={{1,0},{2,1},{3,2},{4,3},{5,4},{6,5},{7,6},{8,7},{9,8},{10,9},{11,1... | collective-permute-start | bytes 393224 | tf_op jit(solution)/shard_map/while/body/eval_jaxpr/ppermute | solution.py:24
  309.3 18.6 %collective-permute-start = (f32[2,4,128,128]{3,2,1,0:T(8,128)}, f32[2,4,128,128]{3,2,1,0:T(8,128)S(1)}, u32[]{:S(2)}, u32[]{:S(2)}) collective-permute-start(f32[2,4,128,128]{3,2,1,0:T(8,128)} %get-tuple-element.245), channel_id=1, source_target_pairs={{0,32},{32,64},{64,96},{96,128},{128,160},{160,192},{192,224},{224... | collective-permute-start | bytes 1572872 | tf_op jit(solution)/shard_map/while/body/eval_jaxpr/ppermute | solution.py:34
  339.2 19.0 %collective-permute-start = (f32[2,4,128,128]{3,2,1,0:T(8,128)}, f32[2,4,128,128]{3,2,1,0:T(8,128)S(1)}, u32[]{:S(2)}, u32[]{:S(2)}) collective-permute-start(f32[2,4,128,128]{3,2,1,0:T(8,128)} %get-tuple-element.245), channel_id=1, source_target_pairs={{0,32},{32,64},{64,96},{96,128},{128,160},{160,192},{192,224},{224... | collective-permute-start | bytes 1572872 | tf_op jit(solution)/shard_map/while/body/eval_jaxpr/ppermute | solution.py:34
  369.5 19.0 %collective-permute-start = (f32[2,4,128,128]{3,2,1,0:T(8,128)}, f32[2,4,128,128]{3,2,1,0:T(8,128)S(1)}, u32[]{:S(2)}, u32[]{:S(2)}) collective-permute-start(f32[2,4,128,128]{3,2,1,0:T(8,128)} %get-tuple-element.245), channel_id=1, source_target_pairs={{0,32},{32,64},{64,96},{96,128},{128,160},{160,192},{192,224},{224... | collective-permute-start | bytes 1572872 | tf_op jit(solution)/shard_map/while/body/eval_jaxpr/ppermute | solution.py:34
  399.8 19.0 %collective-permute-start = (f32[2,4,128,128]{3,2,1,0:T(8,128)}, f32[2,4,128,128]{3,2,1,0:T(8,128)S(1)}, u32[]{:S(2)}, u32[]{:S(2)}) collective-permute-start(f32[2,4,128,128]{3,2,1,0:T(8,128)} %get-tuple-element.245), channel_id=1, source_target_pairs={{0,32},{32,64},{64,96},{96,128},{128,160},{160,192},{192,224},{224... | collective-permute-start | bytes 1572872 | tf_op jit(solution)/shard_map/while/body/eval_jaxpr/ppermute | solution.py:34
  430.1 19.0 %collective-permute-start = (f32[2,4,128,128]{3,2,1,0:T(8,128)}, f32[2,4,128,128]{3,2,1,0:T(8,128)S(1)}, u32[]{:S(2)}, u32[]{:S(2)}) collective-permute-start(f32[2,4,128,128]{3,2,1,0:T(8,128)} %get-tuple-element.245), channel_id=1, source_target_pairs={{0,32},{32,64},{64,96},{96,128},{128,160},{160,192},{192,224},{224... | collective-permute-start | bytes 1572872 | tf_op jit(solution)/shard_map/while/body/eval_jaxpr/ppermute | solution.py:34
  460.4 19.0 %collective-permute-start = (f32[2,4,128,128]{3,2,1,0:T(8,128)}, f32[2,4,128,128]{3,2,1,0:T(8,128)S(1)}, u32[]{:S(2)}, u32[]{:S(2)}) collective-permute-start(f32[2,4,128,128]{3,2,1,0:T(8,128)} %get-tuple-element.245), channel_id=1, source_target_pairs={{0,32},{32,64},{64,96},{96,128},{128,160},{160,192},{192,224},{224... | collective-permute-start | bytes 1572872 | tf_op jit(solution)/shard_map/while/body/eval_jaxpr/ppermute | solution.py:34
  490.7 19.5 %collective-permute-start = (f32[2,4,128,128]{3,2,1,0:T(8,128)}, f32[2,4,128,128]{3,2,1,0:T(8,128)S(1)}, u32[]{:S(2)}, u32[]{:S(2)}) collective-permute-start(f32[2,4,128,128]{3,2,1,0:T(8,128)} %get-tuple-element.245), channel_id=1, source_target_pairs={{0,32},{32,64},{64,96},{96,128},{128,160},{160,192},{192,224},{224... | collective-permute-start | bytes 1572872 | tf_op jit(solution)/shard_map/while/body/eval_jaxpr/ppermute | solution.py:34
  523.1 42.4 %collective-permute-start.12 = (f32[3,2,4,128,128]{4,3,2,1,0:T(8,128)S(1)}, f32[3,2,4,128,128]{4,3,2,1,0:T(8,128)}, u32[]{:S(2)}, u32[]{:S(2)}) collective-permute-start(f32[3,2,4,128,128]{4,3,2,1,0:T(8,128)S(1)} %pad_maximum_fusion.3), channel_id=1, source_target_pairs={{32,0},{64,32},{96,64},{128,96},{160,128},{192,160},{224,192},{256... | collective-permute-start | bytes 4718600 | tf_op jit(solution)/shard_map/ppermute | solution.py:34
  (49 other events, 381.4 us)
where the time goes:
time: 571 us; the launch traced here: 568 us
  waiting for transfers between devices  274 us (48%)
  starting transfers between devices  241 us (42%)
  other arithmetic  33.2 us (6%)
  local copies, waits for them, and re-layouts  17.8 us (3%)
    ppermute x17, waiting for transfers between devices, passed_along(): return lax.ppermute(block, axis, route)  220 us
    ppermute x17, starting transfers between devices, passed_along(): return lax.ppermute(block, axis, route)  123 us
    ppermute x19, starting transfers between devices, padded_2(): lax.ppermute(head, axis, [((i + 1) % count, i) for i in range(count)])  77.2 us
    ppermute x19, starting transfers between devices, padded_2(): lax.ppermute(tail, axis, [(i, (i + 1) % count) for i in range(count)])  40.4 us
    ppermute x19, waiting for transfers between devices, padded_2(): lax.ppermute(head, axis, [((i + 1) % count, i) for i in range(count)])  30.3 us
    ppermute x19, waiting for transfers between devices, padded_2(): lax.ppermute(tail, axis, [(i, (i + 1) % count) for i in range(count)])  23.5 us
    add x15, other arithmetic, chain_turn(): coarse_start + step_time * reaction_rates(padded) + offset  13.9 us
  transfers between devices with their start and end apart: 55, of which 53 were waited for; matrix products, arithmetic and copies ran while one was open for 1% of the time, Pallas kernels for 0%

commit v1 on v0

v1 whole, which is shorter than its diff:
```python
import functools

import jax
import jax.numpy as jnp
from jax import lax
from jax.experimental import pallas as pl
from jax.experimental.pallas import tpu as pltpu
from jax.sharding import PartitionSpec as P

step_time = 0.25
half_step = 0.125
diffuse = (0.6, 0.3)
feed_rate = 0.04
kill_rate = 0.06
sweep_weights = ((5.0 / 24.0, 1.0 / 3.0, -1.0 / 24.0), (-1.0 / 24.0, 1.0 / 3.0, 5.0 / 24.0))
old_weights = (
    (step_time * 5.0 / 24.0 - half_step, step_time / 3.0, -step_time / 24.0),
    (-step_time / 24.0, step_time / 3.0 - half_step, step_time * 5.0 / 24.0),
)
new_weights = (
    -0.5 * step_time - step_time / 3.0,
    step_time * 2.0 / 3.0,
    0.5 * step_time - step_time / 3.0,
)
rows_each = 8
block_len = 4
half_rows = 4
vmem_bytes = 16 * 1024 * 1024


def rank_of(index, count):
    return index // 2 if index % 2 == 0 else count - 1 - index // 2


def index_of(rank, count):
    return 2 * rank if rank < count // 2 else 2 * (count - 1 - rank) + 1


def chain_blocks(count):
    blocks, first = [], 1
    while first < count:
        steps = min(block_len, count - first)
        blocks.append((first, steps, len(blocks) % 2))
        first += steps
    return blocks


even, last, offset_moved, end_moved = range(4)


def kind_of(slab):
    return jnp.where(slab > 0, ((slab - 1) // block_len) & 1, 2)


def flag(flags_ref, which, like):
    return jnp.broadcast_to(flags_ref[which : which + 1, :], like.shape) != 0


def call(kernel, out_shapes, *args):
    size = sum(4 * a.size for a in args) + sum(4 * o.size for o in out_shapes)
    return pl.pallas_call(
        kernel,
        out_shape=tuple(out_shapes),
        in_specs=[pl.BlockSpec(memory_space=pltpu.VMEM)] * len(args),
        out_specs=tuple(pl.BlockSpec(memory_space=pltpu.VMEM) for _ in out_shapes),
        compiler_params=pltpu.CompilerParams(vmem_limit_bytes=vmem_bytes),
        cost_estimate=pl.CostEstimate(flops=10 * size, bytes_accessed=size, transcendentals=0),
    )(*args)


def shape(*dims):
    return jax.ShapeDtypeStruct(dims, jnp.float32)


def plane_sum(x):
    rows, cols = x.shape[-2], x.shape[-1]
    total = pltpu.roll(x, 1, x.ndim - 2) + pltpu.roll(x, rows - 1, x.ndim - 2)
    total = total + pltpu.roll(x, 1, x.ndim - 1) + pltpu.roll(x, cols - 1, x.ndim - 1)
    return total - 6.0 * x


def reactions(s, c):
    product = s * c * c
    return feed_rate * (1.0 - s) - product, product - (feed_rate + kill_rate) * c


def plane_rates(lo, middle, hi):
    lap = [plane_sum(middle[f]) + lo[f] + hi[f] for f in range(2)]
    react = reactions(*middle)
    return [diffuse[f] * lap[f] + react[f] for f in range(2)]


def put_edges(flags_ref, far_ref, near_ref, at, head, tail):
    here = flag(flags_ref, even, head)
    far_ref[at] = jnp.where(here, head, tail)
    near_ref[at] = jnp.where(here, tail, head)


def below(flags_ref, far, near):
    return jnp.where(flag(flags_ref, even, far), far, near)


def above(flags_ref, far, near):
    return jnp.where(flag(flags_ref, even, far), near, far)


def combined(states_ref, way, f, p):
    w = old_weights[way]
    return sum(w[j] * states_ref[j, f, p] for j in range(3))


def start_kernel(flags_ref, states_ref, first_ref, far_ref, near_ref):
    sides = (0, states_ref.shape[2] - 1)
    for f in range(2):
        for way in range(2):
            put_edges(flags_ref, far_ref, near_ref, (way, f), *[combined(states_ref, way, f, p) for p in sides])
        ends = [states_ref[2, f, p] for p in sides]
        ends = [jnp.where(flag(flags_ref, last, x), first_ref[f, p], x) for p, x in zip(sides, ends)]
        put_edges(flags_ref, far_ref, near_ref, (2, f), *ends)


def old_kernel(flags_ref, states_ref, first_ref, part_ref, start_ref):
    depth = states_ref.shape[2]
    for p in range(depth):
        for f in range(2):
            own = states_ref[2, f, p]
            start_ref[f, p] = jnp.where(flag(flags_ref, last, own), first_ref[f, p], own)
        react = [reactions(states_ref[j, 0, p], states_ref[j, 1, p]) for j in range(3)]
        for way in range(2):
            for f in range(2):
                middle = combined(states_ref, way, f, p)
                total = plane_sum(middle)
                if p > 0:
                    total = total + combined(states_ref, way, f, p - 1)
                if p < depth - 1:
                    total = total + combined(states_ref, way, f, p + 1)
                part = diffuse[f] * total
                for j in range(3):
                    part = part + old_weights[way][j] * react[j][f]
                part_ref[way, f, p] = part


def sum_kernel(flags_ref, part_ref, far_ref, near_ref, *out_refs):
    depth = part_ref.shape[2]
    for way, out_ref in enumerate(out_refs):
        for f in range(2):
            for p in range(depth):
                total = part_ref[way, f, p]
                if p == 0:
                    total = total + diffuse[f] * below(flags_ref, far_ref[way, f], near_ref[way, f])
                if p == depth - 1:
                    total = total + diffuse[f] * above(flags_ref, far_ref[way, f], near_ref[way, f])
                out_ref[f, p] = total


def planes_with(flags_ref, x_ref, far_ref, near_ref):
    depth = x_ref.shape[1]

    def plane(p):
        if p < 0:
            return [below(flags_ref, far_ref[f], near_ref[f]) for f in range(2)]
        if p >= depth:
            return [above(flags_ref, far_ref[f], near_ref[f]) for f in range(2)]
        return [x_ref[f, p] for f in range(2)]

    return plane


def node_kernel(way, flags_ref, old_ref, x_ref, far_ref, near_ref, *refs):
    depth = x_ref.shape[1]
    plane = planes_with(flags_ref, x_ref, far_ref, near_ref)
    if way == 0:
        next_ref, keep_ref, next_far_ref, next_near_ref = refs
    else:
        rate_ref, next_ref, keep_ref, next_far_ref, next_near_ref = refs
    for p in range(depth):
        rate = plane_rates(plane(p - 1), plane(p), plane(p + 1))
        for f in range(2):
            next_ref[f, p] = x_ref[f, p] + half_step * rate[f] + old_ref[f, p]
            if way == 0:
                keep_ref[f, p] = rate[f]
            else:
                keep_ref[f, p] = new_weights[0] * rate_ref[f, p] + new_weights[1] * rate[f]
    for f in range(2):
        put_edges(flags_ref, next_far_ref, next_near_ref, f, next_ref[f, 0], next_ref[f, depth - 1])


def offset_kernel(
    count, planes, flags_ref, sum_ref, start_ref, node_ref, rate_ref, x_ref, *refs
):
    send_ref, offset_ref, mid_ref = refs[-3:]
    plane = planes_with(flags_ref, x_ref, *(refs[:2] if len(refs) > 3 else (None, None)))
    for q, p in enumerate(planes):
        rate = plane_rates(plane(p - 1), plane(p), plane(p + 1))
        for f in range(2):
            offset = sum_ref[f, p] + new_weights[2] * rate[f]
            offset_ref[f, q] = offset
            first = start_ref[f, p] + step_time * rate_ref[f, p] + offset
            offset = jnp.where(flag(flags_ref, last, offset), first, offset)
            moved = pltpu.roll(offset, half_rows, 0), pltpu.roll(offset, rows_each, 0)
            offset = jnp.where(flag(flags_ref, offset_moved, offset), *moved)
            offset = jnp.concatenate([offset, offset[:rows_each]], axis=0)
            for i in range(count):
                r = rank_of(i, count)
                send_ref[i, f, q] = offset[r * rows_each : (r + 2) * rows_each]
            mid_ref[f, q] = node_ref[f, p] - 0.5 * (start_ref[f, p] + x_ref[f, p])


def edge_lists(steps):
    return [(0, steps)] + [(j, steps - j) for j in range(1, steps)]


def joined(kind, own, come):
    return jnp.concatenate([come, own] if kind == 0 else [own, come], axis=-2)


def either(p, depth, inner, edges):
    return (inner, p - 1) if 0 < p < depth - 1 else (edges, min(p, 1))


def rows_of(kind, state, inner_ref, edges_ref):
    depth = inner_ref.shape[2] + 2

    def plane(a, f, p):
        if a:
            ref, q = either(p, depth, inner_ref, edges_ref)
            return ref[a - 1, f, q]
        if state[0].shape[2] == rows_each:
            return joined(kind, state[0][f, p], state[1][f, p])
        ref, q = either(p, depth, *state)
        return ref[f, q]

    return plane


def edge_kernel(kind, steps, flags_ref, inner_ref, edges_ref, *refs):
    far_ref, near_ref = refs[-2:]
    depth = inner_ref.shape[2] + 2
    plane = rows_of(kind, refs[:-2], inner_ref, edges_ref)
    at = 0
    for a, n in edge_lists(steps):
        for i in range(n):
            for f in range(2):
                put_edges(flags_ref, far_ref, near_ref, (f, at + i), plane(a, f, i), plane(a, f, depth - n + i))
        at += n


def block_kernel(kind, steps, flags_ref, inner_ref, edges_ref, *refs):
    far_ref, near_ref, out_ref, end_ref = refs[-4:]
    depth = inner_ref.shape[2] + 2
    plane = rows_of(kind, refs[:-4], inner_ref, edges_ref)
    at = {}
    place = 0
    for a, n in edge_lists(steps):
        at[a] = (place, n)
        place += n

    def extended(a, f):
        planes = [plane(a, f, p) for p in range(depth)]
        if a in at:
            place, n = at[a]
            halo = [(far_ref[f, place + i], near_ref[f, place + i]) for i in range(n)]
            lo = [below(flags_ref, *pair) for pair in halo]
            hi = [above(flags_ref, *pair) for pair in halo]
            planes = lo + planes + hi
        return jnp.stack(planes)

    state = [extended(0, f) for f in range(2)]
    for f in range(2):
        own = slice(rows_each, None) if kind == 0 else slice(None, rows_each)
        out_ref[0, f] = state[f][steps - 1 : steps + depth + 1, own]
    for j in range(1, steps + 1):
        middle = [x[1:-1] for x in state]
        rate = plane_rates([x[:-2] for x in state], middle, [x[2:] for x in state])
        state = [middle[f] + step_time * rate[f] + extended(j, f) for f in range(2)]
        halo = steps - j
        for f in range(2):
            if j < steps:
                inner = state[f][halo - 1 : halo + depth + 1]
                out_ref[j, f] = pltpu.roll(inner, 2 * rows_each - half_rows, 1)[:, :rows_each]
            else:
                end_ref[f] = pltpu.roll(state[f], 2 * rows_each - half_rows, 1)[:, :rows_each]
    if out_ref.shape[0] > steps:
        for f in range(2):
            out_ref[steps, f, 1 : depth + 1] = end_ref[f]
            for p in (0, depth + 1):
                out_ref[steps, f, p] = jnp.zeros_like(end_ref[f, 0])


def result_kernel(
    count, flags_ref, come_ref, inner_offset_ref, inner_mid_ref, edges_offset_ref, edges_mid_ref, out_ref
):
    depth = inner_mid_ref.shape[1] + 2

    def whole(f, p):
        full = jnp.concatenate([come_ref[index_of(r, count), f, p + 1] for r in range(count)], axis=0)
        return jnp.where(flag(flags_ref, end_moved, full), pltpu.roll(full, full.shape[0] - half_rows, 0), full)

    planes = [[whole(f, p) for f in range(2)] for p in range(-1, depth + 1)]
    for p in range(depth):
        here = planes[p + 1]
        rate = plane_rates(planes[p], here, planes[p + 2])
        offset_ref, q = either(p, depth, inner_offset_ref, edges_offset_ref)
        mid_ref, q = either(p, depth, inner_mid_ref, edges_mid_ref)
        for f in range(2):
            end = here[f] + step_time * rate[f] + offset_ref[f, q]
            middle = mid_ref[f, q] + 0.5 * (here[f] + end)
            newest = flag(flags_ref, last, end)
            out_ref[0, 0, f, p] = here[f]
            out_ref[0, 1, f, p] = jnp.where(newest, here[f], middle)
            out_ref[0, 2, f, p] = jnp.where(newest, here[f], end)


def swapped(far, near):
    count = lax.axis_size("space")
    far = lax.ppermute(far, "space", [((i + j) % count, (i + 1 - j) % count) for i in range(1, count, 2) for j in range(2)])
    near = lax.ppermute(near, "space", [(i + j, i + 1 - j) for i in range(0, count, 2) for j in range(2)])
    return far, near


def local(states, first_start):
    count = lax.axis_size("tm")
    me = lax.axis_index("tm")
    blocks = chain_blocks(count)
    slab = states[0]
    _, _, depth, rows, cols = slab.shape
    grid = shape(2, depth, rows, cols)
    edge = shape(2, rows, cols)

    newest = me == count - 1
    flags = jnp.stack([
        lax.axis_index("space") & 1 == 0,
        newest,
        ~newest & (kind_of(me + 1) == 1),
        kind_of(me) == 0,
    ]).astype(jnp.int32)
    flags = jnp.broadcast_to(flags[:, None], (4, 128))

    back_one = [(i, (i - 1) % count) for i in range(count)]
    message = shape(3, 2, rows, cols)
    far, near = call(start_kernel, [message] * 2, flags, slab, first_start)
    far, near = swapped(far, near)
    part, fine0 = call(old_kernel, [shape(2, 2, depth, rows, cols), grid], flags, slab, first_start)
    old_first, old_second = call(sum_kernel, [grid] * 2, flags, part, far, near)
    old_first = lax.ppermute(old_first, "tm", back_one)
    old_second = lax.ppermute(old_second, "tm", back_one)

    fine1, rate0, far, near = call(
        functools.partial(node_kernel, 0), [grid] * 2 + [edge] * 2,
        flags, old_first, fine0, far[2], near[2],
    )
    far, near = swapped(far, near)
    fine2, total, far, near = call(
        functools.partial(node_kernel, 1), [grid] * 2 + [edge] * 2,
        flags, old_second, fine1, far, near, rate0,
    )
    known = (flags, total, fine0, fine1, rate0, fine2)

    def offsets_on(planes, *halo):
        some = shape(2, len(planes), rows, cols)
        send, *rest = call(
            functools.partial(offset_kernel, count, planes),
            [shape(count, 2, len(planes), 2 * rows_each, cols), some, some],
            *known, *halo,
        )
        return lax.all_to_all(send, "tm", 0, 0, tiled=True), rest

    far, near = swapped(far, near)
    inner, inner_rest = offsets_on(range(1, depth - 1))
    edges, edges_rest = offsets_on((0, depth - 1), far, near)

    state = [inner[count - 1], edges[count - 1]]
    ends = []
    for first, steps, kind in blocks:
        if ends:
            way = 1 if kind == 0 else -1
            route = [(index_of(r, count), index_of((r + way) % count, count)) for r in range(count)]
            state = [end, lax.ppermute(end, "tm", route)]
        offsets = [x[first - 1 : first - 1 + steps] for x in (inner, edges)]
        message = shape(2, sum(n for _, n in edge_lists(steps)), 2 * rows_each, cols)
        far, near = call(functools.partial(edge_kernel, kind, steps), [message] * 2, flags, *offsets, *state)
        far, near = swapped(far, near)
        kept = steps + (first + steps == count)
        block, end = call(
            functools.partial(block_kernel, kind, steps),
            [shape(kept, 2, depth + 2, rows_each, cols), shape(2, depth, rows_each, cols)],
            flags, *offsets, *state, far, near,
        )
        ends.append(block)
    back = lax.all_to_all(jnp.concatenate(ends), "tm", 0, 0, tiled=True)
    (result,) = call(
        functools.partial(result_kernel, count), [shape(1, 3, 2, depth, rows, cols)], flags, back, *inner_rest, *edges_rest
    )
    return result


def solution(mesh):
    return jax.shard_map(
        local,
        mesh=mesh,
        in_specs=(P("tm", None, None, "space", None, None), P(None, "space", None, None)),
        out_specs=P("tm", None, None, "space", None, None),
        check_vma=False,
    )
```

time: 571 us -> 186 us (0.33)
  the two profiles are of different devices: /device:TPU:220 before, /device:TPU:194 now
where the time goes in v1:
time: 186 us; the launch traced here: 185 us
  starting transfers between devices  86.7 us (47%)
  waiting for transfers between devices  54.4 us (29%)
  blocking collectives  28.6 us (15%)
  Pallas kernels  8.88 us (5%)
  local copies, waits for them, and re-layouts  6 us (3%)
    ppermute x7, starting transfers between devices, swapped(): lax.ppermute(near, 'space', [(i + j, i + 1 - j) for i in range(0, count,...  40.5 us
    all_to_all x1, blocking collectives, local(): back = lax.all_to_all(jnp.concatenate(ends), 'tm', 0, 0, tiled=True)  28.6 us
    all_to_all x2, waiting for transfers between devices, offsets_on(): return (lax.all_to_all(send, 'tm', 0, 0, tiled=True), rest)  19.4 us
    all_to_all x2, starting transfers between devices, offsets_on(): return (lax.all_to_all(send, 'tm', 0, 0, tiled=True), rest)  15.5 us
    ppermute x7, starting transfers between devices, swapped(): lax.ppermute(far, 'space', [((i + j) % count, (i + 1 - j) % count) for i...  14.6 us
    ppermute x3, waiting for transfers between devices, local(): state = [end, lax.ppermute(end, 'tm', route)]  12.1 us
    ppermute x1, waiting for transfers between devices, local(): old_first = lax.ppermute(old_first, 'tm', back_one)  9 us
    pallas_call x16, Pallas kernels, call(): pl.pallas_call(kernel, out_shape=tuple(out_shapes), in_specs=[pl.BlockSpe...  8.88 us
  transfers between devices with their start and end apart: 21, of which 14 were waited for; matrix products, arithmetic and copies ran while one was open for 1% of the time, Pallas kernels for 2%

profile of v1, /device:TPU:194, one launch (start us, length us, event | category | flops | bytes accessed | tf_op | source)
XLA Modules:
  0.0 185.0 jit_solution(12249914505170104082)
XLA Ops:
  4.7 5.6 %collective-permute-start.1 = (f32[3,2,128,128]{3,2,1,0:T(8,128)S(1)}, f32[3,2,128,128]{3,2,1,0:T(8,128)S(1)}, u32[]{:S(2)}, u32[]{:S(2)}) collective-permute-start(f32[3,2,128,128]{3,2,1,0:T(8,128)S(1)} %get-tuple-element.42), channel_id=1, source_target_pairs={{0,1},{1,0},{2,3},{3,2},{4,5},{5,4},{6,7},{7,6},{8,9},{9,8},{10,11... | collective-permute-start | bytes 1179656 | tf_op jit(solution)/shard_map/ppermute | solution.py:317
  11.8 4.3 %collective-permute-done.far_ref = f32[3,2,128,128]{3,2,1,0:T(8,128)S(1)} collective-permute-done((f32[3,2,128,128]{3,2,1,0:T(8,128)S(1)}, f32[3,2,128,128]{3,2,1,0:T(8,128)S(1)}, u32[]{:S(2)}, u32[]{:S(2)}) %collective-permute-start) | collective-permute-done | bytes 393248 | tf_op jit(solution)/shard_map/ppermute | solution.py:316
  16.2 6.9 %collective-permute-start.3 = (f32[2,4,128,128]{3,2,1,0:T(8,128)S(1)}, f32[2,4,128,128]{3,2,1,0:T(8,128)S(1)}, u32[]{:S(2)}, u32[]{:S(2)}) collective-permute-start(f32[2,4,128,128]{3,2,1,0:T(8,128)S(1)} %get-tuple-element.44), channel_id=1, source_target_pairs={{0,480},{32,0},{64,32},{96,64},{128,96},{160,128},{192,160},{224,1... | collective-permute-start | bytes 1572872 | tf_op jit(solution)/shard_map/ppermute | solution.py:345
  23.1 3.3 %collective-permute-start.2 = (f32[2,4,128,128]{3,2,1,0:T(8,128)S(1)}, f32[2,4,128,128]{3,2,1,0:T(8,128)S(1)}, u32[]{:S(2)}, u32[]{:S(2)}) collective-permute-start(f32[2,4,128,128]{3,2,1,0:T(8,128)S(1)} %get-tuple-element.43), channel_id=1, source_target_pairs={{0,480},{32,0},{64,32},{96,64},{128,96},{160,128},{192,160},{224,1... | collective-permute-start | bytes 1572872 | tf_op jit(solution)/shard_map/ppermute | solution.py:346
  26.5 9.0 %collective-permute-done.3.old_ref = f32[2,4,128,128]{3,2,1,0:T(8,128)S(1)} collective-permute-done((f32[2,4,128,128]{3,2,1,0:T(8,128)S(1)}, f32[2,4,128,128]{3,2,1,0:T(8,128)S(1)}, u32[]{:S(2)}, u32[]{:S(2)}) %collective-permute-start.3) | collective-permute-done | bytes 524320 | tf_op jit(solution)/shard_map/ppermute | solution.py:345
  35.9 1.9 %collective-permute-start.4 = (f32[2,128,128]{2,1,0:T(8,128)S(1)}, f32[2,128,128]{2,1,0:T(8,128)S(1)}, u32[]{:S(2)}, u32[]{:S(2)}) collective-permute-start(f32[2,128,128]{2,1,0:T(8,128)S(1)} %get-tuple-element.47), channel_id=1, source_target_pairs={{1,2},{2,1},{3,4},{4,3},{5,6},{6,5},{7,8},{8,7},{9,10},{10,9},{11,... | collective-permute-start | bytes 393224 | tf_op jit(solution)/shard_map/ppermute | solution.py:316
  37.8 3.6 %collective-permute-start.5 = (f32[2,128,128]{2,1,0:T(8,128)S(1)}, f32[2,128,128]{2,1,0:T(8,128)S(1)}, u32[]{:S(2)}, u32[]{:S(2)}) collective-permute-start(f32[2,128,128]{2,1,0:T(8,128)S(1)} %get-tuple-element.48), channel_id=1, source_target_pairs={{0,1},{1,0},{2,3},{3,2},{4,5},{5,4},{6,7},{7,6},{8,9},{9,8},{10,11... | collective-permute-start | bytes 393224 | tf_op jit(solution)/shard_map/ppermute | solution.py:317
  41.4 3.9 %collective-permute-done.2.old_ref = f32[2,4,128,128]{3,2,1,0:T(8,128)S(1)} collective-permute-done((f32[2,4,128,128]{3,2,1,0:T(8,128)S(1)}, f32[2,4,128,128]{3,2,1,0:T(8,128)S(1)}, u32[]{:S(2)}, u32[]{:S(2)}) %collective-permute-start.2) | collective-permute-done | bytes 524320 | tf_op jit(solution)/shard_map/ppermute | solution.py:346
  47.7 7.9 %all-to-all-start = ((f32[16,2,2,16,128]{4,3,2,1,0:T(8,128)}), f32[16,2,2,16,128]{4,3,2,1,0:T(8,128)}, u32[]{:S(2)}, u32[]{:S(2)}) async-start(f32[16,2,2,16,128]{4,3,2,1,0:T(8,128)} %get-tuple-element.52), calls=%async_computation | async-start | bytes 1048576 | tf_op jit(solution)/shard_map/all_to_all | solution.py:366
  55.6 2.1 %collective-permute-start.6 = (f32[2,128,128]{2,1,0:T(8,128)S(1)}, f32[2,128,128]{2,1,0:T(8,128)S(1)}, u32[]{:S(2)}, u32[]{:S(2)}) collective-permute-start(f32[2,128,128]{2,1,0:T(8,128)S(1)} %get-tuple-element.53), channel_id=1, source_target_pairs={{1,2},{2,1},{3,4},{4,3},{5,6},{6,5},{7,8},{8,7},{9,10},{10,9},{11,... | collective-permute-start | bytes 393224 | tf_op jit(solution)/shard_map/ppermute | solution.py:316
  57.7 6.3 %collective-permute-start.7 = (f32[2,128,128]{2,1,0:T(8,128)S(1)}, f32[2,128,128]{2,1,0:T(8,128)S(1)}, u32[]{:S(2)}, u32[]{:S(2)}) collective-permute-start(f32[2,128,128]{2,1,0:T(8,128)S(1)} %get-tuple-element.54), channel_id=1, source_target_pairs={{0,1},{1,0},{2,3},{3,2},{4,5},{5,4},{6,7},{7,6},{8,9},{9,8},{10,11... | collective-permute-start | bytes 393224 | tf_op jit(solution)/shard_map/ppermute | solution.py:317
  66.7 4.9 %all-to-all-done = f32[16,2,2,16,128]{4,3,2,1,0:T(8,128)} async-done(((f32[16,2,2,16,128]{4,3,2,1,0:T(8,128)}), f32[16,2,2,16,128]{4,3,2,1,0:T(8,128)}, u32[]{:S(2)}, u32[]{:S(2)}) %all-to-all-start) | async-done | bytes 524320 | tf_op jit(solution)/shard_map/all_to_all | solution.py:366
  71.7 7.6 %all-to-all-start.1 = ((f32[16,2,2,16,128]{4,3,2,1,0:T(8,128)}), f32[16,2,2,16,128]{4,3,2,1,0:T(8,128)S(1)}, u32[]{:S(2)}, u32[]{:S(2)}) async-start(f32[16,2,2,16,128]{4,3,2,1,0:T(8,128)} %get-tuple-element.55), calls=%async_computation.1 | async-start | bytes 1048576 | tf_op jit(solution)/shard_map/all_to_all | solution.py:366
  81.1 14.5 %all-to-all-done.1 = f32[16,2,2,16,128]{4,3,2,1,0:T(8,128)S(1)} async-done(((f32[16,2,2,16,128]{4,3,2,1,0:T(8,128)}), f32[16,2,2,16,128]{4,3,2,1,0:T(8,128)S(1)}, u32[]{:S(2)}, u32[]{:S(2)}) %all-to-all-start.1) | async-done | bytes 524320 | tf_op jit(solution)/shard_map/all_to_all | solution.py:366
  95.6 2.9 %collective-permute-start.8 = (f32[2,10,16,128]{3,2,1,0:T(8,128)S(1)}, f32[2,10,16,128]{3,2,1,0:T(8,128)S(1)}, u32[]{:S(2)}, u32[]{:S(2)}) collective-permute-start(f32[2,10,16,128]{3,2,1,0:T(8,128)S(1)} %get-tuple-element.56), channel_id=1, source_target_pairs={{1,2},{2,1},{3,4},{4,3},{5,6},{6,5},{7,8},{8,7},{9,10},{10,9},{11,... | collective-permute-start | bytes 491528 | tf_op jit(solution)/shard_map/ppermute | solution.py:316
  98.5 7.6 %collective-permute-start.9 = (f32[2,10,16,128]{3,2,1,0:T(8,128)S(1)}, f32[2,10,16,128]{3,2,1,0:T(8,128)S(1)}, u32[]{:S(2)}, u32[]{:S(2)}) collective-permute-start(f32[2,10,16,128]{3,2,1,0:T(8,128)S(1)} %get-tuple-element.57), channel_id=1, source_target_pairs={{0,1},{1,0},{2,3},{3,2},{4,5},{5,4},{6,7},{7,6},{8,9},{9,8},{10,11... | collective-permute-start | bytes 491528 | tf_op jit(solution)/shard_map/ppermute | solution.py:317
  109.5 3.9 %collective-permute-done.10.refs_1_ = f32[2,4,8,128]{3,2,1,0:T(8,128)S(1)} collective-permute-done((f32[2,4,8,128]{3,2,1,0:T(8,128)S(1)}, f32[2,4,8,128]{3,2,1,0:T(8,128)S(1)}, u32[]{:S(2)}, u32[]{:S(2)}) %collective-permute-start.10) | collective-permute-done | bytes 32800 | tf_op jit(solution)/shard_map/ppermute | solution.py:378
  115.3 5.8 %collective-permute-start.12 = (f32[2,10,16,128]{3,2,1,0:T(8,128)S(1)}, f32[2,10,16,128]{3,2,1,0:T(8,128)S(1)}, u32[]{:S(2)}, u32[]{:S(2)}) collective-permute-start(f32[2,10,16,128]{3,2,1,0:T(8,128)S(1)} %get-tuple-element.61), channel_id=1, source_target_pairs={{0,1},{1,0},{2,3},{3,2},{4,5},{5,4},{6,7},{7,6},{8,9},{9,8},{10,11... | collective-permute-start | bytes 491528 | tf_op jit(solution)/shard_map/ppermute | solution.py:317
  122.6 2.1 %collective-permute-start.13 = (f32[2,4,8,128]{3,2,1,0:T(8,128)S(1)}, f32[2,4,8,128]{3,2,1,0:T(8,128)S(1)}, u32[]{:S(2)}, u32[]{:S(2)}) collective-permute-start(f32[2,4,8,128]{3,2,1,0:T(8,128)S(1)} %get-tuple-element.63.refs_0_), channel_id=1, source_target_pairs={{0,64},{64,128},{128,192},{192,256},{256,320},{320,384},{384,448},... | collective-permute-start | bytes 98312 | tf_op jit(solution)/shard_map/ppermute | solution.py:378
  124.7 5.2 %collective-permute-done.13.refs_1_ = f32[2,4,8,128]{3,2,1,0:T(8,128)S(1)} collective-permute-done((f32[2,4,8,128]{3,2,1,0:T(8,128)S(1)}, f32[2,4,8,128]{3,2,1,0:T(8,128)S(1)}, u32[]{:S(2)}, u32[]{:S(2)}) %collective-permute-start.13) | collective-permute-done | bytes 32800 | tf_op jit(solution)/shard_map/ppermute | solution.py:378
  131.9 5.8 %collective-permute-start.15 = (f32[2,10,16,128]{3,2,1,0:T(8,128)S(1)}, f32[2,10,16,128]{3,2,1,0:T(8,128)S(1)}, u32[]{:S(2)}, u32[]{:S(2)}) collective-permute-start(f32[2,10,16,128]{3,2,1,0:T(8,128)S(1)} %get-tuple-element.65), channel_id=1, source_target_pairs={{0,1},{1,0},{2,3},{3,2},{4,5},{5,4},{6,7},{7,6},{8,9},{9,8},{10,11... | collective-permute-start | bytes 491528 | tf_op jit(solution)/shard_map/ppermute | solution.py:317
  142.0 3.0 %collective-permute-done.16.refs_1_ = f32[2,4,8,128]{3,2,1,0:T(8,128)S(1)} collective-permute-done((f32[2,4,8,128]{3,2,1,0:T(8,128)S(1)}, f32[2,4,8,128]{3,2,1,0:T(8,128)S(1)}, u32[]{:S(2)}, u32[]{:S(2)}) %collective-permute-start.16) | collective-permute-done | bytes 32800 | tf_op jit(solution)/shard_map/ppermute | solution.py:378
  146.9 5.9 %collective-permute-start.18 = (f32[2,6,16,128]{3,2,1,0:T(8,128)S(1)}, f32[2,6,16,128]{3,2,1,0:T(8,128)S(1)}, u32[]{:S(2)}, u32[]{:S(2)}) collective-permute-start(f32[2,6,16,128]{3,2,1,0:T(8,128)S(1)} %get-tuple-element.69), channel_id=1, source_target_pairs={{0,1},{1,0},{2,3},{3,2},{4,5},{5,4},{6,7},{7,6},{8,9},{9,8},{10,11... | collective-permute-start | bytes 294920 | tf_op jit(solution)/shard_map/ppermute | solution.py:317
  154.8 28.6 %all_to_all.15.come_ref = f32[16,2,6,8,128]{4,3,2,1,0:T(8,128)S(1)} all-to-all(f32[16,2,6,8,128]{4,3,2,1,0:T(8,128)S(1)} %pad_maximum_fusion), channel_id=1, replica_groups=mesh['tm'=16,'space'=32] {'tm'}, dimensions={0} | all-to-all | bytes 1572864 | tf_op jit(solution)/shard_map/all_to_all | solution.py:390
  (54 shorter events, 32.3 us)
Async XLA Ops:
  0.2 1.4 copy-start
  1.6 1.0 copy-start.1
  2.8 13.3 %collective-permute-start = (f32[3,2,128,128]{3,2,1,0:T(8,128)S(1)}, f32[3,2,128,128]{3,2,1,0:T(8,128)S(1)}, u32[]{:S(2)}, u32[]{:S(2)}) collective-permute-start(f32[3,2,128,128]{3,2,1,0:T(8,128)S(1)} %get-tuple-element.41), channel_id=1, source_target_pairs={{1,2},{2,1},{3,4},{4,3},{5,6},{6,5},{7,8},{8,7},{9,10},{10,9},{11,... | collective-permute-start | bytes 1179656 | tf_op jit(solution)/shard_map/ppermute | solution.py:316
  4.7 11.4 %collective-permute-start.1 = (f32[3,2,128,128]{3,2,1,0:T(8,128)S(1)}, f32[3,2,128,128]{3,2,1,0:T(8,128)S(1)}, u32[]{:S(2)}, u32[]{:S(2)}) collective-permute-start(f32[3,2,128,128]{3,2,1,0:T(8,128)S(1)} %get-tuple-element.42), channel_id=1, source_target_pairs={{0,1},{1,0},{2,3},{3,2},{4,5},{5,4},{6,7},{7,6},{8,9},{9,8},{10,11... | collective-permute-start | bytes 1179656 | tf_op jit(solution)/shard_map/ppermute | solution.py:317
  16.2 19.3 %collective-permute-start.3 = (f32[2,4,128,128]{3,2,1,0:T(8,128)S(1)}, f32[2,4,128,128]{3,2,1,0:T(8,128)S(1)}, u32[]{:S(2)}, u32[]{:S(2)}) collective-permute-start(f32[2,4,128,128]{3,2,1,0:T(8,128)S(1)} %get-tuple-element.44), channel_id=1, source_target_pairs={{0,480},{32,0},{64,32},{96,64},{128,96},{160,128},{192,160},{224,1... | collective-permute-start | bytes 1572872 | tf_op jit(solution)/shard_map/ppermute | solution.py:345
  23.1 22.1 %collective-permute-start.2 = (f32[2,4,128,128]{3,2,1,0:T(8,128)S(1)}, f32[2,4,128,128]{3,2,1,0:T(8,128)S(1)}, u32[]{:S(2)}, u32[]{:S(2)}) collective-permute-start(f32[2,4,128,128]{3,2,1,0:T(8,128)S(1)} %get-tuple-element.43), channel_id=1, source_target_pairs={{0,480},{32,0},{64,32},{96,64},{128,96},{160,128},{192,160},{224,1... | collective-permute-start | bytes 1572872 | tf_op jit(solution)/shard_map/ppermute | solution.py:346
  35.9 10.2 %collective-permute-start.4 = (f32[2,128,128]{2,1,0:T(8,128)S(1)}, f32[2,128,128]{2,1,0:T(8,128)S(1)}, u32[]{:S(2)}, u32[]{:S(2)}) collective-permute-start(f32[2,128,128]{2,1,0:T(8,128)S(1)} %get-tuple-element.47), channel_id=1, source_target_pairs={{1,2},{2,1},{3,4},{4,3},{5,6},{6,5},{7,8},{8,7},{9,10},{10,9},{11,... | collective-permute-start | bytes 393224 | tf_op jit(solution)/shard_map/ppermute | solution.py:316
  37.8 8.3 %collective-permute-start.5 = (f32[2,128,128]{2,1,0:T(8,128)S(1)}, f32[2,128,128]{2,1,0:T(8,128)S(1)}, u32[]{:S(2)}, u32[]{:S(2)}) collective-permute-start(f32[2,128,128]{2,1,0:T(8,128)S(1)} %get-tuple-element.48), channel_id=1, source_target_pairs={{0,1},{1,0},{2,3},{3,2},{4,5},{5,4},{6,7},{7,6},{8,9},{9,8},{10,11... | collective-permute-start | bytes 393224 | tf_op jit(solution)/shard_map/ppermute | solution.py:317
  47.7 24.0 %all-to-all-start = ((f32[16,2,2,16,128]{4,3,2,1,0:T(8,128)}), f32[16,2,2,16,128]{4,3,2,1,0:T(8,128)}, u32[]{:S(2)}, u32[]{:S(2)}) async-start(f32[16,2,2,16,128]{4,3,2,1,0:T(8,128)} %get-tuple-element.52), calls=%async_computation | async-start | bytes 1048576 | tf_op jit(solution)/shard_map/all_to_all | solution.py:366
  55.6 8.4 %collective-permute-start.6 = (f32[2,128,128]{2,1,0:T(8,128)S(1)}, f32[2,128,128]{2,1,0:T(8,128)S(1)}, u32[]{:S(2)}, u32[]{:S(2)}) collective-permute-start(f32[2,128,128]{2,1,0:T(8,128)S(1)} %get-tuple-element.53), channel_id=1, source_target_pairs={{1,2},{2,1},{3,4},{4,3},{5,6},{6,5},{7,8},{8,7},{9,10},{10,9},{11,... | collective-permute-start | bytes 393224 | tf_op jit(solution)/shard_map/ppermute | solution.py:316
  57.7 7.2 %collective-permute-start.7 = (f32[2,128,128]{2,1,0:T(8,128)S(1)}, f32[2,128,128]{2,1,0:T(8,128)S(1)}, u32[]{:S(2)}, u32[]{:S(2)}) collective-permute-start(f32[2,128,128]{2,1,0:T(8,128)S(1)} %get-tuple-element.54), channel_id=1, source_target_pairs={{0,1},{1,0},{2,3},{3,2},{4,5},{5,4},{6,7},{7,6},{8,9},{9,8},{10,11... | collective-permute-start | bytes 393224 | tf_op jit(solution)/shard_map/ppermute | solution.py:317
  71.7 23.9 %all-to-all-start.1 = ((f32[16,2,2,16,128]{4,3,2,1,0:T(8,128)}), f32[16,2,2,16,128]{4,3,2,1,0:T(8,128)S(1)}, u32[]{:S(2)}, u32[]{:S(2)}) async-start(f32[16,2,2,16,128]{4,3,2,1,0:T(8,128)} %get-tuple-element.55), calls=%async_computation.1 | async-start | bytes 1048576 | tf_op jit(solution)/shard_map/all_to_all | solution.py:366
  95.6 10.5 %collective-permute-start.8 = (f32[2,10,16,128]{3,2,1,0:T(8,128)S(1)}, f32[2,10,16,128]{3,2,1,0:T(8,128)S(1)}, u32[]{:S(2)}, u32[]{:S(2)}) collective-permute-start(f32[2,10,16,128]{3,2,1,0:T(8,128)S(1)} %get-tuple-element.56), channel_id=1, source_target_pairs={{1,2},{2,1},{3,4},{4,3},{5,6},{6,5},{7,8},{8,7},{9,10},{10,9},{11,... | collective-permute-start | bytes 491528 | tf_op jit(solution)/shard_map/ppermute | solution.py:316
  98.5 8.6 %collective-permute-start.9 = (f32[2,10,16,128]{3,2,1,0:T(8,128)S(1)}, f32[2,10,16,128]{3,2,1,0:T(8,128)S(1)}, u32[]{:S(2)}, u32[]{:S(2)}) collective-permute-start(f32[2,10,16,128]{3,2,1,0:T(8,128)S(1)} %get-tuple-element.57), channel_id=1, source_target_pairs={{0,1},{1,0},{2,3},{3,2},{4,5},{5,4},{6,7},{7,6},{8,9},{9,8},{10,11... | collective-permute-start | bytes 491528 | tf_op jit(solution)/shard_map/ppermute | solution.py:317
  107.6 5.8 %collective-permute-start.10 = (f32[2,4,8,128]{3,2,1,0:T(8,128)S(1)}, f32[2,4,8,128]{3,2,1,0:T(8,128)S(1)}, u32[]{:S(2)}, u32[]{:S(2)}) collective-permute-start(f32[2,4,8,128]{3,2,1,0:T(8,128)S(1)} %get-tuple-element.59.refs_0_), channel_id=1, source_target_pairs={{0,32},{64,0},{128,64},{192,128},{256,192},{320,256},{384,320},{44... | collective-permute-start | bytes 98312 | tf_op jit(solution)/shard_map/ppermute | solution.py:378
  113.4 7.7 %collective-permute-start.11 = (f32[2,10,16,128]{3,2,1,0:T(8,128)S(1)}, f32[2,10,16,128]{3,2,1,0:T(8,128)S(1)}, u32[]{:S(2)}, u32[]{:S(2)}) collective-permute-start(f32[2,10,16,128]{3,2,1,0:T(8,128)S(1)} %get-tuple-element.60), channel_id=1, source_target_pairs={{1,2},{2,1},{3,4},{4,3},{5,6},{6,5},{7,8},{8,7},{9,10},{10,9},{11,... | collective-permute-start | bytes 491528 | tf_op jit(solution)/shard_map/ppermute | solution.py:316
  115.3 6.8 %collective-permute-start.12 = (f32[2,10,16,128]{3,2,1,0:T(8,128)S(1)}, f32[2,10,16,128]{3,2,1,0:T(8,128)S(1)}, u32[]{:S(2)}, u32[]{:S(2)}) collective-permute-start(f32[2,10,16,128]{3,2,1,0:T(8,128)S(1)} %get-tuple-element.61), channel_id=1, source_target_pairs={{0,1},{1,0},{2,3},{3,2},{4,5},{5,4},{6,7},{7,6},{8,9},{9,8},{10,11... | collective-permute-start | bytes 491528 | tf_op jit(solution)/shard_map/ppermute | solution.py:317
  122.6 7.3 %collective-permute-start.13 = (f32[2,4,8,128]{3,2,1,0:T(8,128)S(1)}, f32[2,4,8,128]{3,2,1,0:T(8,128)S(1)}, u32[]{:S(2)}, u32[]{:S(2)}) collective-permute-start(f32[2,4,8,128]{3,2,1,0:T(8,128)S(1)} %get-tuple-element.63.refs_0_), channel_id=1, source_target_pairs={{0,64},{64,128},{128,192},{192,256},{256,320},{320,384},{384,448},... | collective-permute-start | bytes 98312 | tf_op jit(solution)/shard_map/ppermute | solution.py:378
  130.0 7.7 %collective-permute-start.14 = (f32[2,10,16,128]{3,2,1,0:T(8,128)S(1)}, f32[2,10,16,128]{3,2,1,0:T(8,128)S(1)}, u32[]{:S(2)}, u32[]{:S(2)}) collective-permute-start(f32[2,10,16,128]{3,2,1,0:T(8,128)S(1)} %get-tuple-element.64), channel_id=1, source_target_pairs={{1,2},{2,1},{3,4},{4,3},{5,6},{6,5},{7,8},{8,7},{9,10},{10,9},{11,... | collective-permute-start | bytes 491528 | tf_op jit(solution)/shard_map/ppermute | solution.py:316
  131.9 6.8 %collective-permute-start.15 = (f32[2,10,16,128]{3,2,1,0:T(8,128)S(1)}, f32[2,10,16,128]{3,2,1,0:T(8,128)S(1)}, u32[]{:S(2)}, u32[]{:S(2)}) collective-permute-start(f32[2,10,16,128]{3,2,1,0:T(8,128)S(1)} %get-tuple-element.65), channel_id=1, source_target_pairs={{0,1},{1,0},{2,3},{3,2},{4,5},{5,4},{6,7},{7,6},{8,9},{9,8},{10,11... | collective-permute-start | bytes 491528 | tf_op jit(solution)/shard_map/ppermute | solution.py:317
  139.2 5.8 %collective-permute-start.16 = (f32[2,4,8,128]{3,2,1,0:T(8,128)S(1)}, f32[2,4,8,128]{3,2,1,0:T(8,128)S(1)}, u32[]{:S(2)}, u32[]{:S(2)}) collective-permute-start(f32[2,4,8,128]{3,2,1,0:T(8,128)S(1)} %get-tuple-element.67.refs_0_), channel_id=1, source_target_pairs={{0,32},{64,0},{128,64},{192,128},{256,192},{320,256},{384,320},{44... | collective-permute-start | bytes 98312 | tf_op jit(solution)/shard_map/ppermute | solution.py:378
  145.0 7.8 %collective-permute-start.17 = (f32[2,6,16,128]{3,2,1,0:T(8,128)S(1)}, f32[2,6,16,128]{3,2,1,0:T(8,128)S(1)}, u32[]{:S(2)}, u32[]{:S(2)}) collective-permute-start(f32[2,6,16,128]{3,2,1,0:T(8,128)S(1)} %get-tuple-element.68), channel_id=1, source_target_pairs={{1,2},{2,1},{3,4},{4,3},{5,6},{6,5},{7,8},{8,7},{9,10},{10,9},{11,... | collective-permute-start | bytes 294920 | tf_op jit(solution)/shard_map/ppermute | solution.py:316
  146.9 6.8 %collective-permute-start.18 = (f32[2,6,16,128]{3,2,1,0:T(8,128)S(1)}, f32[2,6,16,128]{3,2,1,0:T(8,128)S(1)}, u32[]{:S(2)}, u32[]{:S(2)}) collective-permute-start(f32[2,6,16,128]{3,2,1,0:T(8,128)S(1)} %get-tuple-element.69), channel_id=1, source_target_pairs={{0,1},{1,0},{2,3},{3,2},{4,5},{5,4},{6,7},{7,6},{8,9},{9,8},{10,11... | collective-permute-start | bytes 294920 | tf_op jit(solution)/shard_map/ppermute | solution.py:317
  154.7 28.6 %copy-start.3 = (f32[2,2,128,128]{3,2,1,0:T(8,128)S(1)}, f32[2,2,128,128]{3,2,1,0:T(8,128)}, u32[]{:S(2)}) copy-start(f32[2,2,128,128]{3,2,1,0:T(8,128)} %copy-done.2) | copy-start | bytes 786436
  (1 other events, 0.7 us)

commit v2 on v1

--- a/solution.py
+++ b/solution.py
@@ -56,13 +56,14 @@
     return jnp.broadcast_to(flags_ref[which : which + 1, :], like.shape) != 0
 
 
-def call(kernel, out_shapes, *args):
+def call(kernel, out_shapes, *args, result_outside=False, scratch=()):
     size = sum(4 * a.size for a in args) + sum(4 * o.size for o in out_shapes)
     return pl.pallas_call(
         kernel,
         out_shape=tuple(out_shapes),
         in_specs=[pl.BlockSpec(memory_space=pltpu.VMEM)] * len(args),
-        out_specs=tuple(pl.BlockSpec(memory_space=pltpu.VMEM) for _ in out_shapes),
+        out_specs=tuple(pl.BlockSpec(memory_space=pl.ANY if result_outside else pltpu.VMEM) for _ in out_shapes),
+        scratch_shapes=list(scratch),
         compiler_params=pltpu.CompilerParams(vmem_limit_bytes=vmem_bytes),
         cost_estimate=pl.CostEstimate(flops=10 * size, bytes_accessed=size, transcendentals=0),
     )(*args)
@@ -109,22 +110,21 @@
     return sum(w[j] * states_ref[j, f, p] for j in range(3))
 
 
-def start_kernel(flags_ref, states_ref, first_ref, far_ref, near_ref):
-    sides = (0, states_ref.shape[2] - 1)
+def start_kernel(flags_ref, states_ref, first_ref, far_ref, near_ref, start_ref):
+    depth = states_ref.shape[2]
     for f in range(2):
+        for p in range(depth):
+            own = states_ref[2, f, p]
+            start_ref[f, p] = jnp.where(flag(flags_ref, last, own), first_ref[f, p], own)
         for way in range(2):
-            put_edges(flags_ref, far_ref, near_ref, (way, f), *[combined(states_ref, way, f, p) for p in sides])
-        ends = [states_ref[2, f, p] for p in sides]
-        ends = [jnp.where(flag(flags_ref, last, x), first_ref[f, p], x) for p, x in zip(sides, ends)]
-        put_edges(flags_ref, far_ref, near_ref, (2, f), *ends)
-
-
-def old_kernel(flags_ref, states_ref, first_ref, part_ref, start_ref):
+            head, tail = combined(states_ref, way, f, 0), combined(states_ref, way, f, depth - 1)
+            put_edges(flags_ref, far_ref, near_ref, (way, f), head, tail)
+        put_edges(flags_ref, far_ref, near_ref, (2, f), start_ref[f, 0], start_ref[f, depth - 1])
+
+
+def old_kernel(states_ref, part_ref):
     depth = states_ref.shape[2]
     for p in range(depth):
-        for f in range(2):
-            own = states_ref[2, f, p]
-            start_ref[f, p] = jnp.where(flag(flags_ref, last, own), first_ref[f, p], own)
         react = [reactions(states_ref[j, 0, p], states_ref[j, 1, p]) for j in range(3)]
         for way in range(2):
             for f in range(2):
@@ -186,15 +186,16 @@
 
 
 def offset_kernel(
-    count, planes, flags_ref, sum_ref, start_ref, node_ref, rate_ref, x_ref, *refs
+    count, flags_ref, x_ref, far_ref, near_ref, sum_ref, start_ref, node_ref, rate_ref,
+    send_ref, offset_ref, mid_ref,
 ):
-    send_ref, offset_ref, mid_ref = refs[-3:]
-    plane = planes_with(flags_ref, x_ref, *(refs[:2] if len(refs) > 3 else (None, None)))
-    for q, p in enumerate(planes):
+    depth = x_ref.shape[1]
+    plane = planes_with(flags_ref, x_ref, far_ref, near_ref)
+    for p in range(depth):
         rate = plane_rates(plane(p - 1), plane(p), plane(p + 1))
         for f in range(2):
             offset = sum_ref[f, p] + new_weights[2] * rate[f]
-            offset_ref[f, q] = offset
+            offset_ref[f, p] = offset
             first = start_ref[f, p] + step_time * rate_ref[f, p] + offset
             offset = jnp.where(flag(flags_ref, last, offset), first, offset)
             moved = pltpu.roll(offset, half_rows, 0), pltpu.roll(offset, rows_each, 0)
@@ -202,8 +203,8 @@
             offset = jnp.concatenate([offset, offset[:rows_each]], axis=0)
             for i in range(count):
                 r = rank_of(i, count)
-                send_ref[i, f, q] = offset[r * rows_each : (r + 2) * rows_each]
-            mid_ref[f, q] = node_ref[f, p] - 0.5 * (start_ref[f, p] + x_ref[f, p])
+                send_ref[i, f, p] = offset[r * rows_each : (r + 2) * rows_each]
+            mid_ref[f, p] = node_ref[f, p] - 0.5 * (start_ref[f, p] + x_ref[f, p])
 
 
 def edge_lists(steps):
@@ -214,54 +215,62 @@
     return jnp.concatenate([come, own] if kind == 0 else [own, come], axis=-2)
 
 
-def either(p, depth, inner, edges):
-    return (inner, p - 1) if 0 < p < depth - 1 else (edges, min(p, 1))
-
-
-def rows_of(kind, state, inner_ref, edges_ref):
-    depth = inner_ref.shape[2] + 2
-
+def rows_of(kind, state, offsets_ref):
     def plane(a, f, p):
         if a:
-            ref, q = either(p, depth, inner_ref, edges_ref)
-            return ref[a - 1, f, q]
-        if state[0].shape[2] == rows_each:
-            return joined(kind, state[0][f, p], state[1][f, p])
-        ref, q = either(p, depth, *state)
-        return ref[f, q]
+            return offsets_ref[a - 1, f, p]
+        return state[0][f, p] if len(state) == 1 else joined(kind, state[0][f, p], state[1][f, p])
 
     return plane
 
 
-def edge_kernel(kind, steps, flags_ref, inner_ref, edges_ref, *refs):
+def tiles_in(steps):
+    return sum(2 * n - 1 for _, n in edge_lists(steps))
+
+
+def edge_kernel(kind, steps, flags_ref, offsets_ref, *refs):
     far_ref, near_ref = refs[-2:]
-    depth = inner_ref.shape[2] + 2
-    plane = rows_of(kind, refs[:-2], inner_ref, edges_ref)
+    depth = offsets_ref.shape[2]
+    plane = rows_of(kind, refs[:-2], offsets_ref)
     at = 0
     for a, n in edge_lists(steps):
-        for i in range(n):
+        for away in range(1, n + 1):
             for f in range(2):
-                put_edges(flags_ref, far_ref, near_ref, (f, at + i), plane(a, f, i), plane(a, f, depth - n + i))
-        at += n
-
-
-def block_kernel(kind, steps, flags_ref, inner_ref, edges_ref, *refs):
-    far_ref, near_ref, out_ref, end_ref = refs[-4:]
-    depth = inner_ref.shape[2] + 2
-    plane = rows_of(kind, refs[:-4], inner_ref, edges_ref)
+                ends = plane(a, f, away - 1), plane(a, f, depth - away)
+                if away == n:
+                    ends = [pltpu.roll(x, 2 * rows_each - half_rows, 0)[:rows_each] for x in ends]
+                    put_edges(flags_ref, far_ref, near_ref, (f, at), *ends)
+                else:
+                    put_edges(flags_ref, far_ref, near_ref, (f, at), *[x[:rows_each] for x in ends])
+                    put_edges(flags_ref, far_ref, near_ref, (f, at + 1), *[x[rows_each:] for x in ends])
+            at += 1 if away == n else 2
+
+
+def block_kernel(kind, steps, flags_ref, offsets_ref, *refs):
+    closing = refs[-1].shape[0] > steps
+    far_ref, near_ref, out_ref, end_ref = (*refs[-3:], None) if closing else refs[-4:]
+    depth = offsets_ref.shape[2]
+    plane = rows_of(kind, refs[: -3 if closing else -4], offsets_ref)
     at = {}
     place = 0
     for a, n in edge_lists(steps):
         at[a] = (place, n)
-        place += n
+        place += 2 * n - 1
+
+    def halo(a, f, away, side):
+        place, n = at[a]
+        first = place + 2 * (away - 1)
+        tiles = [side(flags_ref, far_ref[f, t], near_ref[f, t]) for t in range(first, first + 1 + (away < n))]
+        if away < n:
+            return jnp.concatenate(tiles, axis=0)
+        return pltpu.roll(jnp.concatenate(tiles * 2, axis=0), half_rows, 0)
 
     def extended(a, f):
         planes = [plane(a, f, p) for p in range(depth)]
         if a in at:
-            place, n = at[a]
-            halo = [(far_ref[f, place + i], near_ref[f, place + i]) for i in range(n)]
-            lo = [below(flags_ref, *pair) for pair in halo]
-            hi = [above(flags_ref, *pair) for pair in halo]
+            aways = range(1, at[a][1] + 1)
+            lo = [halo(a, f, away, below) for away in reversed(aways)]
+            hi = [halo(a, f, away, above) for away in aways]
             planes = lo + planes + hi
         return jnp.stack(planes)
 
@@ -273,42 +282,44 @@
         middle = [x[1:-1] for x in state]
         rate = plane_rates([x[:-2] for x in state], middle, [x[2:] for x in state])
         state = [middle[f] + step_time * rate[f] + extended(j, f) for f in range(2)]
-        halo = steps - j
+        around = steps - j
         for f in range(2):
             if j < steps:
-                inner = state[f][halo - 1 : halo + depth + 1]
+                inner = state[f][around - 1 : around + depth + 1]
                 out_ref[j, f] = pltpu.roll(inner, 2 * rows_each - half_rows, 1)[:, :rows_each]
+                continue
+            end = pltpu.roll(state[f], 2 * rows_each - half_rows, 1)[:, :rows_each]
+            if closing:
+                out_ref[steps, f, 1 : depth + 1] = end
+                for p in (0, depth + 1):
+                    out_ref[steps, f, p] = jnp.zeros_like(end[0])
             else:
-                end_ref[f] = pltpu.roll(state[f], 2 * rows_each - half_rows, 1)[:, :rows_each]
-    if out_ref.shape[0] > steps:
-        for f in range(2):
-            out_ref[steps, f, 1 : depth + 1] = end_ref[f]
-            for p in (0, depth + 1):
-                out_ref[steps, f, p] = jnp.zeros_like(end_ref[f, 0])
-
-
-def result_kernel(
-    count, flags_ref, come_ref, inner_offset_ref, inner_mid_ref, edges_offset_ref, edges_mid_ref, out_ref
-):
-    depth = inner_mid_ref.shape[1] + 2
+                end_ref[f] = end
+
+
+def result_kernel(count, flags_ref, come_ref, offset_ref, mid_ref, out_hbm, out_ref, sems):
+    depth = mid_ref.shape[1]
 
     def whole(f, p):
         full = jnp.concatenate([come_ref[index_of(r, count), f, p + 1] for r in range(count)], axis=0)
         return jnp.where(flag(flags_ref, end_moved, full), pltpu.roll(full, full.shape[0] - half_rows, 0), full)
 
     planes = [[whole(f, p) for f in range(2)] for p in range(-1, depth + 1)]
+    copies = []
     for p in range(depth):
         here = planes[p + 1]
         rate = plane_rates(planes[p], here, planes[p + 2])
-        offset_ref, q = either(p, depth, inner_offset_ref, edges_offset_ref)
-        mid_ref, q = either(p, depth, inner_mid_ref, edges_mid_ref)
         for f in range(2):
-            end = here[f] + step_time * rate[f] + offset_ref[f, q]
-            middle = mid_ref[f, q] + 0.5 * (here[f] + end)
+            end = here[f] + step_time * rate[f] + offset_ref[f, p]
+            middle = mid_ref[f, p] + 0.5 * (here[f] + end)
             newest = flag(flags_ref, last, end)
-            out_ref[0, 0, f, p] = here[f]
-            out_ref[0, 1, f, p] = jnp.where(newest, here[f], middle)
-            out_ref[0, 2, f, p] = jnp.where(newest, here[f], end)
+            out_ref[p, 0, f] = here[f]
+            out_ref[p, 1, f] = jnp.where(newest, here[f], middle)
+            out_ref[p, 2, f] = jnp.where(newest, here[f], end)
+        copies.append(pltpu.make_async_copy(out_ref.at[p], out_hbm.at[0, :, :, p], sems.at[p]))
+        copies[-1].start()
+    for copy in copies:
+        copy.wait()
 
 
 def swapped(far, near):
@@ -338,9 +349,9 @@
 
     back_one = [(i, (i - 1) % count) for i in range(count)]
     message = shape(3, 2, rows, cols)
-    far, near = call(start_kernel, [message] * 2, flags, slab, first_start)
+    far, near, fine0 = call(start_kernel, [message, message, grid], flags, slab, first_start)
     far, near = swapped(far, near)
-    part, fine0 = call(old_kernel, [shape(2, 2, depth, rows, cols), grid], flags, slab, first_start)
+    (part,) = call(old_kernel, [shape(2, 2, depth, rows, cols)], slab)
     old_first, old_second = call(sum_kernel, [grid] * 2, flags, part, far, near)
     old_first = lax.ppermute(old_first, "tm", back_one)
     old_second = lax.ppermute(old_second, "tm", back_one)
@@ -354,42 +365,38 @@
         functools.partial(node_kernel, 1), [grid] * 2 + [edge] * 2,
         flags, old_second, fine1, far, near, rate0,
     )
-    known = (flags, total, fine0, fine1, rate0, fine2)
-
-    def offsets_on(planes, *halo):
-        some = shape(2, len(planes), rows, cols)
-        send, *rest = call(
-            functools.partial(offset_kernel, count, planes),
-            [shape(count, 2, len(planes), 2 * rows_each, cols), some, some],
-            *known, *halo,
-        )
-        return lax.all_to_all(send, "tm", 0, 0, tiled=True), rest
-
     far, near = swapped(far, near)
-    inner, inner_rest = offsets_on(range(1, depth - 1))
-    edges, edges_rest = offsets_on((0, depth - 1), far, near)
-
-    state = [inner[count - 1], edges[count - 1]]
+    send, offset, mid = call(
+        functools.partial(offset_kernel, count),
+        [shape(count, 2, depth, 2 * rows_each, cols), grid, grid],
+        flags, fine2, far, near, total, fine0, fine1, rate0,
+    )
+    held = lax.all_to_all(send, "tm", 0, 0, tiled=True)
+
+    state = [held[count - 1]]
     ends = []
     for first, steps, kind in blocks:
         if ends:
             way = 1 if kind == 0 else -1
             route = [(index_of(r, count), index_of((r + way) % count, count)) for r in range(count)]
-            state = [end, lax.ppermute(end, "tm", route)]
-        offsets = [x[first - 1 : first - 1 + steps] for x in (inner, edges)]
-        message = shape(2, sum(n for _, n in edge_lists(steps)), 2 * rows_each, cols)
-        far, near = call(functools.partial(edge_kernel, kind, steps), [message] * 2, flags, *offsets, *state)
+            state = [end[0], lax.ppermute(end[0], "tm", route)]
+        offsets = held[first - 1 : first - 1 + steps]
+        message = shape(2, tiles_in(steps), rows_each, cols)
+        far, near = call(functools.partial(edge_kernel, kind, steps), [message] * 2, flags, offsets, *state)
         far, near = swapped(far, near)
-        kept = steps + (first + steps == count)
-        block, end = call(
+        closing = first + steps == count
+        block, *end = call(
             functools.partial(block_kernel, kind, steps),
-            [shape(kept, 2, depth + 2, rows_each, cols), shape(2, depth, rows_each, cols)],
-            flags, *offsets, *state, far, near,
+            [shape(steps + closing, 2, depth + 2, rows_each, cols)]
+            + [shape(2, depth, rows_each, cols)] * (not closing),
+            flags, offsets, *state, far, near,
         )
         ends.append(block)
     back = lax.all_to_all(jnp.concatenate(ends), "tm", 0, 0, tiled=True)
     (result,) = call(
-        functools.partial(result_kernel, count), [shape(1, 3, 2, depth, rows, cols)], flags, back, *inner_rest, *edges_rest
+        functools.partial(result_kernel, count), [shape(1, 3, 2, depth, rows, cols)], flags, back, offset, mid,
+        result_outside=True,
+        scratch=[pltpu.VMEM((depth, 3, 2, rows, cols), jnp.float32), pltpu.SemaphoreType.DMA((depth,))],
     )
     return result
 

time: 186 us -> 180 us (0.968)
  blocking collectives: 28.6 us -> 67.5 us
  starting transfers between devices: 86.7 us -> 66.4 us
  waiting for transfers between devices: 54.4 us -> 36.1 us
  local copies, waits for them, and re-layouts: 6 us -> 2.63 us
  Pallas kernels: 8.88 us -> 6.24 us
    all_to_all x0 -> x1, blocking collectives: none -> 38.9 us  [local(): held = lax.all_to_all(send, 'tm', 0, 0, tiled=True)]
    all_to_all x2 -> x0, waiting for transfers between devices: 19.4 us -> none  [offsets_on(): return (lax.all_to_all(send, 'tm', 0, 0, tiled=True), rest)]
    all_to_all x2 -> x0, starting transfers between devices: 15.5 us -> none  [offsets_on(): return (lax.all_to_all(send, 'tm', 0, 0, tiled=True), rest)]
    ppermute x7, starting transfers between devices: 40.5 us -> 36.6 us  [swapped(): lax.ppermute(near, 'space', [(i + j, i + 1 - j) for i in range(0, count,...]
    pallas_call x16 -> x15, Pallas kernels: 8.88 us -> 6.24 us  [call(): pl.pallas_call(kernel, out_shape=tuple(out_shapes), in_specs=[pl.BlockSpe...]
    slice x4 -> x2, local copies, waits for them, and re-layouts: 1.99 us -> 0.08 us  [local(): offsets = held[first - 1:first - 1 + steps]]
  transfers between devices with their start and end apart: 21 -> 19, of which waited for: 14 -> 12; matrix products, arithmetic and copies ran while one was open for 1% -> 0% of each run, Pallas kernels for 2% -> 1%
where the time goes in v2:
time: 180 us; the launch traced here: 179 us
  blocking collectives  67.5 us (38%)
  starting transfers between devices  66.4 us (37%)
  waiting for transfers between devices  36.1 us (20%)
  Pallas kernels  6.24 us (3%)
  local copies, waits for them, and re-layouts  2.63 us (1%)
    all_to_all x1, blocking collectives, local(): held = lax.all_to_all(send, 'tm', 0, 0, tiled=True)  38.9 us
    ppermute x7, starting transfers between devices, swapped(): lax.ppermute(near, 'space', [(i + j, i + 1 - j) for i in range(0, count,...  36.6 us
    all_to_all x1, blocking collectives, local(): back = lax.all_to_all(jnp.concatenate(ends), 'tm', 0, 0, tiled=True)  28.6 us
    ppermute x7, starting transfers between devices, swapped(): lax.ppermute(far, 'space', [((i + j) % count, (i + 1 - j) % count) for i...  13.8 us
    ppermute x3, waiting for transfers between devices, local(): state = [end[0], lax.ppermute(end[0], 'tm', route)]  13.2 us
    ppermute x1, waiting for transfers between devices, local(): old_first = lax.ppermute(old_first, 'tm', back_one)  9 us
    ppermute x1, starting transfers between devices, local(): old_first = lax.ppermute(old_first, 'tm', back_one)  6.94 us
    pallas_call x15, Pallas kernels, call(): pl.pallas_call(kernel, out_shape=tuple(out_shapes), in_specs=[pl.BlockSpe...  6.24 us
  transfers between devices with their start and end apart: 19, of which 12 were waited for; matrix products, arithmetic and copies ran while one was open for 0% of the time, Pallas kernels for 1%

profile of v2, /device:TPU:194, one launch (start us, length us, event | category | flops | bytes accessed | tf_op | source)
XLA Modules:
  0.0 179.3 jit_solution(11339864993920858731)
XLA Ops:
  2.8 1.9 %collective-permute-start = (f32[3,2,128,128]{3,2,1,0:T(8,128)S(1)}, f32[3,2,128,128]{3,2,1,0:T(8,128)S(1)}, u32[]{:S(2)}, u32[]{:S(2)}) collective-permute-start(f32[3,2,128,128]{3,2,1,0:T(8,128)S(1)} %get-tuple-element.35), channel_id=1, source_target_pairs={{1,2},{2,1},{3,4},{4,3},{5,6},{6,5},{7,8},{8,7},{9,10},{10,9},{11,... | collective-permute-start | bytes 1179656 | tf_op jit(solution)/shard_map/ppermute | solution.py:327
  4.8 5.6 %collective-permute-start.1 = (f32[3,2,128,128]{3,2,1,0:T(8,128)S(1)}, f32[3,2,128,128]{3,2,1,0:T(8,128)S(1)}, u32[]{:S(2)}, u32[]{:S(2)}) collective-permute-start(f32[3,2,128,128]{3,2,1,0:T(8,128)S(1)} %get-tuple-element.36), channel_id=1, source_target_pairs={{0,1},{1,0},{2,3},{3,2},{4,5},{5,4},{6,7},{7,6},{8,9},{9,8},{10,11... | collective-permute-start | bytes 1179656 | tf_op jit(solution)/shard_map/ppermute | solution.py:328
  11.6 4.5 %collective-permute-done.far_ref = f32[3,2,128,128]{3,2,1,0:T(8,128)S(1)} collective-permute-done((f32[3,2,128,128]{3,2,1,0:T(8,128)S(1)}, f32[3,2,128,128]{3,2,1,0:T(8,128)S(1)}, u32[]{:S(2)}, u32[]{:S(2)}) %collective-permute-start) | collective-permute-done | bytes 393248 | tf_op jit(solution)/shard_map/ppermute | solution.py:327
  16.2 6.9 %collective-permute-start.3 = (f32[2,4,128,128]{3,2,1,0:T(8,128)S(1)}, f32[2,4,128,128]{3,2,1,0:T(8,128)S(1)}, u32[]{:S(2)}, u32[]{:S(2)}) collective-permute-start(f32[2,4,128,128]{3,2,1,0:T(8,128)S(1)} %get-tuple-element.38), channel_id=1, source_target_pairs={{0,480},{32,0},{64,32},{96,64},{128,96},{160,128},{192,160},{224,1... | collective-permute-start | bytes 1572872 | tf_op jit(solution)/shard_map/ppermute | solution.py:356
  23.2 3.3 %collective-permute-start.2 = (f32[2,4,128,128]{3,2,1,0:T(8,128)S(1)}, f32[2,4,128,128]{3,2,1,0:T(8,128)S(1)}, u32[]{:S(2)}, u32[]{:S(2)}) collective-permute-start(f32[2,4,128,128]{3,2,1,0:T(8,128)S(1)} %get-tuple-element.37), channel_id=1, source_target_pairs={{0,480},{32,0},{64,32},{96,64},{128,96},{160,128},{192,160},{224,1... | collective-permute-start | bytes 1572872 | tf_op jit(solution)/shard_map/ppermute | solution.py:357
  26.5 9.0 %collective-permute-done.3.old_ref = f32[2,4,128,128]{3,2,1,0:T(8,128)S(1)} collective-permute-done((f32[2,4,128,128]{3,2,1,0:T(8,128)S(1)}, f32[2,4,128,128]{3,2,1,0:T(8,128)S(1)}, u32[]{:S(2)}, u32[]{:S(2)}) %collective-permute-start.3) | collective-permute-done | bytes 524320 | tf_op jit(solution)/shard_map/ppermute | solution.py:356
  36.0 1.9 %collective-permute-start.4 = (f32[2,128,128]{2,1,0:T(8,128)S(1)}, f32[2,128,128]{2,1,0:T(8,128)S(1)}, u32[]{:S(2)}, u32[]{:S(2)}) collective-permute-start(f32[2,128,128]{2,1,0:T(8,128)S(1)} %get-tuple-element.41), channel_id=1, source_target_pairs={{1,2},{2,1},{3,4},{4,3},{5,6},{6,5},{7,8},{8,7},{9,10},{10,9},{11,... | collective-permute-start | bytes 393224 | tf_op jit(solution)/shard_map/ppermute | solution.py:327
  37.9 3.6 %collective-permute-start.5 = (f32[2,128,128]{2,1,0:T(8,128)S(1)}, f32[2,128,128]{2,1,0:T(8,128)S(1)}, u32[]{:S(2)}, u32[]{:S(2)}) collective-permute-start(f32[2,128,128]{2,1,0:T(8,128)S(1)} %get-tuple-element.42), channel_id=1, source_target_pairs={{0,1},{1,0},{2,3},{3,2},{4,5},{5,4},{6,7},{7,6},{8,9},{9,8},{10,11... | collective-permute-start | bytes 393224 | tf_op jit(solution)/shard_map/ppermute | solution.py:328
  41.5 3.8 %collective-permute-done.2.old_ref = f32[2,4,128,128]{3,2,1,0:T(8,128)S(1)} collective-permute-done((f32[2,4,128,128]{3,2,1,0:T(8,128)S(1)}, f32[2,4,128,128]{3,2,1,0:T(8,128)S(1)}, u32[]{:S(2)}, u32[]{:S(2)}) %collective-permute-start.2) | collective-permute-done | bytes 524320 | tf_op jit(solution)/shard_map/ppermute | solution.py:357
  46.7 2.3 %collective-permute-start.6 = (f32[2,128,128]{2,1,0:T(8,128)S(1)}, f32[2,128,128]{2,1,0:T(8,128)S(1)}, u32[]{:S(2)}, u32[]{:S(2)}) collective-permute-start(f32[2,128,128]{2,1,0:T(8,128)S(1)} %get-tuple-element.45), channel_id=1, source_target_pairs={{1,2},{2,1},{3,4},{4,3},{5,6},{6,5},{7,8},{8,7},{9,10},{10,9},{11,... | collective-permute-start | bytes 393224 | tf_op jit(solution)/shard_map/ppermute | solution.py:327
  49.0 5.2 %collective-permute-start.7 = (f32[2,128,128]{2,1,0:T(8,128)S(1)}, f32[2,128,128]{2,1,0:T(8,128)S(1)}, u32[]{:S(2)}, u32[]{:S(2)}) collective-permute-start(f32[2,128,128]{2,1,0:T(8,128)S(1)} %get-tuple-element.46), channel_id=1, source_target_pairs={{0,1},{1,0},{2,3},{3,2},{4,5},{5,4},{6,7},{7,6},{8,9},{9,8},{10,11... | collective-permute-start | bytes 393224 | tf_op jit(solution)/shard_map/ppermute | solution.py:328
  55.8 38.9 %all_to_all.10 = f32[16,2,4,16,128]{4,3,2,1,0:T(8,128)S(1)} all-to-all(f32[16,2,4,16,128]{4,3,2,1,0:T(8,128)S(1)} %get-tuple-element.48), channel_id=1, replica_groups=mesh['tm'=16,'space'=32] {'tm'}, dimensions={0} | all-to-all | bytes 2097152 | tf_op jit(solution)/shard_map/all_to_all | solution.py:374
  94.8 1.9 %collective-permute-start.8 = (f32[2,16,8,128]{3,2,1,0:T(8,128)S(1)}, f32[2,16,8,128]{3,2,1,0:T(8,128)S(1)}, u32[]{:S(2)}, u32[]{:S(2)}) collective-permute-start(f32[2,16,8,128]{3,2,1,0:T(8,128)S(1)} %get-tuple-element.49), channel_id=1, source_target_pairs={{1,2},{2,1},{3,4},{4,3},{5,6},{6,5},{7,8},{8,7},{9,10},{10,9},{11,... | collective-permute-start | bytes 393224 | tf_op jit(solution)/shard_map/ppermute | solution.py:327
  96.7 5.7 %collective-permute-start.9 = (f32[2,16,8,128]{3,2,1,0:T(8,128)S(1)}, f32[2,16,8,128]{3,2,1,0:T(8,128)S(1)}, u32[]{:S(2)}, u32[]{:S(2)}) collective-permute-start(f32[2,16,8,128]{3,2,1,0:T(8,128)S(1)} %get-tuple-element.50), channel_id=1, source_target_pairs={{0,1},{1,0},{2,3},{3,2},{4,5},{5,4},{6,7},{7,6},{8,9},{9,8},{10,11... | collective-permute-start | bytes 393224 | tf_op jit(solution)/shard_map/ppermute | solution.py:328
  105.7 3.9 %collective-permute-done.10.refs_1_ = f32[2,4,8,128]{3,2,1,0:T(8,128)S(1)} collective-permute-done((f32[2,4,8,128]{3,2,1,0:T(8,128)S(1)}, f32[2,4,8,128]{3,2,1,0:T(8,128)S(1)}, u32[]{:S(2)}, u32[]{:S(2)}) %collective-permute-start.10) | collective-permute-done | bytes 32800 | tf_op jit(solution)/shard_map/ppermute | solution.py:382
  111.6 5.5 %collective-permute-start.12 = (f32[2,16,8,128]{3,2,1,0:T(8,128)S(1)}, f32[2,16,8,128]{3,2,1,0:T(8,128)S(1)}, u32[]{:S(2)}, u32[]{:S(2)}) collective-permute-start(f32[2,16,8,128]{3,2,1,0:T(8,128)S(1)} %get-tuple-element.54), channel_id=1, source_target_pairs={{0,1},{1,0},{2,3},{3,2},{4,5},{5,4},{6,7},{7,6},{8,9},{9,8},{10,11... | collective-permute-start | bytes 393224 | tf_op jit(solution)/shard_map/ppermute | solution.py:328
  120.4 5.4 %collective-permute-done.13.refs_1_ = f32[2,4,8,128]{3,2,1,0:T(8,128)S(1)} collective-permute-done((f32[2,4,8,128]{3,2,1,0:T(8,128)S(1)}, f32[2,4,8,128]{3,2,1,0:T(8,128)S(1)}, u32[]{:S(2)}, u32[]{:S(2)}) %collective-permute-start.13) | collective-permute-done | bytes 32800 | tf_op jit(solution)/shard_map/ppermute | solution.py:382
  125.9 1.9 %collective-permute-start.14 = (f32[2,16,8,128]{3,2,1,0:T(8,128)S(1)}, f32[2,16,8,128]{3,2,1,0:T(8,128)S(1)}, u32[]{:S(2)}, u32[]{:S(2)}) collective-permute-start(f32[2,16,8,128]{3,2,1,0:T(8,128)S(1)} %get-tuple-element.57), channel_id=1, source_target_pairs={{1,2},{2,1},{3,4},{4,3},{5,6},{6,5},{7,8},{8,7},{9,10},{10,9},{11,... | collective-permute-start | bytes 393224 | tf_op jit(solution)/shard_map/ppermute | solution.py:327
  127.8 5.5 %collective-permute-start.15 = (f32[2,16,8,128]{3,2,1,0:T(8,128)S(1)}, f32[2,16,8,128]{3,2,1,0:T(8,128)S(1)}, u32[]{:S(2)}, u32[]{:S(2)}) collective-permute-start(f32[2,16,8,128]{3,2,1,0:T(8,128)S(1)} %get-tuple-element.58), channel_id=1, source_target_pairs={{0,1},{1,0},{2,3},{3,2},{4,5},{5,4},{6,7},{7,6},{8,9},{9,8},{10,11... | collective-permute-start | bytes 393224 | tf_op jit(solution)/shard_map/ppermute | solution.py:328
  134.7 1.9 %collective-permute-start.16 = (f32[2,4,8,128]{3,2,1,0:T(8,128)S(1)}, f32[2,4,8,128]{3,2,1,0:T(8,128)S(1)}, u32[]{:S(2)}, u32[]{:S(2)}) collective-permute-start(f32[2,4,8,128]{3,2,1,0:T(8,128)S(1)} %get-tuple-element.60.refs_0_), channel_id=1, source_target_pairs={{0,32},{64,0},{128,64},{192,128},{256,192},{320,256},{384,320},{44... | collective-permute-start | bytes 98312 | tf_op jit(solution)/shard_map/ppermute | solution.py:382
  136.7 3.9 %collective-permute-done.16.refs_1_ = f32[2,4,8,128]{3,2,1,0:T(8,128)S(1)} collective-permute-done((f32[2,4,8,128]{3,2,1,0:T(8,128)S(1)}, f32[2,4,8,128]{3,2,1,0:T(8,128)S(1)}, u32[]{:S(2)}, u32[]{:S(2)}) %collective-permute-start.16) | collective-permute-done | bytes 32800 | tf_op jit(solution)/shard_map/ppermute | solution.py:382
  140.5 1.9 %collective-permute-start.17 = (f32[2,9,8,128]{3,2,1,0:T(8,128)S(1)}, f32[2,9,8,128]{3,2,1,0:T(8,128)S(1)}, u32[]{:S(2)}, u32[]{:S(2)}) collective-permute-start(f32[2,9,8,128]{3,2,1,0:T(8,128)S(1)} %get-tuple-element.61), channel_id=1, source_target_pairs={{1,2},{2,1},{3,4},{4,3},{5,6},{6,5},{7,8},{8,7},{9,10},{10,9},{11,... | collective-permute-start | bytes 221192 | tf_op jit(solution)/shard_map/ppermute | solution.py:327
  142.5 5.6 %collective-permute-start.18 = (f32[2,9,8,128]{3,2,1,0:T(8,128)S(1)}, f32[2,9,8,128]{3,2,1,0:T(8,128)S(1)}, u32[]{:S(2)}, u32[]{:S(2)}) collective-permute-start(f32[2,9,8,128]{3,2,1,0:T(8,128)S(1)} %get-tuple-element.62), channel_id=1, source_target_pairs={{0,1},{1,0},{2,3},{3,2},{4,5},{5,4},{6,7},{7,6},{8,9},{9,8},{10,11... | collective-permute-start | bytes 221192 | tf_op jit(solution)/shard_map/ppermute | solution.py:328
  149.4 28.6 %all_to_all.11.come_ref = f32[16,2,6,8,128]{4,3,2,1,0:T(8,128)S(1)} all-to-all(f32[16,2,6,8,128]{4,3,2,1,0:T(8,128)S(1)} %pad_maximum_fusion), channel_id=1, replica_groups=mesh['tm'=16,'space'=32] {'tm'}, dimensions={0} | all-to-all | bytes 1572864 | tf_op jit(solution)/shard_map/all_to_all | solution.py:395
  (43 shorter events, 20.4 us)
Async XLA Ops:
  0.2 1.4 copy-start
  1.6 1.0 copy-start.1
  2.8 13.3 %collective-permute-start = (f32[3,2,128,128]{3,2,1,0:T(8,128)S(1)}, f32[3,2,128,128]{3,2,1,0:T(8,128)S(1)}, u32[]{:S(2)}, u32[]{:S(2)}) collective-permute-start(f32[3,2,128,128]{3,2,1,0:T(8,128)S(1)} %get-tuple-element.35), channel_id=1, source_target_pairs={{1,2},{2,1},{3,4},{4,3},{5,6},{6,5},{7,8},{8,7},{9,10},{10,9},{11,... | collective-permute-start | bytes 1179656 | tf_op jit(solution)/shard_map/ppermute | solution.py:327
  4.8 11.4 %collective-permute-start.1 = (f32[3,2,128,128]{3,2,1,0:T(8,128)S(1)}, f32[3,2,128,128]{3,2,1,0:T(8,128)S(1)}, u32[]{:S(2)}, u32[]{:S(2)}) collective-permute-start(f32[3,2,128,128]{3,2,1,0:T(8,128)S(1)} %get-tuple-element.36), channel_id=1, source_target_pairs={{0,1},{1,0},{2,3},{3,2},{4,5},{5,4},{6,7},{7,6},{8,9},{9,8},{10,11... | collective-permute-start | bytes 1179656 | tf_op jit(solution)/shard_map/ppermute | solution.py:328
  16.2 19.3 %collective-permute-start.3 = (f32[2,4,128,128]{3,2,1,0:T(8,128)S(1)}, f32[2,4,128,128]{3,2,1,0:T(8,128)S(1)}, u32[]{:S(2)}, u32[]{:S(2)}) collective-permute-start(f32[2,4,128,128]{3,2,1,0:T(8,128)S(1)} %get-tuple-element.38), channel_id=1, source_target_pairs={{0,480},{32,0},{64,32},{96,64},{128,96},{160,128},{192,160},{224,1... | collective-permute-start | bytes 1572872 | tf_op jit(solution)/shard_map/ppermute | solution.py:356
  23.2 22.1 %collective-permute-start.2 = (f32[2,4,128,128]{3,2,1,0:T(8,128)S(1)}, f32[2,4,128,128]{3,2,1,0:T(8,128)S(1)}, u32[]{:S(2)}, u32[]{:S(2)}) collective-permute-start(f32[2,4,128,128]{3,2,1,0:T(8,128)S(1)} %get-tuple-element.37), channel_id=1, source_target_pairs={{0,480},{32,0},{64,32},{96,64},{128,96},{160,128},{192,160},{224,1... | collective-permute-start | bytes 1572872 | tf_op jit(solution)/shard_map/ppermute | solution.py:357
  36.0 10.2 %collective-permute-start.4 = (f32[2,128,128]{2,1,0:T(8,128)S(1)}, f32[2,128,128]{2,1,0:T(8,128)S(1)}, u32[]{:S(2)}, u32[]{:S(2)}) collective-permute-start(f32[2,128,128]{2,1,0:T(8,128)S(1)} %get-tuple-element.41), channel_id=1, source_target_pairs={{1,2},{2,1},{3,4},{4,3},{5,6},{6,5},{7,8},{8,7},{9,10},{10,9},{11,... | collective-permute-start | bytes 393224 | tf_op jit(solution)/shard_map/ppermute | solution.py:327
  37.9 8.3 %collective-permute-start.5 = (f32[2,128,128]{2,1,0:T(8,128)S(1)}, f32[2,128,128]{2,1,0:T(8,128)S(1)}, u32[]{:S(2)}, u32[]{:S(2)}) collective-permute-start(f32[2,128,128]{2,1,0:T(8,128)S(1)} %get-tuple-element.42), channel_id=1, source_target_pairs={{0,1},{1,0},{2,3},{3,2},{4,5},{5,4},{6,7},{7,6},{8,9},{9,8},{10,11... | collective-permute-start | bytes 393224 | tf_op jit(solution)/shard_map/ppermute | solution.py:328
  46.7 7.5 %collective-permute-start.6 = (f32[2,128,128]{2,1,0:T(8,128)S(1)}, f32[2,128,128]{2,1,0:T(8,128)S(1)}, u32[]{:S(2)}, u32[]{:S(2)}) collective-permute-start(f32[2,128,128]{2,1,0:T(8,128)S(1)} %get-tuple-element.45), channel_id=1, source_target_pairs={{1,2},{2,1},{3,4},{4,3},{5,6},{6,5},{7,8},{8,7},{9,10},{10,9},{11,... | collective-permute-start | bytes 393224 | tf_op jit(solution)/shard_map/ppermute | solution.py:327
  49.0 6.2 %collective-permute-start.7 = (f32[2,128,128]{2,1,0:T(8,128)S(1)}, f32[2,128,128]{2,1,0:T(8,128)S(1)}, u32[]{:S(2)}, u32[]{:S(2)}) collective-permute-start(f32[2,128,128]{2,1,0:T(8,128)S(1)} %get-tuple-element.46), channel_id=1, source_target_pairs={{0,1},{1,0},{2,3},{3,2},{4,5},{5,4},{6,7},{7,6},{8,9},{9,8},{10,11... | collective-permute-start | bytes 393224 | tf_op jit(solution)/shard_map/ppermute | solution.py:328
  94.8 7.6 %collective-permute-start.8 = (f32[2,16,8,128]{3,2,1,0:T(8,128)S(1)}, f32[2,16,8,128]{3,2,1,0:T(8,128)S(1)}, u32[]{:S(2)}, u32[]{:S(2)}) collective-permute-start(f32[2,16,8,128]{3,2,1,0:T(8,128)S(1)} %get-tuple-element.49), channel_id=1, source_target_pairs={{1,2},{2,1},{3,4},{4,3},{5,6},{6,5},{7,8},{8,7},{9,10},{10,9},{11,... | collective-permute-start | bytes 393224 | tf_op jit(solution)/shard_map/ppermute | solution.py:327
  96.7 6.6 %collective-permute-start.9 = (f32[2,16,8,128]{3,2,1,0:T(8,128)S(1)}, f32[2,16,8,128]{3,2,1,0:T(8,128)S(1)}, u32[]{:S(2)}, u32[]{:S(2)}) collective-permute-start(f32[2,16,8,128]{3,2,1,0:T(8,128)S(1)} %get-tuple-element.50), channel_id=1, source_target_pairs={{0,1},{1,0},{2,3},{3,2},{4,5},{5,4},{6,7},{7,6},{8,9},{9,8},{10,11... | collective-permute-start | bytes 393224 | tf_op jit(solution)/shard_map/ppermute | solution.py:328
  103.8 5.8 %collective-permute-start.10 = (f32[2,4,8,128]{3,2,1,0:T(8,128)S(1)}, f32[2,4,8,128]{3,2,1,0:T(8,128)S(1)}, u32[]{:S(2)}, u32[]{:S(2)}) collective-permute-start(f32[2,4,8,128]{3,2,1,0:T(8,128)S(1)} %get-tuple-element.52.refs_0_), channel_id=1, source_target_pairs={{0,32},{64,0},{128,64},{192,128},{256,192},{320,256},{384,320},{44... | collective-permute-start | bytes 98312 | tf_op jit(solution)/shard_map/ppermute | solution.py:382
  109.7 7.4 %collective-permute-start.11 = (f32[2,16,8,128]{3,2,1,0:T(8,128)S(1)}, f32[2,16,8,128]{3,2,1,0:T(8,128)S(1)}, u32[]{:S(2)}, u32[]{:S(2)}) collective-permute-start(f32[2,16,8,128]{3,2,1,0:T(8,128)S(1)} %get-tuple-element.53), channel_id=1, source_target_pairs={{1,2},{2,1},{3,4},{4,3},{5,6},{6,5},{7,8},{8,7},{9,10},{10,9},{11,... | collective-permute-start | bytes 393224 | tf_op jit(solution)/shard_map/ppermute | solution.py:327
  111.6 6.5 %collective-permute-start.12 = (f32[2,16,8,128]{3,2,1,0:T(8,128)S(1)}, f32[2,16,8,128]{3,2,1,0:T(8,128)S(1)}, u32[]{:S(2)}, u32[]{:S(2)}) collective-permute-start(f32[2,16,8,128]{3,2,1,0:T(8,128)S(1)} %get-tuple-element.54), channel_id=1, source_target_pairs={{0,1},{1,0},{2,3},{3,2},{4,5},{5,4},{6,7},{7,6},{8,9},{9,8},{10,11... | collective-permute-start | bytes 393224 | tf_op jit(solution)/shard_map/ppermute | solution.py:328
  118.5 7.3 %collective-permute-start.13 = (f32[2,4,8,128]{3,2,1,0:T(8,128)S(1)}, f32[2,4,8,128]{3,2,1,0:T(8,128)S(1)}, u32[]{:S(2)}, u32[]{:S(2)}) collective-permute-start(f32[2,4,8,128]{3,2,1,0:T(8,128)S(1)} %get-tuple-element.56.refs_0_), channel_id=1, source_target_pairs={{0,64},{64,128},{128,192},{192,256},{256,320},{320,384},{384,448},... | collective-permute-start | bytes 98312 | tf_op jit(solution)/shard_map/ppermute | solution.py:382
  125.9 7.4 %collective-permute-start.14 = (f32[2,16,8,128]{3,2,1,0:T(8,128)S(1)}, f32[2,16,8,128]{3,2,1,0:T(8,128)S(1)}, u32[]{:S(2)}, u32[]{:S(2)}) collective-permute-start(f32[2,16,8,128]{3,2,1,0:T(8,128)S(1)} %get-tuple-element.57), channel_id=1, source_target_pairs={{1,2},{2,1},{3,4},{4,3},{5,6},{6,5},{7,8},{8,7},{9,10},{10,9},{11,... | collective-permute-start | bytes 393224 | tf_op jit(solution)/shard_map/ppermute | solution.py:327
  127.8 6.5 %collective-permute-start.15 = (f32[2,16,8,128]{3,2,1,0:T(8,128)S(1)}, f32[2,16,8,128]{3,2,1,0:T(8,128)S(1)}, u32[]{:S(2)}, u32[]{:S(2)}) collective-permute-start(f32[2,16,8,128]{3,2,1,0:T(8,128)S(1)} %get-tuple-element.58), channel_id=1, source_target_pairs={{0,1},{1,0},{2,3},{3,2},{4,5},{5,4},{6,7},{7,6},{8,9},{9,8},{10,11... | collective-permute-start | bytes 393224 | tf_op jit(solution)/shard_map/ppermute | solution.py:328
  134.7 5.8 %collective-permute-start.16 = (f32[2,4,8,128]{3,2,1,0:T(8,128)S(1)}, f32[2,4,8,128]{3,2,1,0:T(8,128)S(1)}, u32[]{:S(2)}, u32[]{:S(2)}) collective-permute-start(f32[2,4,8,128]{3,2,1,0:T(8,128)S(1)} %get-tuple-element.60.refs_0_), channel_id=1, source_target_pairs={{0,32},{64,0},{128,64},{192,128},{256,192},{320,256},{384,320},{44... | collective-permute-start | bytes 98312 | tf_op jit(solution)/shard_map/ppermute | solution.py:382
  140.5 7.5 %collective-permute-start.17 = (f32[2,9,8,128]{3,2,1,0:T(8,128)S(1)}, f32[2,9,8,128]{3,2,1,0:T(8,128)S(1)}, u32[]{:S(2)}, u32[]{:S(2)}) collective-permute-start(f32[2,9,8,128]{3,2,1,0:T(8,128)S(1)} %get-tuple-element.61), channel_id=1, source_target_pairs={{1,2},{2,1},{3,4},{4,3},{5,6},{6,5},{7,8},{8,7},{9,10},{10,9},{11,... | collective-permute-start | bytes 221192 | tf_op jit(solution)/shard_map/ppermute | solution.py:327
  142.5 6.5 %collective-permute-start.18 = (f32[2,9,8,128]{3,2,1,0:T(8,128)S(1)}, f32[2,9,8,128]{3,2,1,0:T(8,128)S(1)}, u32[]{:S(2)}, u32[]{:S(2)}) collective-permute-start(f32[2,9,8,128]{3,2,1,0:T(8,128)S(1)} %get-tuple-element.62), channel_id=1, source_target_pairs={{0,1},{1,0},{2,3},{3,2},{4,5},{5,4},{6,7},{7,6},{8,9},{9,8},{10,11... | collective-permute-start | bytes 221192 | tf_op jit(solution)/shard_map/ppermute | solution.py:328

commit v3 on v2

--- a/solution.py
+++ b/solution.py
@@ -25,6 +25,7 @@
 rows_each = 8
 block_len = 4
 half_rows = 4
+rows_sent = 14
 vmem_bytes = 16 * 1024 * 1024
 
 
@@ -37,19 +38,16 @@
 
 
 def chain_blocks(count):
-    blocks, first = [], 1
-    while first < count:
-        steps = min(block_len, count - first)
-        blocks.append((first, steps, len(blocks) % 2))
-        first += steps
-    return blocks
+    ends = [min(b, count) for b in range(block_len, count + block_len, block_len)]
+    firsts = [1] + ends[:-1]
+    return [(a, b - a, n % 2) for n, (a, b) in enumerate(zip(firsts, ends)) if b > a]
 
 
 even, last, offset_moved, end_moved = range(4)
 
 
 def kind_of(slab):
-    return jnp.where(slab > 0, ((slab - 1) // block_len) & 1, 2)
+    return (slab // block_len) & 1
 
 
 def flag(flags_ref, which, like):
@@ -200,10 +198,14 @@
             offset = jnp.where(flag(flags_ref, last, offset), first, offset)
             moved = pltpu.roll(offset, half_rows, 0), pltpu.roll(offset, rows_each, 0)
             offset = jnp.where(flag(flags_ref, offset_moved, offset), *moved)
-            offset = jnp.concatenate([offset, offset[:rows_each]], axis=0)
+            offset = jnp.concatenate([offset, offset[: 2 * rows_each]], axis=0)
+            place = rows_sent * p
+            shift = (place - 1) % rows_each
+            if shift:
+                offset = pltpu.roll(offset, shift, 0)
             for i in range(count):
-                r = rank_of(i, count)
-                send_ref[i, f, p] = offset[r * rows_each : (r + 2) * rows_each]
+                start = rank_of(i, count) * rows_each + 1 + shift
+                send_ref[i, f, place : place + rows_sent] = offset[start : start + rows_sent]
             mid_ref[f, p] = node_ref[f, p] - 0.5 * (start_ref[f, p] + x_ref[f, p])
 
 
@@ -216,10 +218,22 @@
 
 
 def rows_of(kind, state, offsets_ref):
+    kept = 2 * rows_each
+
+    def unpacked(ref, *at):
+        p = at[-1]
+        total = ref.shape[-2]
+        start = min(max(rows_sent * p - 1, 0), total - kept)
+        rows = ref[(*at[:-1], slice(start, start + kept))]
+        shift = (start + 1 - rows_sent * p) % kept
+        return pltpu.roll(rows, shift, 0) if shift else rows
+
     def plane(a, f, p):
         if a:
-            return offsets_ref[a - 1, f, p]
-        return state[0][f, p] if len(state) == 1 else joined(kind, state[0][f, p], state[1][f, p])
+            return unpacked(offsets_ref, a - 1, f, p)
+        if len(state) == 1:
+            return unpacked(state[0], f, p)
+        return joined(kind, state[0][f, p], state[1][f, p])
 
     return plane
 
@@ -230,7 +244,7 @@
 
 def edge_kernel(kind, steps, flags_ref, offsets_ref, *refs):
     far_ref, near_ref = refs[-2:]
-    depth = offsets_ref.shape[2]
+    depth = offsets_ref.shape[2] // rows_sent
     plane = rows_of(kind, refs[:-2], offsets_ref)
     at = 0
     for a, n in edge_lists(steps):
@@ -249,8 +263,10 @@
 def block_kernel(kind, steps, flags_ref, offsets_ref, *refs):
     closing = refs[-1].shape[0] > steps
     far_ref, near_ref, out_ref, end_ref = (*refs[-3:], None) if closing else refs[-4:]
-    depth = offsets_ref.shape[2]
-    plane = rows_of(kind, refs[: -3 if closing else -4], offsets_ref)
+    depth = offsets_ref.shape[2] // rows_sent
+    state = refs[: -3 if closing else -4]
+    opening = len(state) == 1
+    plane = rows_of(kind, state, offsets_ref)
     at = {}
     place = 0
     for a, n in edge_lists(steps):
@@ -276,8 +292,11 @@
 
     state = [extended(0, f) for f in range(2)]
     for f in range(2):
-        own = slice(rows_each, None) if kind == 0 else slice(None, rows_each)
-        out_ref[0, f] = state[f][steps - 1 : steps + depth + 1, own]
+        before = state[f][steps - 1 : steps + depth + 1]
+        if opening:
+            out_ref[0, f] = pltpu.roll(before, 2 * rows_each - half_rows, 1)[:, :rows_each]
+        else:
+            out_ref[0, f] = before[:, rows_each:] if kind == 0 else before[:, :rows_each]
     for j in range(1, steps + 1):
         middle = [x[1:-1] for x in state]
         rate = plane_rates([x[:-2] for x in state], middle, [x[2:] for x in state])
@@ -368,7 +387,7 @@
     far, near = swapped(far, near)
     send, offset, mid = call(
         functools.partial(offset_kernel, count),
-        [shape(count, 2, depth, 2 * rows_each, cols), grid, grid],
+        [shape(count, 2, depth * rows_sent, cols), grid, grid],
         flags, fine2, far, near, total, fine0, fine1, rate0,
     )
     held = lax.all_to_all(send, "tm", 0, 0, tiled=True)

time: 180 us -> 177 us (0.983)
  blocking collectives: 67.5 us -> 64.7 us
    all_to_all x1, blocking collectives: 38.9 us -> 35.9 us  [local(): held = lax.all_to_all(send, 'tm', 0, 0, tiled=True)]
where the time goes in v3:
time: 177 us; the launch traced here: 176 us
  starting transfers between devices  66.1 us (37%)
  blocking collectives  64.7 us (37%)
  waiting for transfers between devices  35.8 us (20%)
  Pallas kernels  6.31 us (4%)
  local copies, waits for them, and re-layouts  2.61 us (1%)
    ppermute x7, starting transfers between devices, swapped(): lax.ppermute(near, 'space', [(i + j, i + 1 - j) for i in range(0, count,...  36.1 us
    all_to_all x1, blocking collectives, local(): held = lax.all_to_all(send, 'tm', 0, 0, tiled=True)  35.9 us
    all_to_all x1, blocking collectives, local(): back = lax.all_to_all(jnp.concatenate(ends), 'tm', 0, 0, tiled=True)  28.8 us
    ppermute x7, starting transfers between devices, swapped(): lax.ppermute(far, 'space', [((i + j) % count, (i + 1 - j) % count) for i...  13.8 us
    ppermute x3, waiting for transfers between devices, local(): state = [end[0], lax.ppermute(end[0], 'tm', route)]  12.9 us
    ppermute x1, waiting for transfers between devices, local(): old_first = lax.ppermute(old_first, 'tm', back_one)  9 us
    ppermute x1, starting transfers between devices, local(): old_first = lax.ppermute(old_first, 'tm', back_one)  6.94 us
    pallas_call x15, Pallas kernels, call(): pl.pallas_call(kernel, out_shape=tuple(out_shapes), in_specs=[pl.BlockSpe...  6.31 us
  transfers between devices with their start and end apart: 19, of which 12 were waited for; matrix products, arithmetic and copies ran while one was open for 0% of the time, Pallas kernels for 1%

profile of v3, /device:TPU:194, one launch (start us, length us, event | category | flops | bytes accessed | tf_op | source)
XLA Modules:
  0.0 176.0 jit_solution(14214804388555843696)
XLA Ops:
  2.8 1.9 %collective-permute-start = (f32[3,2,128,128]{3,2,1,0:T(8,128)S(1)}, f32[3,2,128,128]{3,2,1,0:T(8,128)S(1)}, u32[]{:S(2)}, u32[]{:S(2)}) collective-permute-start(f32[3,2,128,128]{3,2,1,0:T(8,128)S(1)} %get-tuple-element.35), channel_id=1, source_target_pairs={{1,2},{2,1},{3,4},{4,3},{5,6},{6,5},{7,8},{8,7},{9,10},{10,9},{11,... | collective-permute-start | bytes 1179656 | tf_op jit(solution)/shard_map/ppermute | solution.py:346
  4.8 5.6 %collective-permute-start.1 = (f32[3,2,128,128]{3,2,1,0:T(8,128)S(1)}, f32[3,2,128,128]{3,2,1,0:T(8,128)S(1)}, u32[]{:S(2)}, u32[]{:S(2)}) collective-permute-start(f32[3,2,128,128]{3,2,1,0:T(8,128)S(1)} %get-tuple-element.36), channel_id=1, source_target_pairs={{0,1},{1,0},{2,3},{3,2},{4,5},{5,4},{6,7},{7,6},{8,9},{9,8},{10,11... | collective-permute-start | bytes 1179656 | tf_op jit(solution)/shard_map/ppermute | solution.py:347
  11.6 4.5 %collective-permute-done.far_ref = f32[3,2,128,128]{3,2,1,0:T(8,128)S(1)} collective-permute-done((f32[3,2,128,128]{3,2,1,0:T(8,128)S(1)}, f32[3,2,128,128]{3,2,1,0:T(8,128)S(1)}, u32[]{:S(2)}, u32[]{:S(2)}) %collective-permute-start) | collective-permute-done | bytes 393248 | tf_op jit(solution)/shard_map/ppermute | solution.py:346
  16.2 6.9 %collective-permute-start.3 = (f32[2,4,128,128]{3,2,1,0:T(8,128)S(1)}, f32[2,4,128,128]{3,2,1,0:T(8,128)S(1)}, u32[]{:S(2)}, u32[]{:S(2)}) collective-permute-start(f32[2,4,128,128]{3,2,1,0:T(8,128)S(1)} %get-tuple-element.38), channel_id=1, source_target_pairs={{0,480},{32,0},{64,32},{96,64},{128,96},{160,128},{192,160},{224,1... | collective-permute-start | bytes 1572872 | tf_op jit(solution)/shard_map/ppermute | solution.py:375
  23.2 3.3 %collective-permute-start.2 = (f32[2,4,128,128]{3,2,1,0:T(8,128)S(1)}, f32[2,4,128,128]{3,2,1,0:T(8,128)S(1)}, u32[]{:S(2)}, u32[]{:S(2)}) collective-permute-start(f32[2,4,128,128]{3,2,1,0:T(8,128)S(1)} %get-tuple-element.37), channel_id=1, source_target_pairs={{0,480},{32,0},{64,32},{96,64},{128,96},{160,128},{192,160},{224,1... | collective-permute-start | bytes 1572872 | tf_op jit(solution)/shard_map/ppermute | solution.py:376
  26.5 9.0 %collective-permute-done.3.old_ref = f32[2,4,128,128]{3,2,1,0:T(8,128)S(1)} collective-permute-done((f32[2,4,128,128]{3,2,1,0:T(8,128)S(1)}, f32[2,4,128,128]{3,2,1,0:T(8,128)S(1)}, u32[]{:S(2)}, u32[]{:S(2)}) %collective-permute-start.3) | collective-permute-done | bytes 524320 | tf_op jit(solution)/shard_map/ppermute | solution.py:375
  36.0 1.9 %collective-permute-start.4 = (f32[2,128,128]{2,1,0:T(8,128)S(1)}, f32[2,128,128]{2,1,0:T(8,128)S(1)}, u32[]{:S(2)}, u32[]{:S(2)}) collective-permute-start(f32[2,128,128]{2,1,0:T(8,128)S(1)} %get-tuple-element.41), channel_id=1, source_target_pairs={{1,2},{2,1},{3,4},{4,3},{5,6},{6,5},{7,8},{8,7},{9,10},{10,9},{11,... | collective-permute-start | bytes 393224 | tf_op jit(solution)/shard_map/ppermute | solution.py:346
  37.9 3.6 %collective-permute-start.5 = (f32[2,128,128]{2,1,0:T(8,128)S(1)}, f32[2,128,128]{2,1,0:T(8,128)S(1)}, u32[]{:S(2)}, u32[]{:S(2)}) collective-permute-start(f32[2,128,128]{2,1,0:T(8,128)S(1)} %get-tuple-element.42), channel_id=1, source_target_pairs={{0,1},{1,0},{2,3},{3,2},{4,5},{5,4},{6,7},{7,6},{8,9},{9,8},{10,11... | collective-permute-start | bytes 393224 | tf_op jit(solution)/shard_map/ppermute | solution.py:347
  41.5 3.8 %collective-permute-done.2.old_ref = f32[2,4,128,128]{3,2,1,0:T(8,128)S(1)} collective-permute-done((f32[2,4,128,128]{3,2,1,0:T(8,128)S(1)}, f32[2,4,128,128]{3,2,1,0:T(8,128)S(1)}, u32[]{:S(2)}, u32[]{:S(2)}) %collective-permute-start.2) | collective-permute-done | bytes 524320 | tf_op jit(solution)/shard_map/ppermute | solution.py:376
  46.7 2.3 %collective-permute-start.6 = (f32[2,128,128]{2,1,0:T(8,128)S(1)}, f32[2,128,128]{2,1,0:T(8,128)S(1)}, u32[]{:S(2)}, u32[]{:S(2)}) collective-permute-start(f32[2,128,128]{2,1,0:T(8,128)S(1)} %get-tuple-element.45), channel_id=1, source_target_pairs={{1,2},{2,1},{3,4},{4,3},{5,6},{6,5},{7,8},{8,7},{9,10},{10,9},{11,... | collective-permute-start | bytes 393224 | tf_op jit(solution)/shard_map/ppermute | solution.py:346
  49.0 5.2 %collective-permute-start.7 = (f32[2,128,128]{2,1,0:T(8,128)S(1)}, f32[2,128,128]{2,1,0:T(8,128)S(1)}, u32[]{:S(2)}, u32[]{:S(2)}) collective-permute-start(f32[2,128,128]{2,1,0:T(8,128)S(1)} %get-tuple-element.46), channel_id=1, source_target_pairs={{0,1},{1,0},{2,3},{3,2},{4,5},{5,4},{6,7},{7,6},{8,9},{9,8},{10,11... | collective-permute-start | bytes 393224 | tf_op jit(solution)/shard_map/ppermute | solution.py:347
  55.8 35.9 %all_to_all.10 = f32[16,2,56,128]{3,2,1,0:T(8,128)S(1)} all-to-all(f32[16,2,56,128]{3,2,1,0:T(8,128)S(1)} %get-tuple-element.48), channel_id=1, replica_groups=mesh['tm'=16,'space'=32] {'tm'}, dimensions={0} | all-to-all | bytes 1835008 | tf_op jit(solution)/shard_map/all_to_all | solution.py:393
  91.8 1.9 %collective-permute-start.8 = (f32[2,9,8,128]{3,2,1,0:T(8,128)S(1)}, f32[2,9,8,128]{3,2,1,0:T(8,128)S(1)}, u32[]{:S(2)}, u32[]{:S(2)}) collective-permute-start(f32[2,9,8,128]{3,2,1,0:T(8,128)S(1)} %get-tuple-element.49), channel_id=1, source_target_pairs={{1,2},{2,1},{3,4},{4,3},{5,6},{6,5},{7,8},{8,7},{9,10},{10,9},{11,... | collective-permute-start | bytes 221192 | tf_op jit(solution)/shard_map/ppermute | solution.py:346
  93.7 5.7 %collective-permute-start.9 = (f32[2,9,8,128]{3,2,1,0:T(8,128)S(1)}, f32[2,9,8,128]{3,2,1,0:T(8,128)S(1)}, u32[]{:S(2)}, u32[]{:S(2)}) collective-permute-start(f32[2,9,8,128]{3,2,1,0:T(8,128)S(1)} %get-tuple-element.50), channel_id=1, source_target_pairs={{0,1},{1,0},{2,3},{3,2},{4,5},{5,4},{6,7},{7,6},{8,9},{9,8},{10,11... | collective-permute-start | bytes 221192 | tf_op jit(solution)/shard_map/ppermute | solution.py:347
  102.6 3.8 %collective-permute-done.10.refs_1_ = f32[2,4,8,128]{3,2,1,0:T(8,128)S(1)} collective-permute-done((f32[2,4,8,128]{3,2,1,0:T(8,128)S(1)}, f32[2,4,8,128]{3,2,1,0:T(8,128)S(1)}, u32[]{:S(2)}, u32[]{:S(2)}) %collective-permute-start.10) | collective-permute-done | bytes 32800 | tf_op jit(solution)/shard_map/ppermute | solution.py:401
  106.5 1.9 %collective-permute-start.11 = (f32[2,16,8,128]{3,2,1,0:T(8,128)S(1)}, f32[2,16,8,128]{3,2,1,0:T(8,128)S(1)}, u32[]{:S(2)}, u32[]{:S(2)}) collective-permute-start(f32[2,16,8,128]{3,2,1,0:T(8,128)S(1)} %get-tuple-element.53), channel_id=1, source_target_pairs={{1,2},{2,1},{3,4},{4,3},{5,6},{6,5},{7,8},{8,7},{9,10},{10,9},{11,... | collective-permute-start | bytes 393224 | tf_op jit(solution)/shard_map/ppermute | solution.py:346
  108.4 5.0 %collective-permute-start.12 = (f32[2,16,8,128]{3,2,1,0:T(8,128)S(1)}, f32[2,16,8,128]{3,2,1,0:T(8,128)S(1)}, u32[]{:S(2)}, u32[]{:S(2)}) collective-permute-start(f32[2,16,8,128]{3,2,1,0:T(8,128)S(1)} %get-tuple-element.54), channel_id=1, source_target_pairs={{0,1},{1,0},{2,3},{3,2},{4,5},{5,4},{6,7},{7,6},{8,9},{9,8},{10,11... | collective-permute-start | bytes 393224 | tf_op jit(solution)/shard_map/ppermute | solution.py:347
  114.8 2.2 %collective-permute-start.13 = (f32[2,4,8,128]{3,2,1,0:T(8,128)S(1)}, f32[2,4,8,128]{3,2,1,0:T(8,128)S(1)}, u32[]{:S(2)}, u32[]{:S(2)}) collective-permute-start(f32[2,4,8,128]{3,2,1,0:T(8,128)S(1)} %get-tuple-element.56.refs_0_), channel_id=1, source_target_pairs={{0,64},{64,128},{128,192},{192,256},{256,320},{320,384},{384,448},... | collective-permute-start | bytes 98312 | tf_op jit(solution)/shard_map/ppermute | solution.py:401
  116.9 5.2 %collective-permute-done.13.refs_1_ = f32[2,4,8,128]{3,2,1,0:T(8,128)S(1)} collective-permute-done((f32[2,4,8,128]{3,2,1,0:T(8,128)S(1)}, f32[2,4,8,128]{3,2,1,0:T(8,128)S(1)}, u32[]{:S(2)}, u32[]{:S(2)}) %collective-permute-start.13) | collective-permute-done | bytes 32800 | tf_op jit(solution)/shard_map/ppermute | solution.py:401
  124.1 5.5 %collective-permute-start.15 = (f32[2,16,8,128]{3,2,1,0:T(8,128)S(1)}, f32[2,16,8,128]{3,2,1,0:T(8,128)S(1)}, u32[]{:S(2)}, u32[]{:S(2)}) collective-permute-start(f32[2,16,8,128]{3,2,1,0:T(8,128)S(1)} %get-tuple-element.58), channel_id=1, source_target_pairs={{0,1},{1,0},{2,3},{3,2},{4,5},{5,4},{6,7},{7,6},{8,9},{9,8},{10,11... | collective-permute-start | bytes 393224 | tf_op jit(solution)/shard_map/ppermute | solution.py:347
  131.0 1.9 %collective-permute-start.16 = (f32[2,4,8,128]{3,2,1,0:T(8,128)S(1)}, f32[2,4,8,128]{3,2,1,0:T(8,128)S(1)}, u32[]{:S(2)}, u32[]{:S(2)}) collective-permute-start(f32[2,4,8,128]{3,2,1,0:T(8,128)S(1)} %get-tuple-element.60.refs_0_), channel_id=1, source_target_pairs={{0,32},{64,0},{128,64},{192,128},{256,192},{320,256},{384,320},{44... | collective-permute-start | bytes 98312 | tf_op jit(solution)/shard_map/ppermute | solution.py:401
  132.9 3.9 %collective-permute-done.16.refs_1_ = f32[2,4,8,128]{3,2,1,0:T(8,128)S(1)} collective-permute-done((f32[2,4,8,128]{3,2,1,0:T(8,128)S(1)}, f32[2,4,8,128]{3,2,1,0:T(8,128)S(1)}, u32[]{:S(2)}, u32[]{:S(2)}) %collective-permute-start.16) | collective-permute-done | bytes 32800 | tf_op jit(solution)/shard_map/ppermute | solution.py:401
  138.8 5.6 %collective-permute-start.18 = (f32[2,16,8,128]{3,2,1,0:T(8,128)S(1)}, f32[2,16,8,128]{3,2,1,0:T(8,128)S(1)}, u32[]{:S(2)}, u32[]{:S(2)}) collective-permute-start(f32[2,16,8,128]{3,2,1,0:T(8,128)S(1)} %get-tuple-element.62), channel_id=1, source_target_pairs={{0,1},{1,0},{2,3},{3,2},{4,5},{5,4},{6,7},{7,6},{8,9},{9,8},{10,11... | collective-permute-start | bytes 393224 | tf_op jit(solution)/shard_map/ppermute | solution.py:347
  145.8 28.8 %all_to_all.11.come_ref = f32[16,2,6,8,128]{4,3,2,1,0:T(8,128)S(1)} all-to-all(f32[16,2,6,8,128]{4,3,2,1,0:T(8,128)S(1)} %pad_maximum_fusion), channel_id=1, replica_groups=mesh['tm'=16,'space'=32] {'tm'}, dimensions={0} | all-to-all | bytes 1572864 | tf_op jit(solution)/shard_map/all_to_all | solution.py:414
  (43 shorter events, 20.4 us)
Async XLA Ops:
  0.2 1.4 copy-start
  1.6 1.0 copy-start.1
  2.8 13.3 %collective-permute-start = (f32[3,2,128,128]{3,2,1,0:T(8,128)S(1)}, f32[3,2,128,128]{3,2,1,0:T(8,128)S(1)}, u32[]{:S(2)}, u32[]{:S(2)}) collective-permute-start(f32[3,2,128,128]{3,2,1,0:T(8,128)S(1)} %get-tuple-element.35), channel_id=1, source_target_pairs={{1,2},{2,1},{3,4},{4,3},{5,6},{6,5},{7,8},{8,7},{9,10},{10,9},{11,... | collective-permute-start | bytes 1179656 | tf_op jit(solution)/shard_map/ppermute | solution.py:346
  4.8 11.4 %collective-permute-start.1 = (f32[3,2,128,128]{3,2,1,0:T(8,128)S(1)}, f32[3,2,128,128]{3,2,1,0:T(8,128)S(1)}, u32[]{:S(2)}, u32[]{:S(2)}) collective-permute-start(f32[3,2,128,128]{3,2,1,0:T(8,128)S(1)} %get-tuple-element.36), channel_id=1, source_target_pairs={{0,1},{1,0},{2,3},{3,2},{4,5},{5,4},{6,7},{7,6},{8,9},{9,8},{10,11... | collective-permute-start | bytes 1179656 | tf_op jit(solution)/shard_map/ppermute | solution.py:347
  16.2 19.3 %collective-permute-start.3 = (f32[2,4,128,128]{3,2,1,0:T(8,128)S(1)}, f32[2,4,128,128]{3,2,1,0:T(8,128)S(1)}, u32[]{:S(2)}, u32[]{:S(2)}) collective-permute-start(f32[2,4,128,128]{3,2,1,0:T(8,128)S(1)} %get-tuple-element.38), channel_id=1, source_target_pairs={{0,480},{32,0},{64,32},{96,64},{128,96},{160,128},{192,160},{224,1... | collective-permute-start | bytes 1572872 | tf_op jit(solution)/shard_map/ppermute | solution.py:375
  23.2 22.1 %collective-permute-start.2 = (f32[2,4,128,128]{3,2,1,0:T(8,128)S(1)}, f32[2,4,128,128]{3,2,1,0:T(8,128)S(1)}, u32[]{:S(2)}, u32[]{:S(2)}) collective-permute-start(f32[2,4,128,128]{3,2,1,0:T(8,128)S(1)} %get-tuple-element.37), channel_id=1, source_target_pairs={{0,480},{32,0},{64,32},{96,64},{128,96},{160,128},{192,160},{224,1... | collective-permute-start | bytes 1572872 | tf_op jit(solution)/shard_map/ppermute | solution.py:376
  36.0 10.2 %collective-permute-start.4 = (f32[2,128,128]{2,1,0:T(8,128)S(1)}, f32[2,128,128]{2,1,0:T(8,128)S(1)}, u32[]{:S(2)}, u32[]{:S(2)}) collective-permute-start(f32[2,128,128]{2,1,0:T(8,128)S(1)} %get-tuple-element.41), channel_id=1, source_target_pairs={{1,2},{2,1},{3,4},{4,3},{5,6},{6,5},{7,8},{8,7},{9,10},{10,9},{11,... | collective-permute-start | bytes 393224 | tf_op jit(solution)/shard_map/ppermute | solution.py:346
  37.9 8.3 %collective-permute-start.5 = (f32[2,128,128]{2,1,0:T(8,128)S(1)}, f32[2,128,128]{2,1,0:T(8,128)S(1)}, u32[]{:S(2)}, u32[]{:S(2)}) collective-permute-start(f32[2,128,128]{2,1,0:T(8,128)S(1)} %get-tuple-element.42), channel_id=1, source_target_pairs={{0,1},{1,0},{2,3},{3,2},{4,5},{5,4},{6,7},{7,6},{8,9},{9,8},{10,11... | collective-permute-start | bytes 393224 | tf_op jit(solution)/shard_map/ppermute | solution.py:347
  46.7 7.5 %collective-permute-start.6 = (f32[2,128,128]{2,1,0:T(8,128)S(1)}, f32[2,128,128]{2,1,0:T(8,128)S(1)}, u32[]{:S(2)}, u32[]{:S(2)}) collective-permute-start(f32[2,128,128]{2,1,0:T(8,128)S(1)} %get-tuple-element.45), channel_id=1, source_target_pairs={{1,2},{2,1},{3,4},{4,3},{5,6},{6,5},{7,8},{8,7},{9,10},{10,9},{11,... | collective-permute-start | bytes 393224 | tf_op jit(solution)/shard_map/ppermute | solution.py:346
  49.0 6.2 %collective-permute-start.7 = (f32[2,128,128]{2,1,0:T(8,128)S(1)}, f32[2,128,128]{2,1,0:T(8,128)S(1)}, u32[]{:S(2)}, u32[]{:S(2)}) collective-permute-start(f32[2,128,128]{2,1,0:T(8,128)S(1)} %get-tuple-element.46), channel_id=1, source_target_pairs={{0,1},{1,0},{2,3},{3,2},{4,5},{5,4},{6,7},{7,6},{8,9},{9,8},{10,11... | collective-permute-start | bytes 393224 | tf_op jit(solution)/shard_map/ppermute | solution.py:347
  91.8 7.6 %collective-permute-start.8 = (f32[2,9,8,128]{3,2,1,0:T(8,128)S(1)}, f32[2,9,8,128]{3,2,1,0:T(8,128)S(1)}, u32[]{:S(2)}, u32[]{:S(2)}) collective-permute-start(f32[2,9,8,128]{3,2,1,0:T(8,128)S(1)} %get-tuple-element.49), channel_id=1, source_target_pairs={{1,2},{2,1},{3,4},{4,3},{5,6},{6,5},{7,8},{8,7},{9,10},{10,9},{11,... | collective-permute-start | bytes 221192 | tf_op jit(solution)/shard_map/ppermute | solution.py:346
  93.7 6.6 %collective-permute-start.9 = (f32[2,9,8,128]{3,2,1,0:T(8,128)S(1)}, f32[2,9,8,128]{3,2,1,0:T(8,128)S(1)}, u32[]{:S(2)}, u32[]{:S(2)}) collective-permute-start(f32[2,9,8,128]{3,2,1,0:T(8,128)S(1)} %get-tuple-element.50), channel_id=1, source_target_pairs={{0,1},{1,0},{2,3},{3,2},{4,5},{5,4},{6,7},{7,6},{8,9},{9,8},{10,11... | collective-permute-start | bytes 221192 | tf_op jit(solution)/shard_map/ppermute | solution.py:347
  100.6 5.8 %collective-permute-start.10 = (f32[2,4,8,128]{3,2,1,0:T(8,128)S(1)}, f32[2,4,8,128]{3,2,1,0:T(8,128)S(1)}, u32[]{:S(2)}, u32[]{:S(2)}) collective-permute-start(f32[2,4,8,128]{3,2,1,0:T(8,128)S(1)} %get-tuple-element.52.refs_0_), channel_id=1, source_target_pairs={{0,32},{64,0},{128,64},{192,128},{256,192},{320,256},{384,320},{44... | collective-permute-start | bytes 98312 | tf_op jit(solution)/shard_map/ppermute | solution.py:401
  106.5 6.9 %collective-permute-start.11 = (f32[2,16,8,128]{3,2,1,0:T(8,128)S(1)}, f32[2,16,8,128]{3,2,1,0:T(8,128)S(1)}, u32[]{:S(2)}, u32[]{:S(2)}) collective-permute-start(f32[2,16,8,128]{3,2,1,0:T(8,128)S(1)} %get-tuple-element.53), channel_id=1, source_target_pairs={{1,2},{2,1},{3,4},{4,3},{5,6},{6,5},{7,8},{8,7},{9,10},{10,9},{11,... | collective-permute-start | bytes 393224 | tf_op jit(solution)/shard_map/ppermute | solution.py:346
  108.4 5.9 %collective-permute-start.12 = (f32[2,16,8,128]{3,2,1,0:T(8,128)S(1)}, f32[2,16,8,128]{3,2,1,0:T(8,128)S(1)}, u32[]{:S(2)}, u32[]{:S(2)}) collective-permute-start(f32[2,16,8,128]{3,2,1,0:T(8,128)S(1)} %get-tuple-element.54), channel_id=1, source_target_pairs={{0,1},{1,0},{2,3},{3,2},{4,5},{5,4},{6,7},{7,6},{8,9},{9,8},{10,11... | collective-permute-start | bytes 393224 | tf_op jit(solution)/shard_map/ppermute | solution.py:347
  114.8 7.3 %collective-permute-start.13 = (f32[2,4,8,128]{3,2,1,0:T(8,128)S(1)}, f32[2,4,8,128]{3,2,1,0:T(8,128)S(1)}, u32[]{:S(2)}, u32[]{:S(2)}) collective-permute-start(f32[2,4,8,128]{3,2,1,0:T(8,128)S(1)} %get-tuple-element.56.refs_0_), channel_id=1, source_target_pairs={{0,64},{64,128},{128,192},{192,256},{256,320},{320,384},{384,448},... | collective-permute-start | bytes 98312 | tf_op jit(solution)/shard_map/ppermute | solution.py:401
  122.1 7.4 %collective-permute-start.14 = (f32[2,16,8,128]{3,2,1,0:T(8,128)S(1)}, f32[2,16,8,128]{3,2,1,0:T(8,128)S(1)}, u32[]{:S(2)}, u32[]{:S(2)}) collective-permute-start(f32[2,16,8,128]{3,2,1,0:T(8,128)S(1)} %get-tuple-element.57), channel_id=1, source_target_pairs={{1,2},{2,1},{3,4},{4,3},{5,6},{6,5},{7,8},{8,7},{9,10},{10,9},{11,... | collective-permute-start | bytes 393224 | tf_op jit(solution)/shard_map/ppermute | solution.py:346
  124.1 6.5 %collective-permute-start.15 = (f32[2,16,8,128]{3,2,1,0:T(8,128)S(1)}, f32[2,16,8,128]{3,2,1,0:T(8,128)S(1)}, u32[]{:S(2)}, u32[]{:S(2)}) collective-permute-start(f32[2,16,8,128]{3,2,1,0:T(8,128)S(1)} %get-tuple-element.58), channel_id=1, source_target_pairs={{0,1},{1,0},{2,3},{3,2},{4,5},{5,4},{6,7},{7,6},{8,9},{9,8},{10,11... | collective-permute-start | bytes 393224 | tf_op jit(solution)/shard_map/ppermute | solution.py:347
  131.0 5.8 %collective-permute-start.16 = (f32[2,4,8,128]{3,2,1,0:T(8,128)S(1)}, f32[2,4,8,128]{3,2,1,0:T(8,128)S(1)}, u32[]{:S(2)}, u32[]{:S(2)}) collective-permute-start(f32[2,4,8,128]{3,2,1,0:T(8,128)S(1)} %get-tuple-element.60.refs_0_), channel_id=1, source_target_pairs={{0,32},{64,0},{128,64},{192,128},{256,192},{320,256},{384,320},{44... | collective-permute-start | bytes 98312 | tf_op jit(solution)/shard_map/ppermute | solution.py:401
  136.8 7.5 %collective-permute-start.17 = (f32[2,16,8,128]{3,2,1,0:T(8,128)S(1)}, f32[2,16,8,128]{3,2,1,0:T(8,128)S(1)}, u32[]{:S(2)}, u32[]{:S(2)}) collective-permute-start(f32[2,16,8,128]{3,2,1,0:T(8,128)S(1)} %get-tuple-element.61), channel_id=1, source_target_pairs={{1,2},{2,1},{3,4},{4,3},{5,6},{6,5},{7,8},{8,7},{9,10},{10,9},{11,... | collective-permute-start | bytes 393224 | tf_op jit(solution)/shard_map/ppermute | solution.py:346
  138.8 6.6 %collective-permute-start.18 = (f32[2,16,8,128]{3,2,1,0:T(8,128)S(1)}, f32[2,16,8,128]{3,2,1,0:T(8,128)S(1)}, u32[]{:S(2)}, u32[]{:S(2)}) collective-permute-start(f32[2,16,8,128]{3,2,1,0:T(8,128)S(1)} %get-tuple-element.62), channel_id=1, source_target_pairs={{0,1},{1,0},{2,3},{3,2},{4,5},{5,4},{6,7},{7,6},{8,9},{9,8},{10,11... | collective-permute-start | bytes 393224 | tf_op jit(solution)/shard_map/ppermute | solution.py:347

commit v4 on v3

--- a/solution.py
+++ b/solution.py
@@ -217,47 +217,51 @@
     return jnp.concatenate([come, own] if kind == 0 else [own, come], axis=-2)
 
 
+def unpacked(ref, lead, at, first):
+    kept = 2 * rows_each
+    start = min(max(at - first, 0), ref.shape[-2] - kept)
+    rows = ref[(*lead, slice(start, start + kept))]
+    shift = (start + first - at) % kept
+    return pltpu.roll(rows, shift, 0) if shift else rows
+
+
 def rows_of(kind, state, offsets_ref):
-    kept = 2 * rows_each
-
-    def unpacked(ref, *at):
-        p = at[-1]
-        total = ref.shape[-2]
-        start = min(max(rows_sent * p - 1, 0), total - kept)
-        rows = ref[(*at[:-1], slice(start, start + kept))]
-        shift = (start + 1 - rows_sent * p) % kept
-        return pltpu.roll(rows, shift, 0) if shift else rows
-
     def plane(a, f, p):
         if a:
-            return unpacked(offsets_ref, a - 1, f, p)
+            return unpacked(offsets_ref, (a - 1, f), rows_sent * p, 1)
         if len(state) == 1:
-            return unpacked(state[0], f, p)
+            return unpacked(state[0], (f,), rows_sent * p, 1)
         return joined(kind, state[0][f, p], state[1][f, p])
 
     return plane
 
 
-def tiles_in(steps):
-    return sum(2 * n - 1 for _, n in edge_lists(steps))
+def edge_pieces(steps):
+    pieces, at = [], 0
+    for a, n in edge_lists(steps):
+        for away in range(1, n + 1):
+            around = half_rows if a == 0 and away == 1 else n - away
+            first, end = half_rows - around, half_rows + rows_each + around
+            pieces.append((a, away, at, first, end))
+            at += end - first
+    return pieces, -(-at // rows_each) * rows_each
 
 
 def edge_kernel(kind, steps, flags_ref, offsets_ref, *refs):
     far_ref, near_ref = refs[-2:]
     depth = offsets_ref.shape[2] // rows_sent
     plane = rows_of(kind, refs[:-2], offsets_ref)
-    at = 0
-    for a, n in edge_lists(steps):
-        for away in range(1, n + 1):
-            for f in range(2):
-                ends = plane(a, f, away - 1), plane(a, f, depth - away)
-                if away == n:
-                    ends = [pltpu.roll(x, 2 * rows_each - half_rows, 0)[:rows_each] for x in ends]
-                    put_edges(flags_ref, far_ref, near_ref, (f, at), *ends)
-                else:
-                    put_edges(flags_ref, far_ref, near_ref, (f, at), *[x[:rows_each] for x in ends])
-                    put_edges(flags_ref, far_ref, near_ref, (f, at + 1), *[x[rows_each:] for x in ends])
-            at += 1 if away == n else 2
+    pieces, total = edge_pieces(steps)
+    used = 0
+    for a, away, at, first, end in pieces:
+        used = at + end - first
+        for f in range(2):
+            ends = plane(a, f, away - 1), plane(a, f, depth - away)
+            put_edges(flags_ref, far_ref, near_ref, (f, slice(at, used)), *[x[first:end] for x in ends])
+    if used < total:
+        for f in range(2):
+            for ref in (far_ref, near_ref):
+                ref[f, used:total] = jnp.zeros((total - used, ref.shape[-1]), jnp.float32)
 
 
 def block_kernel(kind, steps, flags_ref, offsets_ref, *refs):
@@ -267,28 +271,19 @@
     state = refs[: -3 if closing else -4]
     opening = len(state) == 1
     plane = rows_of(kind, state, offsets_ref)
-    at = {}
-    place = 0
-    for a, n in edge_lists(steps):
-        at[a] = (place, n)
-        place += 2 * n - 1
-
-    def halo(a, f, away, side):
-        place, n = at[a]
-        first = place + 2 * (away - 1)
-        tiles = [side(flags_ref, far_ref[f, t], near_ref[f, t]) for t in range(first, first + 1 + (away < n))]
-        if away < n:
-            return jnp.concatenate(tiles, axis=0)
-        return pltpu.roll(jnp.concatenate(tiles * 2, axis=0), half_rows, 0)
+    halos = {}
+    for a, away, at, first, _ in edge_pieces(steps)[0]:
+        halos.setdefault(a, []).append((at, first))
+
+    def halo(f, piece, side):
+        return side(flags_ref, *[unpacked(ref, (f,), *piece) for ref in (far_ref, near_ref)])
 
     def extended(a, f):
         planes = [plane(a, f, p) for p in range(depth)]
-        if a in at:
-            aways = range(1, at[a][1] + 1)
-            lo = [halo(a, f, away, below) for away in reversed(aways)]
-            hi = [halo(a, f, away, above) for away in aways]
-            planes = lo + planes + hi
-        return jnp.stack(planes)
+        pieces = halos.get(a, [])
+        lo = [halo(f, piece, below) for piece in reversed(pieces)]
+        hi = [halo(f, piece, above) for piece in pieces]
+        return jnp.stack(lo + planes + hi)
 
     state = [extended(0, f) for f in range(2)]
     for f in range(2):
@@ -400,7 +395,7 @@
             route = [(index_of(r, count), index_of((r + way) % count, count)) for r in range(count)]
             state = [end[0], lax.ppermute(end[0], "tm", route)]
         offsets = held[first - 1 : first - 1 + steps]
-        message = shape(2, tiles_in(steps), rows_each, cols)
+        message = shape(2, edge_pieces(steps)[1], cols)
         far, near = call(functools.partial(edge_kernel, kind, steps), [message] * 2, flags, offsets, *state)
         far, near = swapped(far, near)
         closing = first + steps == count

time: 177 us -> 176 us (level)
  no operation moved by 1% of the time
where the time goes in v4:
time: 176 us; the launch traced here: 175 us
  starting transfers between devices  65.6 us (37%)
  blocking collectives  64.7 us (37%)
  waiting for transfers between devices  35.7 us (20%)
  Pallas kernels  6.3 us (4%)
  local copies, waits for them, and re-layouts  2.61 us (1%)
    all_to_all x1, blocking collectives, local(): held = lax.all_to_all(send, 'tm', 0, 0, tiled=True)  35.9 us
    ppermute x7, starting transfers between devices, swapped(): lax.ppermute(near, 'space', [(i + j, i + 1 - j) for i in range(0, count,...  35.5 us
    all_to_all x1, blocking collectives, local(): back = lax.all_to_all(jnp.concatenate(ends), 'tm', 0, 0, tiled=True)  28.8 us
    ppermute x7, starting transfers between devices, swapped(): lax.ppermute(far, 'space', [((i + j) % count, (i + 1 - j) % count) for i...  13.8 us
    ppermute x3, waiting for transfers between devices, local(): state = [end[0], lax.ppermute(end[0], 'tm', route)]  12.9 us
    ppermute x1, waiting for transfers between devices, local(): old_first = lax.ppermute(old_first, 'tm', back_one)  9 us
    ppermute x1, starting transfers between devices, local(): old_first = lax.ppermute(old_first, 'tm', back_one)  6.94 us
    pallas_call x15, Pallas kernels, call(): pl.pallas_call(kernel, out_shape=tuple(out_shapes), in_specs=[pl.BlockSpe...  6.3 us
  transfers between devices with their start and end apart: 19, of which 12 were waited for; matrix products, arithmetic and copies ran while one was open for 0% of the time, Pallas kernels for 1%

profile of v4, /device:TPU:194, one launch (start us, length us, event | category | flops | bytes accessed | tf_op | source)
XLA Modules:
  0.0 175.3 jit_solution(1421792776405964637)
XLA Ops:
  2.8 1.9 %collective-permute-start = (f32[3,2,128,128]{3,2,1,0:T(8,128)S(1)}, f32[3,2,128,128]{3,2,1,0:T(8,128)S(1)}, u32[]{:S(2)}, u32[]{:S(2)}) collective-permute-start(f32[3,2,128,128]{3,2,1,0:T(8,128)S(1)} %get-tuple-element.35), channel_id=1, source_target_pairs={{1,2},{2,1},{3,4},{4,3},{5,6},{6,5},{7,8},{8,7},{9,10},{10,9},{11,... | collective-permute-start | bytes 1179656 | tf_op jit(solution)/shard_map/ppermute | solution.py:341
  4.8 5.6 %collective-permute-start.1 = (f32[3,2,128,128]{3,2,1,0:T(8,128)S(1)}, f32[3,2,128,128]{3,2,1,0:T(8,128)S(1)}, u32[]{:S(2)}, u32[]{:S(2)}) collective-permute-start(f32[3,2,128,128]{3,2,1,0:T(8,128)S(1)} %get-tuple-element.36), channel_id=1, source_target_pairs={{0,1},{1,0},{2,3},{3,2},{4,5},{5,4},{6,7},{7,6},{8,9},{9,8},{10,11... | collective-permute-start | bytes 1179656 | tf_op jit(solution)/shard_map/ppermute | solution.py:342
  11.6 4.5 %collective-permute-done.far_ref = f32[3,2,128,128]{3,2,1,0:T(8,128)S(1)} collective-permute-done((f32[3,2,128,128]{3,2,1,0:T(8,128)S(1)}, f32[3,2,128,128]{3,2,1,0:T(8,128)S(1)}, u32[]{:S(2)}, u32[]{:S(2)}) %collective-permute-start) | collective-permute-done | bytes 393248 | tf_op jit(solution)/shard_map/ppermute | solution.py:341
  16.2 6.9 %collective-permute-start.3 = (f32[2,4,128,128]{3,2,1,0:T(8,128)S(1)}, f32[2,4,128,128]{3,2,1,0:T(8,128)S(1)}, u32[]{:S(2)}, u32[]{:S(2)}) collective-permute-start(f32[2,4,128,128]{3,2,1,0:T(8,128)S(1)} %get-tuple-element.38), channel_id=1, source_target_pairs={{0,480},{32,0},{64,32},{96,64},{128,96},{160,128},{192,160},{224,1... | collective-permute-start | bytes 1572872 | tf_op jit(solution)/shard_map/ppermute | solution.py:370
  23.2 3.3 %collective-permute-start.2 = (f32[2,4,128,128]{3,2,1,0:T(8,128)S(1)}, f32[2,4,128,128]{3,2,1,0:T(8,128)S(1)}, u32[]{:S(2)}, u32[]{:S(2)}) collective-permute-start(f32[2,4,128,128]{3,2,1,0:T(8,128)S(1)} %get-tuple-element.37), channel_id=1, source_target_pairs={{0,480},{32,0},{64,32},{96,64},{128,96},{160,128},{192,160},{224,1... | collective-permute-start | bytes 1572872 | tf_op jit(solution)/shard_map/ppermute | solution.py:371
  26.5 9.0 %collective-permute-done.3.old_ref = f32[2,4,128,128]{3,2,1,0:T(8,128)S(1)} collective-permute-done((f32[2,4,128,128]{3,2,1,0:T(8,128)S(1)}, f32[2,4,128,128]{3,2,1,0:T(8,128)S(1)}, u32[]{:S(2)}, u32[]{:S(2)}) %collective-permute-start.3) | collective-permute-done | bytes 524320 | tf_op jit(solution)/shard_map/ppermute | solution.py:370
  36.0 1.9 %collective-permute-start.4 = (f32[2,128,128]{2,1,0:T(8,128)S(1)}, f32[2,128,128]{2,1,0:T(8,128)S(1)}, u32[]{:S(2)}, u32[]{:S(2)}) collective-permute-start(f32[2,128,128]{2,1,0:T(8,128)S(1)} %get-tuple-element.41), channel_id=1, source_target_pairs={{1,2},{2,1},{3,4},{4,3},{5,6},{6,5},{7,8},{8,7},{9,10},{10,9},{11,... | collective-permute-start | bytes 393224 | tf_op jit(solution)/shard_map/ppermute | solution.py:341
  37.9 3.6 %collective-permute-start.5 = (f32[2,128,128]{2,1,0:T(8,128)S(1)}, f32[2,128,128]{2,1,0:T(8,128)S(1)}, u32[]{:S(2)}, u32[]{:S(2)}) collective-permute-start(f32[2,128,128]{2,1,0:T(8,128)S(1)} %get-tuple-element.42), channel_id=1, source_target_pairs={{0,1},{1,0},{2,3},{3,2},{4,5},{5,4},{6,7},{7,6},{8,9},{9,8},{10,11... | collective-permute-start | bytes 393224 | tf_op jit(solution)/shard_map/ppermute | solution.py:342
  41.5 3.8 %collective-permute-done.2.old_ref = f32[2,4,128,128]{3,2,1,0:T(8,128)S(1)} collective-permute-done((f32[2,4,128,128]{3,2,1,0:T(8,128)S(1)}, f32[2,4,128,128]{3,2,1,0:T(8,128)S(1)}, u32[]{:S(2)}, u32[]{:S(2)}) %collective-permute-start.2) | collective-permute-done | bytes 524320 | tf_op jit(solution)/shard_map/ppermute | solution.py:371
  46.7 2.3 %collective-permute-start.6 = (f32[2,128,128]{2,1,0:T(8,128)S(1)}, f32[2,128,128]{2,1,0:T(8,128)S(1)}, u32[]{:S(2)}, u32[]{:S(2)}) collective-permute-start(f32[2,128,128]{2,1,0:T(8,128)S(1)} %get-tuple-element.45), channel_id=1, source_target_pairs={{1,2},{2,1},{3,4},{4,3},{5,6},{6,5},{7,8},{8,7},{9,10},{10,9},{11,... | collective-permute-start | bytes 393224 | tf_op jit(solution)/shard_map/ppermute | solution.py:341
  49.0 5.2 %collective-permute-start.7 = (f32[2,128,128]{2,1,0:T(8,128)S(1)}, f32[2,128,128]{2,1,0:T(8,128)S(1)}, u32[]{:S(2)}, u32[]{:S(2)}) collective-permute-start(f32[2,128,128]{2,1,0:T(8,128)S(1)} %get-tuple-element.46), channel_id=1, source_target_pairs={{0,1},{1,0},{2,3},{3,2},{4,5},{5,4},{6,7},{7,6},{8,9},{9,8},{10,11... | collective-permute-start | bytes 393224 | tf_op jit(solution)/shard_map/ppermute | solution.py:342
  55.8 35.9 %all_to_all.10 = f32[16,2,56,128]{3,2,1,0:T(8,128)S(1)} all-to-all(f32[16,2,56,128]{3,2,1,0:T(8,128)S(1)} %get-tuple-element.48), channel_id=1, replica_groups=mesh['tm'=16,'space'=32] {'tm'}, dimensions={0} | all-to-all | bytes 1835008 | tf_op jit(solution)/shard_map/all_to_all | solution.py:388
  91.8 1.9 %collective-permute-start.8 = (f32[2,64,128]{2,1,0:T(8,128)S(1)}, f32[2,64,128]{2,1,0:T(8,128)S(1)}, u32[]{:S(2)}, u32[]{:S(2)}) collective-permute-start(f32[2,64,128]{2,1,0:T(8,128)S(1)} %get-tuple-element.49), channel_id=1, source_target_pairs={{1,2},{2,1},{3,4},{4,3},{5,6},{6,5},{7,8},{8,7},{9,10},{10,9},{11,... | collective-permute-start | bytes 196616 | tf_op jit(solution)/shard_map/ppermute | solution.py:341
  93.7 5.7 %collective-permute-start.9 = (f32[2,64,128]{2,1,0:T(8,128)S(1)}, f32[2,64,128]{2,1,0:T(8,128)S(1)}, u32[]{:S(2)}, u32[]{:S(2)}) collective-permute-start(f32[2,64,128]{2,1,0:T(8,128)S(1)} %get-tuple-element.50), channel_id=1, source_target_pairs={{0,1},{1,0},{2,3},{3,2},{4,5},{5,4},{6,7},{7,6},{8,9},{9,8},{10,11... | collective-permute-start | bytes 196616 | tf_op jit(solution)/shard_map/ppermute | solution.py:342
  100.6 1.9 %collective-permute-start.10 = (f32[2,4,8,128]{3,2,1,0:T(8,128)S(1)}, f32[2,4,8,128]{3,2,1,0:T(8,128)S(1)}, u32[]{:S(2)}, u32[]{:S(2)}) collective-permute-start(f32[2,4,8,128]{3,2,1,0:T(8,128)S(1)} %get-tuple-element.52.refs_0_), channel_id=1, source_target_pairs={{0,32},{64,0},{128,64},{192,128},{256,192},{320,256},{384,320},{44... | collective-permute-start | bytes 98312 | tf_op jit(solution)/shard_map/ppermute | solution.py:396
  102.6 3.8 %collective-permute-done.10.refs_1_ = f32[2,4,8,128]{3,2,1,0:T(8,128)S(1)} collective-permute-done((f32[2,4,8,128]{3,2,1,0:T(8,128)S(1)}, f32[2,4,8,128]{3,2,1,0:T(8,128)S(1)}, u32[]{:S(2)}, u32[]{:S(2)}) %collective-permute-start.10) | collective-permute-done | bytes 32800 | tf_op jit(solution)/shard_map/ppermute | solution.py:396
  106.4 1.9 %collective-permute-start.11 = (f32[2,104,128]{2,1,0:T(8,128)S(1)}, f32[2,104,128]{2,1,0:T(8,128)S(1)}, u32[]{:S(2)}, u32[]{:S(2)}) collective-permute-start(f32[2,104,128]{2,1,0:T(8,128)S(1)} %get-tuple-element.53), channel_id=1, source_target_pairs={{1,2},{2,1},{3,4},{4,3},{5,6},{6,5},{7,8},{8,7},{9,10},{10,9},{11,... | collective-permute-start | bytes 319496 | tf_op jit(solution)/shard_map/ppermute | solution.py:341
  108.4 4.9 %collective-permute-start.12 = (f32[2,104,128]{2,1,0:T(8,128)S(1)}, f32[2,104,128]{2,1,0:T(8,128)S(1)}, u32[]{:S(2)}, u32[]{:S(2)}) collective-permute-start(f32[2,104,128]{2,1,0:T(8,128)S(1)} %get-tuple-element.54), channel_id=1, source_target_pairs={{0,1},{1,0},{2,3},{3,2},{4,5},{5,4},{6,7},{7,6},{8,9},{9,8},{10,11... | collective-permute-start | bytes 319496 | tf_op jit(solution)/shard_map/ppermute | solution.py:342
  114.7 2.2 %collective-permute-start.13 = (f32[2,4,8,128]{3,2,1,0:T(8,128)S(1)}, f32[2,4,8,128]{3,2,1,0:T(8,128)S(1)}, u32[]{:S(2)}, u32[]{:S(2)}) collective-permute-start(f32[2,4,8,128]{3,2,1,0:T(8,128)S(1)} %get-tuple-element.56.refs_0_), channel_id=1, source_target_pairs={{0,64},{64,128},{128,192},{192,256},{256,320},{320,384},{384,448},... | collective-permute-start | bytes 98312 | tf_op jit(solution)/shard_map/ppermute | solution.py:396
  116.8 5.2 %collective-permute-done.13.refs_1_ = f32[2,4,8,128]{3,2,1,0:T(8,128)S(1)} collective-permute-done((f32[2,4,8,128]{3,2,1,0:T(8,128)S(1)}, f32[2,4,8,128]{3,2,1,0:T(8,128)S(1)}, u32[]{:S(2)}, u32[]{:S(2)}) %collective-permute-start.13) | collective-permute-done | bytes 32800 | tf_op jit(solution)/shard_map/ppermute | solution.py:396
  123.9 5.3 %collective-permute-start.15 = (f32[2,104,128]{2,1,0:T(8,128)S(1)}, f32[2,104,128]{2,1,0:T(8,128)S(1)}, u32[]{:S(2)}, u32[]{:S(2)}) collective-permute-start(f32[2,104,128]{2,1,0:T(8,128)S(1)} %get-tuple-element.58), channel_id=1, source_target_pairs={{0,1},{1,0},{2,3},{3,2},{4,5},{5,4},{6,7},{7,6},{8,9},{9,8},{10,11... | collective-permute-start | bytes 319496 | tf_op jit(solution)/shard_map/ppermute | solution.py:342
  132.5 3.9 %collective-permute-done.16.refs_1_ = f32[2,4,8,128]{3,2,1,0:T(8,128)S(1)} collective-permute-done((f32[2,4,8,128]{3,2,1,0:T(8,128)S(1)}, f32[2,4,8,128]{3,2,1,0:T(8,128)S(1)}, u32[]{:S(2)}, u32[]{:S(2)}) %collective-permute-start.16) | collective-permute-done | bytes 32800 | tf_op jit(solution)/shard_map/ppermute | solution.py:396
  138.4 5.4 %collective-permute-start.18 = (f32[2,104,128]{2,1,0:T(8,128)S(1)}, f32[2,104,128]{2,1,0:T(8,128)S(1)}, u32[]{:S(2)}, u32[]{:S(2)}) collective-permute-start(f32[2,104,128]{2,1,0:T(8,128)S(1)} %get-tuple-element.62), channel_id=1, source_target_pairs={{0,1},{1,0},{2,3},{3,2},{4,5},{5,4},{6,7},{7,6},{8,9},{9,8},{10,11... | collective-permute-start | bytes 319496 | tf_op jit(solution)/shard_map/ppermute | solution.py:342
  145.2 28.8 %all_to_all.11.come_ref = f32[16,2,6,8,128]{4,3,2,1,0:T(8,128)S(1)} all-to-all(f32[16,2,6,8,128]{4,3,2,1,0:T(8,128)S(1)} %pad_maximum_fusion), channel_id=1, replica_groups=mesh['tm'=16,'space'=32] {'tm'}, dimensions={0} | all-to-all | bytes 1572864 | tf_op jit(solution)/shard_map/all_to_all | solution.py:409
  (43 shorter events, 20.3 us)
Async XLA Ops:
  0.2 1.4 copy-start
  1.6 1.0 copy-start.1
  2.8 13.3 %collective-permute-start = (f32[3,2,128,128]{3,2,1,0:T(8,128)S(1)}, f32[3,2,128,128]{3,2,1,0:T(8,128)S(1)}, u32[]{:S(2)}, u32[]{:S(2)}) collective-permute-start(f32[3,2,128,128]{3,2,1,0:T(8,128)S(1)} %get-tuple-element.35), channel_id=1, source_target_pairs={{1,2},{2,1},{3,4},{4,3},{5,6},{6,5},{7,8},{8,7},{9,10},{10,9},{11,... | collective-permute-start | bytes 1179656 | tf_op jit(solution)/shard_map/ppermute | solution.py:341
  4.8 11.4 %collective-permute-start.1 = (f32[3,2,128,128]{3,2,1,0:T(8,128)S(1)}, f32[3,2,128,128]{3,2,1,0:T(8,128)S(1)}, u32[]{:S(2)}, u32[]{:S(2)}) collective-permute-start(f32[3,2,128,128]{3,2,1,0:T(8,128)S(1)} %get-tuple-element.36), channel_id=1, source_target_pairs={{0,1},{1,0},{2,3},{3,2},{4,5},{5,4},{6,7},{7,6},{8,9},{9,8},{10,11... | collective-permute-start | bytes 1179656 | tf_op jit(solution)/shard_map/ppermute | solution.py:342
  16.2 19.3 %collective-permute-start.3 = (f32[2,4,128,128]{3,2,1,0:T(8,128)S(1)}, f32[2,4,128,128]{3,2,1,0:T(8,128)S(1)}, u32[]{:S(2)}, u32[]{:S(2)}) collective-permute-start(f32[2,4,128,128]{3,2,1,0:T(8,128)S(1)} %get-tuple-element.38), channel_id=1, source_target_pairs={{0,480},{32,0},{64,32},{96,64},{128,96},{160,128},{192,160},{224,1... | collective-permute-start | bytes 1572872 | tf_op jit(solution)/shard_map/ppermute | solution.py:370
  23.2 22.1 %collective-permute-start.2 = (f32[2,4,128,128]{3,2,1,0:T(8,128)S(1)}, f32[2,4,128,128]{3,2,1,0:T(8,128)S(1)}, u32[]{:S(2)}, u32[]{:S(2)}) collective-permute-start(f32[2,4,128,128]{3,2,1,0:T(8,128)S(1)} %get-tuple-element.37), channel_id=1, source_target_pairs={{0,480},{32,0},{64,32},{96,64},{128,96},{160,128},{192,160},{224,1... | collective-permute-start | bytes 1572872 | tf_op jit(solution)/shard_map/ppermute | solution.py:371
  36.0 10.2 %collective-permute-start.4 = (f32[2,128,128]{2,1,0:T(8,128)S(1)}, f32[2,128,128]{2,1,0:T(8,128)S(1)}, u32[]{:S(2)}, u32[]{:S(2)}) collective-permute-start(f32[2,128,128]{2,1,0:T(8,128)S(1)} %get-tuple-element.41), channel_id=1, source_target_pairs={{1,2},{2,1},{3,4},{4,3},{5,6},{6,5},{7,8},{8,7},{9,10},{10,9},{11,... | collective-permute-start | bytes 393224 | tf_op jit(solution)/shard_map/ppermute | solution.py:341
  37.9 8.3 %collective-permute-start.5 = (f32[2,128,128]{2,1,0:T(8,128)S(1)}, f32[2,128,128]{2,1,0:T(8,128)S(1)}, u32[]{:S(2)}, u32[]{:S(2)}) collective-permute-start(f32[2,128,128]{2,1,0:T(8,128)S(1)} %get-tuple-element.42), channel_id=1, source_target_pairs={{0,1},{1,0},{2,3},{3,2},{4,5},{5,4},{6,7},{7,6},{8,9},{9,8},{10,11... | collective-permute-start | bytes 393224 | tf_op jit(solution)/shard_map/ppermute | solution.py:342
  46.7 7.5 %collective-permute-start.6 = (f32[2,128,128]{2,1,0:T(8,128)S(1)}, f32[2,128,128]{2,1,0:T(8,128)S(1)}, u32[]{:S(2)}, u32[]{:S(2)}) collective-permute-start(f32[2,128,128]{2,1,0:T(8,128)S(1)} %get-tuple-element.45), channel_id=1, source_target_pairs={{1,2},{2,1},{3,4},{4,3},{5,6},{6,5},{7,8},{8,7},{9,10},{10,9},{11,... | collective-permute-start | bytes 393224 | tf_op jit(solution)/shard_map/ppermute | solution.py:341
  49.0 6.2 %collective-permute-start.7 = (f32[2,128,128]{2,1,0:T(8,128)S(1)}, f32[2,128,128]{2,1,0:T(8,128)S(1)}, u32[]{:S(2)}, u32[]{:S(2)}) collective-permute-start(f32[2,128,128]{2,1,0:T(8,128)S(1)} %get-tuple-element.46), channel_id=1, source_target_pairs={{0,1},{1,0},{2,3},{3,2},{4,5},{5,4},{6,7},{7,6},{8,9},{9,8},{10,11... | collective-permute-start | bytes 393224 | tf_op jit(solution)/shard_map/ppermute | solution.py:342
  91.8 7.6 %collective-permute-start.8 = (f32[2,64,128]{2,1,0:T(8,128)S(1)}, f32[2,64,128]{2,1,0:T(8,128)S(1)}, u32[]{:S(2)}, u32[]{:S(2)}) collective-permute-start(f32[2,64,128]{2,1,0:T(8,128)S(1)} %get-tuple-element.49), channel_id=1, source_target_pairs={{1,2},{2,1},{3,4},{4,3},{5,6},{6,5},{7,8},{8,7},{9,10},{10,9},{11,... | collective-permute-start | bytes 196616 | tf_op jit(solution)/shard_map/ppermute | solution.py:341
  93.7 6.6 %collective-permute-start.9 = (f32[2,64,128]{2,1,0:T(8,128)S(1)}, f32[2,64,128]{2,1,0:T(8,128)S(1)}, u32[]{:S(2)}, u32[]{:S(2)}) collective-permute-start(f32[2,64,128]{2,1,0:T(8,128)S(1)} %get-tuple-element.50), channel_id=1, source_target_pairs={{0,1},{1,0},{2,3},{3,2},{4,5},{5,4},{6,7},{7,6},{8,9},{9,8},{10,11... | collective-permute-start | bytes 196616 | tf_op jit(solution)/shard_map/ppermute | solution.py:342
  100.6 5.8 %collective-permute-start.10 = (f32[2,4,8,128]{3,2,1,0:T(8,128)S(1)}, f32[2,4,8,128]{3,2,1,0:T(8,128)S(1)}, u32[]{:S(2)}, u32[]{:S(2)}) collective-permute-start(f32[2,4,8,128]{3,2,1,0:T(8,128)S(1)} %get-tuple-element.52.refs_0_), channel_id=1, source_target_pairs={{0,32},{64,0},{128,64},{192,128},{256,192},{320,256},{384,320},{44... | collective-permute-start | bytes 98312 | tf_op jit(solution)/shard_map/ppermute | solution.py:396
  106.4 6.8 %collective-permute-start.11 = (f32[2,104,128]{2,1,0:T(8,128)S(1)}, f32[2,104,128]{2,1,0:T(8,128)S(1)}, u32[]{:S(2)}, u32[]{:S(2)}) collective-permute-start(f32[2,104,128]{2,1,0:T(8,128)S(1)} %get-tuple-element.53), channel_id=1, source_target_pairs={{1,2},{2,1},{3,4},{4,3},{5,6},{6,5},{7,8},{8,7},{9,10},{10,9},{11,... | collective-permute-start | bytes 319496 | tf_op jit(solution)/shard_map/ppermute | solution.py:341
  108.4 5.8 %collective-permute-start.12 = (f32[2,104,128]{2,1,0:T(8,128)S(1)}, f32[2,104,128]{2,1,0:T(8,128)S(1)}, u32[]{:S(2)}, u32[]{:S(2)}) collective-permute-start(f32[2,104,128]{2,1,0:T(8,128)S(1)} %get-tuple-element.54), channel_id=1, source_target_pairs={{0,1},{1,0},{2,3},{3,2},{4,5},{5,4},{6,7},{7,6},{8,9},{9,8},{10,11... | collective-permute-start | bytes 319496 | tf_op jit(solution)/shard_map/ppermute | solution.py:342
  114.7 7.3 %collective-permute-start.13 = (f32[2,4,8,128]{3,2,1,0:T(8,128)S(1)}, f32[2,4,8,128]{3,2,1,0:T(8,128)S(1)}, u32[]{:S(2)}, u32[]{:S(2)}) collective-permute-start(f32[2,4,8,128]{3,2,1,0:T(8,128)S(1)} %get-tuple-element.56.refs_0_), channel_id=1, source_target_pairs={{0,64},{64,128},{128,192},{192,256},{256,320},{320,384},{384,448},... | collective-permute-start | bytes 98312 | tf_op jit(solution)/shard_map/ppermute | solution.py:396
  122.0 7.2 %collective-permute-start.14 = (f32[2,104,128]{2,1,0:T(8,128)S(1)}, f32[2,104,128]{2,1,0:T(8,128)S(1)}, u32[]{:S(2)}, u32[]{:S(2)}) collective-permute-start(f32[2,104,128]{2,1,0:T(8,128)S(1)} %get-tuple-element.57), channel_id=1, source_target_pairs={{1,2},{2,1},{3,4},{4,3},{5,6},{6,5},{7,8},{8,7},{9,10},{10,9},{11,... | collective-permute-start | bytes 319496 | tf_op jit(solution)/shard_map/ppermute | solution.py:341
  123.9 6.2 %collective-permute-start.15 = (f32[2,104,128]{2,1,0:T(8,128)S(1)}, f32[2,104,128]{2,1,0:T(8,128)S(1)}, u32[]{:S(2)}, u32[]{:S(2)}) collective-permute-start(f32[2,104,128]{2,1,0:T(8,128)S(1)} %get-tuple-element.58), channel_id=1, source_target_pairs={{0,1},{1,0},{2,3},{3,2},{4,5},{5,4},{6,7},{7,6},{8,9},{9,8},{10,11... | collective-permute-start | bytes 319496 | tf_op jit(solution)/shard_map/ppermute | solution.py:342
  130.6 5.8 %collective-permute-start.16 = (f32[2,4,8,128]{3,2,1,0:T(8,128)S(1)}, f32[2,4,8,128]{3,2,1,0:T(8,128)S(1)}, u32[]{:S(2)}, u32[]{:S(2)}) collective-permute-start(f32[2,4,8,128]{3,2,1,0:T(8,128)S(1)} %get-tuple-element.60.refs_0_), channel_id=1, source_target_pairs={{0,32},{64,0},{128,64},{192,128},{256,192},{320,256},{384,320},{44... | collective-permute-start | bytes 98312 | tf_op jit(solution)/shard_map/ppermute | solution.py:396
  136.4 7.3 %collective-permute-start.17 = (f32[2,104,128]{2,1,0:T(8,128)S(1)}, f32[2,104,128]{2,1,0:T(8,128)S(1)}, u32[]{:S(2)}, u32[]{:S(2)}) collective-permute-start(f32[2,104,128]{2,1,0:T(8,128)S(1)} %get-tuple-element.61), channel_id=1, source_target_pairs={{1,2},{2,1},{3,4},{4,3},{5,6},{6,5},{7,8},{8,7},{9,10},{10,9},{11,... | collective-permute-start | bytes 319496 | tf_op jit(solution)/shard_map/ppermute | solution.py:341
  138.4 6.3 %collective-permute-start.18 = (f32[2,104,128]{2,1,0:T(8,128)S(1)}, f32[2,104,128]{2,1,0:T(8,128)S(1)}, u32[]{:S(2)}, u32[]{:S(2)}) collective-permute-start(f32[2,104,128]{2,1,0:T(8,128)S(1)} %get-tuple-element.62), channel_id=1, source_target_pairs={{0,1},{1,0},{2,3},{3,2},{4,5},{5,4},{6,7},{7,6},{8,9},{9,8},{10,11... | collective-permute-start | bytes 319496 | tf_op jit(solution)/shard_map/ppermute | solution.py:342

commit v5 on v4

--- a/solution.py
+++ b/solution.py
@@ -138,7 +138,7 @@
                 part_ref[way, f, p] = part
 
 
-def sum_kernel(flags_ref, part_ref, far_ref, near_ref, *out_refs):
+def sum_kernel(flags_ref, near_ref, far_ref, part_ref, *out_refs):
     depth = part_ref.shape[2]
     for way, out_ref in enumerate(out_refs):
         for f in range(2):
@@ -366,7 +366,7 @@
     far, near, fine0 = call(start_kernel, [message, message, grid], flags, slab, first_start)
     far, near = swapped(far, near)
     (part,) = call(old_kernel, [shape(2, 2, depth, rows, cols)], slab)
-    old_first, old_second = call(sum_kernel, [grid] * 2, flags, part, far, near)
+    old_first, old_second = call(sum_kernel, [grid] * 2, flags, near, far, part)
     old_first = lax.ppermute(old_first, "tm", back_one)
     old_second = lax.ppermute(old_second, "tm", back_one)
 

time: 176 us -> 179 us (1.017)
  the two profiles are of different devices: /device:TPU:194 before, /device:TPU:8 now
where the time goes in v5:
time: 179 us
  starting transfers between devices  66.3 us (37%)
  blocking collectives  61.5 us (34%)
  waiting for transfers between devices  41.3 us (23%)
  Pallas kernels  6.47 us (4%)
  local copies, waits for them, and re-layouts  2.61 us (1%)
    all_to_all x1, blocking collectives, local(): held = lax.all_to_all(send, 'tm', 0, 0, tiled=True)  35.1 us
    all_to_all x1, blocking collectives, local(): back = lax.all_to_all(jnp.concatenate(ends), 'tm', 0, 0, tiled=True)  26.4 us
    ppermute x7, starting transfers between devices, swapped(): lax.ppermute(far, 'space', [((i + j) % count, (i + 1 - j) % count) for i...  24.2 us
    ppermute x7, waiting for transfers between devices, swapped(): lax.ppermute(far, 'space', [((i + j) % count, (i + 1 - j) % count) for i...  22.9 us
    ppermute x7, starting transfers between devices, swapped(): lax.ppermute(near, 'space', [(i + j, i + 1 - j) for i in range(0, count,...  21.7 us
    ppermute x3, starting transfers between devices, local(): state = [end[0], lax.ppermute(end[0], 'tm', route)]  13 us
    ppermute x1, waiting for transfers between devices, local(): old_first = lax.ppermute(old_first, 'tm', back_one)  11.9 us
    pallas_call x15, Pallas kernels, call(): pl.pallas_call(kernel, out_shape=tuple(out_shapes), in_specs=[pl.BlockSpe...  6.47 us
  transfers between devices with their start and end apart: 19, of which 11 were waited for; matrix products, arithmetic and copies ran while one was open for 0% of the time, Pallas kernels for 1%

profile of v5, /device:TPU:8, one launch (start us, length us, event | category | flops | bytes accessed | tf_op | source)
XLA Modules:
  0.0 178.6 jit_solution(5538028252074732869)
XLA Ops:
  2.8 2.1 %collective-permute-start = (f32[3,2,128,128]{3,2,1,0:T(8,128)S(1)}, f32[3,2,128,128]{3,2,1,0:T(8,128)S(1)}, u32[]{:S(2)}, u32[]{:S(2)}) collective-permute-start(f32[3,2,128,128]{3,2,1,0:T(8,128)S(1)} %get-tuple-element.35), channel_id=1, source_target_pairs={{0,1},{1,0},{2,3},{3,2},{4,5},{5,4},{6,7},{7,6},{8,9},{9,8},{10,11... | collective-permute-start | bytes 1179656 | tf_op jit(solution)/shard_map/ppermute | solution.py:342
  4.9 12.0 %collective-permute-start.1 = (f32[3,2,128,128]{3,2,1,0:T(8,128)S(1)}, f32[3,2,128,128]{3,2,1,0:T(8,128)S(1)}, u32[]{:S(2)}, u32[]{:S(2)}) collective-permute-start(f32[3,2,128,128]{3,2,1,0:T(8,128)S(1)} %get-tuple-element.36), channel_id=1, source_target_pairs={{1,2},{2,1},{3,4},{4,3},{5,6},{6,5},{7,8},{8,7},{9,10},{10,9},{11,... | collective-permute-start | bytes 1179656 | tf_op jit(solution)/shard_map/ppermute | solution.py:341
  18.3 4.0 %collective-permute-done.1.far_ref = f32[3,2,128,128]{3,2,1,0:T(8,128)S(1)} collective-permute-done((f32[3,2,128,128]{3,2,1,0:T(8,128)S(1)}, f32[3,2,128,128]{3,2,1,0:T(8,128)S(1)}, u32[]{:S(2)}, u32[]{:S(2)}) %collective-permute-start.1) | collective-permute-done | bytes 393248 | tf_op jit(solution)/shard_map/ppermute | solution.py:341
  22.4 4.6 %collective-permute-start.3 = (f32[2,4,128,128]{3,2,1,0:T(8,128)S(1)}, f32[2,4,128,128]{3,2,1,0:T(8,128)S(1)}, u32[]{:S(2)}, u32[]{:S(2)}) collective-permute-start(f32[2,4,128,128]{3,2,1,0:T(8,128)S(1)} %get-tuple-element.38), channel_id=1, source_target_pairs={{0,480},{32,0},{64,32},{96,64},{128,96},{160,128},{192,160},{224,1... | collective-permute-start | bytes 1572872 | tf_op jit(solution)/shard_map/ppermute | solution.py:370
  27.1 2.7 %collective-permute-start.2 = (f32[2,4,128,128]{3,2,1,0:T(8,128)S(1)}, f32[2,4,128,128]{3,2,1,0:T(8,128)S(1)}, u32[]{:S(2)}, u32[]{:S(2)}) collective-permute-start(f32[2,4,128,128]{3,2,1,0:T(8,128)S(1)} %get-tuple-element.37), channel_id=1, source_target_pairs={{0,480},{32,0},{64,32},{96,64},{128,96},{160,128},{192,160},{224,1... | collective-permute-start | bytes 1572872 | tf_op jit(solution)/shard_map/ppermute | solution.py:371
  29.8 11.9 %collective-permute-done.3.old_ref = f32[2,4,128,128]{3,2,1,0:T(8,128)S(1)} collective-permute-done((f32[2,4,128,128]{3,2,1,0:T(8,128)S(1)}, f32[2,4,128,128]{3,2,1,0:T(8,128)S(1)}, u32[]{:S(2)}, u32[]{:S(2)}) %collective-permute-start.3) | collective-permute-done | bytes 524320 | tf_op jit(solution)/shard_map/ppermute | solution.py:370
  42.1 1.9 %collective-permute-start.4 = (f32[2,128,128]{2,1,0:T(8,128)S(1)}, f32[2,128,128]{2,1,0:T(8,128)S(1)}, u32[]{:S(2)}, u32[]{:S(2)}) collective-permute-start(f32[2,128,128]{2,1,0:T(8,128)S(1)} %get-tuple-element.41), channel_id=1, source_target_pairs={{1,2},{2,1},{3,4},{4,3},{5,6},{6,5},{7,8},{8,7},{9,10},{10,9},{11,... | collective-permute-start | bytes 393224 | tf_op jit(solution)/shard_map/ppermute | solution.py:341
  44.0 8.4 %collective-permute-start.5 = (f32[2,128,128]{2,1,0:T(8,128)S(1)}, f32[2,128,128]{2,1,0:T(8,128)S(1)}, u32[]{:S(2)}, u32[]{:S(2)}) collective-permute-start(f32[2,128,128]{2,1,0:T(8,128)S(1)} %get-tuple-element.42), channel_id=1, source_target_pairs={{0,1},{1,0},{2,3},{3,2},{4,5},{5,4},{6,7},{7,6},{8,9},{9,8},{10,11... | collective-permute-start | bytes 393224 | tf_op jit(solution)/shard_map/ppermute | solution.py:342
  53.9 2.3 %collective-permute-start.6 = (f32[2,128,128]{2,1,0:T(8,128)S(1)}, f32[2,128,128]{2,1,0:T(8,128)S(1)}, u32[]{:S(2)}, u32[]{:S(2)}) collective-permute-start(f32[2,128,128]{2,1,0:T(8,128)S(1)} %get-tuple-element.45), channel_id=1, source_target_pairs={{1,2},{2,1},{3,4},{4,3},{5,6},{6,5},{7,8},{8,7},{9,10},{10,9},{11,... | collective-permute-start | bytes 393224 | tf_op jit(solution)/shard_map/ppermute | solution.py:341
  56.2 3.5 %collective-permute-start.7 = (f32[2,128,128]{2,1,0:T(8,128)S(1)}, f32[2,128,128]{2,1,0:T(8,128)S(1)}, u32[]{:S(2)}, u32[]{:S(2)}) collective-permute-start(f32[2,128,128]{2,1,0:T(8,128)S(1)} %get-tuple-element.46), channel_id=1, source_target_pairs={{0,1},{1,0},{2,3},{3,2},{4,5},{5,4},{6,7},{7,6},{8,9},{9,8},{10,11... | collective-permute-start | bytes 393224 | tf_op jit(solution)/shard_map/ppermute | solution.py:342
  59.7 2.7 %collective-permute-done.6.far_ref = f32[2,128,128]{2,1,0:T(8,128)S(1)} collective-permute-done((f32[2,128,128]{2,1,0:T(8,128)S(1)}, f32[2,128,128]{2,1,0:T(8,128)S(1)}, u32[]{:S(2)}, u32[]{:S(2)}) %collective-permute-start.6) | collective-permute-done | bytes 131104 | tf_op jit(solution)/shard_map/ppermute | solution.py:341
  63.0 35.1 %all_to_all.10 = f32[16,2,56,128]{3,2,1,0:T(8,128)S(1)} all-to-all(f32[16,2,56,128]{3,2,1,0:T(8,128)S(1)} %get-tuple-element.48), channel_id=1, replica_groups=mesh['tm'=16,'space'=32] {'tm'}, dimensions={0} | all-to-all | bytes 1835008 | tf_op jit(solution)/shard_map/all_to_all | solution.py:388
  100.2 2.0 %collective-permute-start.9 = (f32[2,64,128]{2,1,0:T(8,128)S(1)}, f32[2,64,128]{2,1,0:T(8,128)S(1)}, u32[]{:S(2)}, u32[]{:S(2)}) collective-permute-start(f32[2,64,128]{2,1,0:T(8,128)S(1)} %get-tuple-element.50), channel_id=1, source_target_pairs={{0,1},{1,0},{2,3},{3,2},{4,5},{5,4},{6,7},{7,6},{8,9},{9,8},{10,11... | collective-permute-start | bytes 196616 | tf_op jit(solution)/shard_map/ppermute | solution.py:342
  102.2 3.7 %collective-permute-done.8.refs_1_ = f32[2,64,128]{2,1,0:T(8,128)S(1)} collective-permute-done((f32[2,64,128]{2,1,0:T(8,128)S(1)}, f32[2,64,128]{2,1,0:T(8,128)S(1)}, u32[]{:S(2)}, u32[]{:S(2)}) %collective-permute-start.8) | collective-permute-done | bytes 65568 | tf_op jit(solution)/shard_map/ppermute | solution.py:341
  106.3 3.9 %collective-permute-start.10 = (f32[2,4,8,128]{3,2,1,0:T(8,128)S(1)}, f32[2,4,8,128]{3,2,1,0:T(8,128)S(1)}, u32[]{:S(2)}, u32[]{:S(2)}) collective-permute-start(f32[2,4,8,128]{3,2,1,0:T(8,128)S(1)} %get-tuple-element.52.refs_0_), channel_id=1, source_target_pairs={{0,32},{64,0},{128,64},{192,128},{256,192},{320,256},{384,320},{44... | collective-permute-start | bytes 98312 | tf_op jit(solution)/shard_map/ppermute | solution.py:396
  112.1 2.0 %collective-permute-start.11 = (f32[2,104,128]{2,1,0:T(8,128)S(1)}, f32[2,104,128]{2,1,0:T(8,128)S(1)}, u32[]{:S(2)}, u32[]{:S(2)}) collective-permute-start(f32[2,104,128]{2,1,0:T(8,128)S(1)} %get-tuple-element.53), channel_id=1, source_target_pairs={{1,2},{2,1},{3,4},{4,3},{5,6},{6,5},{7,8},{8,7},{9,10},{10,9},{11,... | collective-permute-start | bytes 319496 | tf_op jit(solution)/shard_map/ppermute | solution.py:341
  116.0 4.2 %collective-permute-done.11.refs_2_ = f32[2,104,128]{2,1,0:T(8,128)S(1)} collective-permute-done((f32[2,104,128]{2,1,0:T(8,128)S(1)}, f32[2,104,128]{2,1,0:T(8,128)S(1)}, u32[]{:S(2)}, u32[]{:S(2)}) %collective-permute-start.11) | collective-permute-done | bytes 106528 | tf_op jit(solution)/shard_map/ppermute | solution.py:341
  120.7 3.6 %collective-permute-start.13 = (f32[2,4,8,128]{3,2,1,0:T(8,128)S(1)}, f32[2,4,8,128]{3,2,1,0:T(8,128)S(1)}, u32[]{:S(2)}, u32[]{:S(2)}) collective-permute-start(f32[2,4,8,128]{3,2,1,0:T(8,128)S(1)} %get-tuple-element.56.refs_0_), channel_id=1, source_target_pairs={{0,64},{64,128},{128,192},{192,256},{256,320},{320,384},{384,448},... | collective-permute-start | bytes 98312 | tf_op jit(solution)/shard_map/ppermute | solution.py:396
  124.3 2.2 %collective-permute-done.13.refs_1_ = f32[2,4,8,128]{3,2,1,0:T(8,128)S(1)} collective-permute-done((f32[2,4,8,128]{3,2,1,0:T(8,128)S(1)}, f32[2,4,8,128]{3,2,1,0:T(8,128)S(1)}, u32[]{:S(2)}, u32[]{:S(2)}) %collective-permute-start.13) | collective-permute-done | bytes 32800 | tf_op jit(solution)/shard_map/ppermute | solution.py:396
  126.5 2.2 %collective-permute-start.14 = (f32[2,104,128]{2,1,0:T(8,128)S(1)}, f32[2,104,128]{2,1,0:T(8,128)S(1)}, u32[]{:S(2)}, u32[]{:S(2)}) collective-permute-start(f32[2,104,128]{2,1,0:T(8,128)S(1)} %get-tuple-element.57), channel_id=1, source_target_pairs={{1,2},{2,1},{3,4},{4,3},{5,6},{6,5},{7,8},{8,7},{9,10},{10,9},{11,... | collective-permute-start | bytes 319496 | tf_op jit(solution)/shard_map/ppermute | solution.py:341
  130.7 4.0 %collective-permute-done.14.refs_2_ = f32[2,104,128]{2,1,0:T(8,128)S(1)} collective-permute-done((f32[2,104,128]{2,1,0:T(8,128)S(1)}, f32[2,104,128]{2,1,0:T(8,128)S(1)}, u32[]{:S(2)}, u32[]{:S(2)}) %collective-permute-start.14) | collective-permute-done | bytes 106528 | tf_op jit(solution)/shard_map/ppermute | solution.py:341
  135.1 5.5 %collective-permute-start.16 = (f32[2,4,8,128]{3,2,1,0:T(8,128)S(1)}, f32[2,4,8,128]{3,2,1,0:T(8,128)S(1)}, u32[]{:S(2)}, u32[]{:S(2)}) collective-permute-start(f32[2,4,8,128]{3,2,1,0:T(8,128)S(1)} %get-tuple-element.60.refs_0_), channel_id=1, source_target_pairs={{0,32},{64,0},{128,64},{192,128},{256,192},{320,256},{384,320},{44... | collective-permute-start | bytes 98312 | tf_op jit(solution)/shard_map/ppermute | solution.py:396
  146.1 4.3 %collective-permute-done.17.refs_2_ = f32[2,104,128]{2,1,0:T(8,128)S(1)} collective-permute-done((f32[2,104,128]{2,1,0:T(8,128)S(1)}, f32[2,104,128]{2,1,0:T(8,128)S(1)}, u32[]{:S(2)}, u32[]{:S(2)}) %collective-permute-start.17) | collective-permute-done | bytes 106528 | tf_op jit(solution)/shard_map/ppermute | solution.py:341
  150.9 26.4 %all_to_all.11.come_ref = f32[16,2,6,8,128]{4,3,2,1,0:T(8,128)S(1)} all-to-all(f32[16,2,6,8,128]{4,3,2,1,0:T(8,128)S(1)} %pad_maximum_fusion), channel_id=1, replica_groups=mesh['tm'=16,'space'=32] {'tm'}, dimensions={0} | all-to-all | bytes 1572864 | tf_op jit(solution)/shard_map/all_to_all | solution.py:409
  (45 shorter events, 23.2 us)
Async XLA Ops:
  0.2 1.4 copy-start
  1.6 1.0 copy-start.2
  2.6 14.3 %copy-start.1 = (f32[1,3,2,4,128,128]{5,4,3,2,1,0:T(8,128)S(1)}, f32[1,3,2,4,128,128]{5,4,3,2,1,0:T(8,128)}, u32[]{:S(2)}) copy-start(f32[1,3,2,4,128,128]{5,4,3,2,1,0:T(8,128)} %param.2) | copy-start | bytes 4718596
  2.8 15.5 %collective-permute-start = (f32[3,2,128,128]{3,2,1,0:T(8,128)S(1)}, f32[3,2,128,128]{3,2,1,0:T(8,128)S(1)}, u32[]{:S(2)}, u32[]{:S(2)}) collective-permute-start(f32[3,2,128,128]{3,2,1,0:T(8,128)S(1)} %get-tuple-element.35), channel_id=1, source_target_pairs={{0,1},{1,0},{2,3},{3,2},{4,5},{5,4},{6,7},{7,6},{8,9},{9,8},{10,11... | collective-permute-start | bytes 1179656 | tf_op jit(solution)/shard_map/ppermute | solution.py:342
  4.9 17.4 %collective-permute-start.1 = (f32[3,2,128,128]{3,2,1,0:T(8,128)S(1)}, f32[3,2,128,128]{3,2,1,0:T(8,128)S(1)}, u32[]{:S(2)}, u32[]{:S(2)}) collective-permute-start(f32[3,2,128,128]{3,2,1,0:T(8,128)S(1)} %get-tuple-element.36), channel_id=1, source_target_pairs={{1,2},{2,1},{3,4},{4,3},{5,6},{6,5},{7,8},{8,7},{9,10},{10,9},{11,... | collective-permute-start | bytes 1179656 | tf_op jit(solution)/shard_map/ppermute | solution.py:341
  22.4 19.3 %collective-permute-start.3 = (f32[2,4,128,128]{3,2,1,0:T(8,128)S(1)}, f32[2,4,128,128]{3,2,1,0:T(8,128)S(1)}, u32[]{:S(2)}, u32[]{:S(2)}) collective-permute-start(f32[2,4,128,128]{3,2,1,0:T(8,128)S(1)} %get-tuple-element.38), channel_id=1, source_target_pairs={{0,480},{32,0},{64,32},{96,64},{128,96},{160,128},{192,160},{224,1... | collective-permute-start | bytes 1572872 | tf_op jit(solution)/shard_map/ppermute | solution.py:370
  27.1 25.4 %collective-permute-start.2 = (f32[2,4,128,128]{3,2,1,0:T(8,128)S(1)}, f32[2,4,128,128]{3,2,1,0:T(8,128)S(1)}, u32[]{:S(2)}, u32[]{:S(2)}) collective-permute-start(f32[2,4,128,128]{3,2,1,0:T(8,128)S(1)} %get-tuple-element.37), channel_id=1, source_target_pairs={{0,480},{32,0},{64,32},{96,64},{128,96},{160,128},{192,160},{224,1... | collective-permute-start | bytes 1572872 | tf_op jit(solution)/shard_map/ppermute | solution.py:371
  42.1 10.3 %collective-permute-start.4 = (f32[2,128,128]{2,1,0:T(8,128)S(1)}, f32[2,128,128]{2,1,0:T(8,128)S(1)}, u32[]{:S(2)}, u32[]{:S(2)}) collective-permute-start(f32[2,128,128]{2,1,0:T(8,128)S(1)} %get-tuple-element.41), channel_id=1, source_target_pairs={{1,2},{2,1},{3,4},{4,3},{5,6},{6,5},{7,8},{8,7},{9,10},{10,9},{11,... | collective-permute-start | bytes 393224 | tf_op jit(solution)/shard_map/ppermute | solution.py:341
  44.0 9.4 %collective-permute-start.5 = (f32[2,128,128]{2,1,0:T(8,128)S(1)}, f32[2,128,128]{2,1,0:T(8,128)S(1)}, u32[]{:S(2)}, u32[]{:S(2)}) collective-permute-start(f32[2,128,128]{2,1,0:T(8,128)S(1)} %get-tuple-element.42), channel_id=1, source_target_pairs={{0,1},{1,0},{2,3},{3,2},{4,5},{5,4},{6,7},{7,6},{8,9},{9,8},{10,11... | collective-permute-start | bytes 393224 | tf_op jit(solution)/shard_map/ppermute | solution.py:342
  53.9 8.5 %collective-permute-start.6 = (f32[2,128,128]{2,1,0:T(8,128)S(1)}, f32[2,128,128]{2,1,0:T(8,128)S(1)}, u32[]{:S(2)}, u32[]{:S(2)}) collective-permute-start(f32[2,128,128]{2,1,0:T(8,128)S(1)} %get-tuple-element.45), channel_id=1, source_target_pairs={{1,2},{2,1},{3,4},{4,3},{5,6},{6,5},{7,8},{8,7},{9,10},{10,9},{11,... | collective-permute-start | bytes 393224 | tf_op jit(solution)/shard_map/ppermute | solution.py:341
  56.2 6.2 %collective-permute-start.7 = (f32[2,128,128]{2,1,0:T(8,128)S(1)}, f32[2,128,128]{2,1,0:T(8,128)S(1)}, u32[]{:S(2)}, u32[]{:S(2)}) collective-permute-start(f32[2,128,128]{2,1,0:T(8,128)S(1)} %get-tuple-element.46), channel_id=1, source_target_pairs={{0,1},{1,0},{2,3},{3,2},{4,5},{5,4},{6,7},{7,6},{8,9},{9,8},{10,11... | collective-permute-start | bytes 393224 | tf_op jit(solution)/shard_map/ppermute | solution.py:342
  98.2 7.7 %collective-permute-start.8 = (f32[2,64,128]{2,1,0:T(8,128)S(1)}, f32[2,64,128]{2,1,0:T(8,128)S(1)}, u32[]{:S(2)}, u32[]{:S(2)}) collective-permute-start(f32[2,64,128]{2,1,0:T(8,128)S(1)} %get-tuple-element.49), channel_id=1, source_target_pairs={{1,2},{2,1},{3,4},{4,3},{5,6},{6,5},{7,8},{8,7},{9,10},{10,9},{11,... | collective-permute-start | bytes 196616 | tf_op jit(solution)/shard_map/ppermute | solution.py:341
  100.2 5.8 %collective-permute-start.9 = (f32[2,64,128]{2,1,0:T(8,128)S(1)}, f32[2,64,128]{2,1,0:T(8,128)S(1)}, u32[]{:S(2)}, u32[]{:S(2)}) collective-permute-start(f32[2,64,128]{2,1,0:T(8,128)S(1)} %get-tuple-element.50), channel_id=1, source_target_pairs={{0,1},{1,0},{2,3},{3,2},{4,5},{5,4},{6,7},{7,6},{8,9},{9,8},{10,11... | collective-permute-start | bytes 196616 | tf_op jit(solution)/shard_map/ppermute | solution.py:342
  106.3 5.8 %collective-permute-start.10 = (f32[2,4,8,128]{3,2,1,0:T(8,128)S(1)}, f32[2,4,8,128]{3,2,1,0:T(8,128)S(1)}, u32[]{:S(2)}, u32[]{:S(2)}) collective-permute-start(f32[2,4,8,128]{3,2,1,0:T(8,128)S(1)} %get-tuple-element.52.refs_0_), channel_id=1, source_target_pairs={{0,32},{64,0},{128,64},{192,128},{256,192},{320,256},{384,320},{44... | collective-permute-start | bytes 98312 | tf_op jit(solution)/shard_map/ppermute | solution.py:396
  112.1 8.1 %collective-permute-start.11 = (f32[2,104,128]{2,1,0:T(8,128)S(1)}, f32[2,104,128]{2,1,0:T(8,128)S(1)}, u32[]{:S(2)}, u32[]{:S(2)}) collective-permute-start(f32[2,104,128]{2,1,0:T(8,128)S(1)} %get-tuple-element.53), channel_id=1, source_target_pairs={{1,2},{2,1},{3,4},{4,3},{5,6},{6,5},{7,8},{8,7},{9,10},{10,9},{11,... | collective-permute-start | bytes 319496 | tf_op jit(solution)/shard_map/ppermute | solution.py:341
  114.1 6.1 %collective-permute-start.12 = (f32[2,104,128]{2,1,0:T(8,128)S(1)}, f32[2,104,128]{2,1,0:T(8,128)S(1)}, u32[]{:S(2)}, u32[]{:S(2)}) collective-permute-start(f32[2,104,128]{2,1,0:T(8,128)S(1)} %get-tuple-element.54), channel_id=1, source_target_pairs={{0,1},{1,0},{2,3},{3,2},{4,5},{5,4},{6,7},{7,6},{8,9},{9,8},{10,11... | collective-permute-start | bytes 319496 | tf_op jit(solution)/shard_map/ppermute | solution.py:342
  120.7 5.8 %collective-permute-start.13 = (f32[2,4,8,128]{3,2,1,0:T(8,128)S(1)}, f32[2,4,8,128]{3,2,1,0:T(8,128)S(1)}, u32[]{:S(2)}, u32[]{:S(2)}) collective-permute-start(f32[2,4,8,128]{3,2,1,0:T(8,128)S(1)} %get-tuple-element.56.refs_0_), channel_id=1, source_target_pairs={{0,64},{64,128},{128,192},{192,256},{256,320},{320,384},{384,448},... | collective-permute-start | bytes 98312 | tf_op jit(solution)/shard_map/ppermute | solution.py:396
  126.5 8.1 %collective-permute-start.14 = (f32[2,104,128]{2,1,0:T(8,128)S(1)}, f32[2,104,128]{2,1,0:T(8,128)S(1)}, u32[]{:S(2)}, u32[]{:S(2)}) collective-permute-start(f32[2,104,128]{2,1,0:T(8,128)S(1)} %get-tuple-element.57), channel_id=1, source_target_pairs={{1,2},{2,1},{3,4},{4,3},{5,6},{6,5},{7,8},{8,7},{9,10},{10,9},{11,... | collective-permute-start | bytes 319496 | tf_op jit(solution)/shard_map/ppermute | solution.py:341
  128.7 5.9 %collective-permute-start.15 = (f32[2,104,128]{2,1,0:T(8,128)S(1)}, f32[2,104,128]{2,1,0:T(8,128)S(1)}, u32[]{:S(2)}, u32[]{:S(2)}) collective-permute-start(f32[2,104,128]{2,1,0:T(8,128)S(1)} %get-tuple-element.58), channel_id=1, source_target_pairs={{0,1},{1,0},{2,3},{3,2},{4,5},{5,4},{6,7},{7,6},{8,9},{9,8},{10,11... | collective-permute-start | bytes 319496 | tf_op jit(solution)/shard_map/ppermute | solution.py:342
  135.1 7.1 %collective-permute-start.16 = (f32[2,4,8,128]{3,2,1,0:T(8,128)S(1)}, f32[2,4,8,128]{3,2,1,0:T(8,128)S(1)}, u32[]{:S(2)}, u32[]{:S(2)}) collective-permute-start(f32[2,4,8,128]{3,2,1,0:T(8,128)S(1)} %get-tuple-element.60.refs_0_), channel_id=1, source_target_pairs={{0,32},{64,0},{128,64},{192,128},{256,192},{320,256},{384,320},{44... | collective-permute-start | bytes 98312 | tf_op jit(solution)/shard_map/ppermute | solution.py:396
  142.3 8.1 %collective-permute-start.17 = (f32[2,104,128]{2,1,0:T(8,128)S(1)}, f32[2,104,128]{2,1,0:T(8,128)S(1)}, u32[]{:S(2)}, u32[]{:S(2)}) collective-permute-start(f32[2,104,128]{2,1,0:T(8,128)S(1)} %get-tuple-element.61), channel_id=1, source_target_pairs={{1,2},{2,1},{3,4},{4,3},{5,6},{6,5},{7,8},{8,7},{9,10},{10,9},{11,... | collective-permute-start | bytes 319496 | tf_op jit(solution)/shard_map/ppermute | solution.py:341
  144.2 6.2 %collective-permute-start.18 = (f32[2,104,128]{2,1,0:T(8,128)S(1)}, f32[2,104,128]{2,1,0:T(8,128)S(1)}, u32[]{:S(2)}, u32[]{:S(2)}) collective-permute-start(f32[2,104,128]{2,1,0:T(8,128)S(1)} %get-tuple-element.62), channel_id=1, source_target_pairs={{0,1},{1,0},{2,3},{3,2},{4,5},{5,4},{6,7},{7,6},{8,9},{9,8},{10,11... | collective-permute-start | bytes 319496 | tf_op jit(solution)/shard_map/ppermute | solution.py:342

commit v6 on v5

--- a/solution.py
+++ b/solution.py
@@ -120,7 +120,7 @@
         put_edges(flags_ref, far_ref, near_ref, (2, f), start_ref[f, 0], start_ref[f, depth - 1])
 
 
-def old_kernel(states_ref, part_ref):
+def old_kernel(states_ref, inner_ref, part_ref):
     depth = states_ref.shape[2]
     for p in range(depth):
         react = [reactions(states_ref[j, 0, p], states_ref[j, 1, p]) for j in range(3)]
@@ -135,20 +135,27 @@
                 part = diffuse[f] * total
                 for j in range(3):
                     part = part + old_weights[way][j] * react[j][f]
-                part_ref[way, f, p] = part
-
-
-def sum_kernel(flags_ref, near_ref, far_ref, part_ref, *out_refs):
+                if way == 0 and 0 < p < depth - 1:
+                    inner_ref[f, p - 1] = part
+                else:
+                    part_ref[way, f, p] = part
+
+
+def sum_kernel(flags_ref, part_ref, far_ref, near_ref, edge_ref, second_ref):
     depth = part_ref.shape[2]
-    for way, out_ref in enumerate(out_refs):
-        for f in range(2):
-            for p in range(depth):
-                total = part_ref[way, f, p]
-                if p == 0:
-                    total = total + diffuse[f] * below(flags_ref, far_ref[way, f], near_ref[way, f])
-                if p == depth - 1:
-                    total = total + diffuse[f] * above(flags_ref, far_ref[way, f], near_ref[way, f])
-                out_ref[f, p] = total
+    for f in range(2):
+        for way in range(2):
+            lo = diffuse[f] * below(flags_ref, far_ref[way, f], near_ref[way, f])
+            hi = diffuse[f] * above(flags_ref, far_ref[way, f], near_ref[way, f])
+            head, tail = part_ref[way, f, 0] + lo, part_ref[way, f, depth - 1] + hi
+            if way == 0:
+                edge_ref[f, 0] = head
+                edge_ref[f, 1] = tail
+            else:
+                second_ref[f, 0] = head
+                second_ref[f, depth - 1] = tail
+                for p in range(1, depth - 1):
+                    second_ref[f, p] = part_ref[way, f, p]
 
 
 def planes_with(flags_ref, x_ref, far_ref, near_ref):
@@ -168,13 +175,19 @@
     depth = x_ref.shape[1]
     plane = planes_with(flags_ref, x_ref, far_ref, near_ref)
     if way == 0:
-        next_ref, keep_ref, next_far_ref, next_near_ref = refs
+        edge_ref, next_ref, keep_ref, next_far_ref, next_near_ref = refs
     else:
         rate_ref, next_ref, keep_ref, next_far_ref, next_near_ref = refs
     for p in range(depth):
         rate = plane_rates(plane(p - 1), plane(p), plane(p + 1))
         for f in range(2):
-            next_ref[f, p] = x_ref[f, p] + half_step * rate[f] + old_ref[f, p]
+            if way == 1:
+                old = old_ref[f, p]
+            elif 0 < p < depth - 1:
+                old = old_ref[f, p - 1]
+            else:
+                old = edge_ref[f, min(p, 1)]
+            next_ref[f, p] = x_ref[f, p] + half_step * rate[f] + old
             if way == 0:
                 keep_ref[f, p] = rate[f]
             else:
@@ -365,14 +378,17 @@
     message = shape(3, 2, rows, cols)
     far, near, fine0 = call(start_kernel, [message, message, grid], flags, slab, first_start)
     far, near = swapped(far, near)
-    (part,) = call(old_kernel, [shape(2, 2, depth, rows, cols)], slab)
-    old_first, old_second = call(sum_kernel, [grid] * 2, flags, near, far, part)
-    old_first = lax.ppermute(old_first, "tm", back_one)
+    inner, part = call(
+        old_kernel, [shape(2, depth - 2, rows, cols), shape(2, 2, depth, rows, cols)], slab
+    )
+    inner = lax.ppermute(inner, "tm", back_one)
+    edges, old_second = call(sum_kernel, [shape(2, 2, rows, cols), grid], flags, part, far, near)
+    edges = lax.ppermute(edges, "tm", back_one)
     old_second = lax.ppermute(old_second, "tm", back_one)
 
     fine1, rate0, far, near = call(
         functools.partial(node_kernel, 0), [grid] * 2 + [edge] * 2,
-        flags, old_first, fine0, far[2], near[2],
+        flags, inner, fine0, far[2], near[2], edges,
     )
     far, near = swapped(far, near)
     fine2, total, far, near = call(

time: 179 us -> 179 us (level)
  starting transfers between devices: 66.3 us -> 74.2 us
  waiting for transfers between devices: 41.3 us -> 34 us
    ppermute x1 -> x2, waiting for transfers between devices: 11.9 us -> 3.16 us  [the longest x1 3.16 us: local(): edges = lax.ppermute(edges, 'tm', back_one)]
    ppermute x7, starting transfers between devices: 21.7 us -> 13.4 us  [swapped(): lax.ppermute(near, 'space', [(i + j, i + 1 - j) for i in range(0, count,...]
    ppermute x7, starting transfers between devices: 24.2 us -> 31.6 us  [swapped(): lax.ppermute(far, 'space', [((i + j) % count, (i + 1 - j) % count) for i...]
    ppermute x1, starting transfers between devices: 2.72 us -> 7.54 us  [local(): old_second = lax.ppermute(old_second, 'tm', back_one)]
    ppermute x1, waiting for transfers between devices: 0.01 us -> 3.69 us  [local(): old_second = lax.ppermute(old_second, 'tm', back_one)]
    ppermute x1 -> x2, starting transfers between devices: 4.62 us -> 7.23 us  [the longest x1 4.52 us: local(): inner = lax.ppermute(inner, 'tm', back_one)]
  transfers between devices with their start and end apart: 19 -> 20, of which waited for: 11 -> 12; matrix products, arithmetic and copies ran while one was open for 0% -> 0% of each run, Pallas kernels for 1% -> 1%
where the time goes in v6:
time: 179 us; the launch traced here: 178 us
  starting transfers between devices  74.2 us (41%)
  blocking collectives  60.4 us (34%)
  waiting for transfers between devices  34 us (19%)
  Pallas kernels  6.3 us (4%)
  local copies, waits for them, and re-layouts  2.61 us (1%)
    all_to_all x1, blocking collectives, local(): held = lax.all_to_all(send, 'tm', 0, 0, tiled=True)  33.9 us
    ppermute x7, starting transfers between devices, swapped(): lax.ppermute(far, 'space', [((i + j) % count, (i + 1 - j) % count) for i...  31.6 us
    all_to_all x1, blocking collectives, local(): back = lax.all_to_all(jnp.concatenate(ends), 'tm', 0, 0, tiled=True)  26.5 us
    ppermute x7, waiting for transfers between devices, swapped(): lax.ppermute(far, 'space', [((i + j) % count, (i + 1 - j) % count) for i...  21.1 us
    ppermute x3, starting transfers between devices, local(): state = [end[0], lax.ppermute(end[0], 'tm', route)]  14.4 us
    ppermute x7, starting transfers between devices, swapped(): lax.ppermute(near, 'space', [(i + j, i + 1 - j) for i in range(0, count,...  13.4 us
    ppermute x1, starting transfers between devices, local(): old_second = lax.ppermute(old_second, 'tm', back_one)  7.54 us
    pallas_call x15, Pallas kernels, call(): pl.pallas_call(kernel, out_shape=tuple(out_shapes), in_specs=[pl.BlockSpe...  6.3 us
  transfers between devices with their start and end apart: 20, of which 12 were waited for; matrix products, arithmetic and copies ran while one was open for 0% of the time, Pallas kernels for 1%

profile of v6, /device:TPU:8, one launch (start us, length us, event | category | flops | bytes accessed | tf_op | source)
XLA Modules:
  0.0 177.9 jit_solution(17190744086585518869)
XLA Ops:
  2.8 11.3 %collective-permute-start = (f32[3,2,128,128]{3,2,1,0:T(8,128)S(1)}, f32[3,2,128,128]{3,2,1,0:T(8,128)S(1)}, u32[]{:S(2)}, u32[]{:S(2)}) collective-permute-start(f32[3,2,128,128]{3,2,1,0:T(8,128)S(1)} %get-tuple-element.38), channel_id=1, source_target_pairs={{1,2},{2,1},{3,4},{4,3},{5,6},{6,5},{7,8},{8,7},{9,10},{10,9},{11,... | collective-permute-start | bytes 1179656 | tf_op jit(solution)/shard_map/ppermute | solution.py:354
  14.2 1.9 %collective-permute-start.1 = (f32[3,2,128,128]{3,2,1,0:T(8,128)S(1)}, f32[3,2,128,128]{3,2,1,0:T(8,128)S(1)}, u32[]{:S(2)}, u32[]{:S(2)}) collective-permute-start(f32[3,2,128,128]{3,2,1,0:T(8,128)S(1)} %get-tuple-element.39), channel_id=1, source_target_pairs={{0,1},{1,0},{2,3},{3,2},{4,5},{5,4},{6,7},{7,6},{8,9},{9,8},{10,11... | collective-permute-start | bytes 1179656 | tf_op jit(solution)/shard_map/ppermute | solution.py:355
  17.4 4.5 %collective-permute-start.3 = (f32[2,2,128,128]{3,2,1,0:T(8,128)S(1)}, f32[2,2,128,128]{3,2,1,0:T(8,128)S(1)}, u32[]{:S(2)}, u32[]{:S(2)}) collective-permute-start(f32[2,2,128,128]{3,2,1,0:T(8,128)S(1)} %get-tuple-element.41), channel_id=1, source_target_pairs={{0,480},{32,0},{64,32},{96,64},{128,96},{160,128},{192,160},{224,1... | collective-permute-start | bytes 786440 | tf_op jit(solution)/shard_map/ppermute | solution.py:384
  22.0 2.7 %collective-permute-start.4 = (f32[2,2,128,128]{3,2,1,0:T(8,128)S(1)}, f32[2,2,128,128]{3,2,1,0:T(8,128)S(1)}, u32[]{:S(2)}, u32[]{:S(2)}) collective-permute-start(f32[2,2,128,128]{3,2,1,0:T(8,128)S(1)} %get-tuple-element.43), channel_id=1, source_target_pairs={{0,480},{32,0},{64,32},{96,64},{128,96},{160,128},{192,160},{224,1... | collective-permute-start | bytes 786440 | tf_op jit(solution)/shard_map/ppermute | solution.py:386
  24.7 7.5 %collective-permute-start.2 = (f32[2,4,128,128]{3,2,1,0:T(8,128)S(1)}, f32[2,4,128,128]{3,2,1,0:T(8,128)S(1)}, u32[]{:S(2)}, u32[]{:S(2)}) collective-permute-start(f32[2,4,128,128]{3,2,1,0:T(8,128)S(1)} %get-tuple-element.40), channel_id=1, source_target_pairs={{0,480},{32,0},{64,32},{96,64},{128,96},{160,128},{192,160},{224,1... | collective-permute-start | bytes 1572872 | tf_op jit(solution)/shard_map/ppermute | solution.py:387
  32.3 3.2 %collective-permute-done.4.refs_0_ = f32[2,2,128,128]{3,2,1,0:T(8,128)S(1)} collective-permute-done((f32[2,2,128,128]{3,2,1,0:T(8,128)S(1)}, f32[2,2,128,128]{3,2,1,0:T(8,128)S(1)}, u32[]{:S(2)}, u32[]{:S(2)}) %collective-permute-start.4) | collective-permute-done | bytes 262176 | tf_op jit(solution)/shard_map/ppermute | solution.py:386
  35.9 1.9 %collective-permute-start.5 = (f32[2,128,128]{2,1,0:T(8,128)S(1)}, f32[2,128,128]{2,1,0:T(8,128)S(1)}, u32[]{:S(2)}, u32[]{:S(2)}) collective-permute-start(f32[2,128,128]{2,1,0:T(8,128)S(1)} %get-tuple-element.45), channel_id=1, source_target_pairs={{1,2},{2,1},{3,4},{4,3},{5,6},{6,5},{7,8},{8,7},{9,10},{10,9},{11,... | collective-permute-start | bytes 393224 | tf_op jit(solution)/shard_map/ppermute | solution.py:354
  37.9 1.9 %collective-permute-start.6 = (f32[2,128,128]{2,1,0:T(8,128)S(1)}, f32[2,128,128]{2,1,0:T(8,128)S(1)}, u32[]{:S(2)}, u32[]{:S(2)}) collective-permute-start(f32[2,128,128]{2,1,0:T(8,128)S(1)} %get-tuple-element.46), channel_id=1, source_target_pairs={{0,1},{1,0},{2,3},{3,2},{4,5},{5,4},{6,7},{7,6},{8,9},{9,8},{10,11... | collective-permute-start | bytes 393224 | tf_op jit(solution)/shard_map/ppermute | solution.py:355
  39.8 4.6 %collective-permute-done.5.far_ref = f32[2,128,128]{2,1,0:T(8,128)S(1)} collective-permute-done((f32[2,128,128]{2,1,0:T(8,128)S(1)}, f32[2,128,128]{2,1,0:T(8,128)S(1)}, u32[]{:S(2)}, u32[]{:S(2)}) %collective-permute-start.5) | collective-permute-done | bytes 131104 | tf_op jit(solution)/shard_map/ppermute | solution.py:354
  44.5 3.7 %collective-permute-done.2.old_ref = f32[2,4,128,128]{3,2,1,0:T(8,128)S(1)} collective-permute-done((f32[2,4,128,128]{3,2,1,0:T(8,128)S(1)}, f32[2,4,128,128]{3,2,1,0:T(8,128)S(1)}, u32[]{:S(2)}, u32[]{:S(2)}) %collective-permute-start.2) | collective-permute-done | bytes 524320 | tf_op jit(solution)/shard_map/ppermute | solution.py:387
  48.6 9.7 %collective-permute-start.7 = (f32[2,128,128]{2,1,0:T(8,128)S(1)}, f32[2,128,128]{2,1,0:T(8,128)S(1)}, u32[]{:S(2)}, u32[]{:S(2)}) collective-permute-start(f32[2,128,128]{2,1,0:T(8,128)S(1)} %get-tuple-element.49), channel_id=1, source_target_pairs={{1,2},{2,1},{3,4},{4,3},{5,6},{6,5},{7,8},{8,7},{9,10},{10,9},{11,... | collective-permute-start | bytes 393224 | tf_op jit(solution)/shard_map/ppermute | solution.py:354
  62.2 33.9 %all_to_all.10 = f32[16,2,56,128]{3,2,1,0:T(8,128)S(1)} all-to-all(f32[16,2,56,128]{3,2,1,0:T(8,128)S(1)} %get-tuple-element.52), channel_id=1, replica_groups=mesh['tm'=16,'space'=32] {'tm'}, dimensions={0} | all-to-all | bytes 1835008 | tf_op jit(solution)/shard_map/all_to_all | solution.py:404
  96.2 2.4 %collective-permute-start.9 = (f32[2,64,128]{2,1,0:T(8,128)S(1)}, f32[2,64,128]{2,1,0:T(8,128)S(1)}, u32[]{:S(2)}, u32[]{:S(2)}) collective-permute-start(f32[2,64,128]{2,1,0:T(8,128)S(1)} %get-tuple-element.53), channel_id=1, source_target_pairs={{1,2},{2,1},{3,4},{4,3},{5,6},{6,5},{7,8},{8,7},{9,10},{10,9},{11,... | collective-permute-start | bytes 196616 | tf_op jit(solution)/shard_map/ppermute | solution.py:354
  100.5 3.4 %collective-permute-done.9.refs_1_ = f32[2,64,128]{2,1,0:T(8,128)S(1)} collective-permute-done((f32[2,64,128]{2,1,0:T(8,128)S(1)}, f32[2,64,128]{2,1,0:T(8,128)S(1)}, u32[]{:S(2)}, u32[]{:S(2)}) %collective-permute-start.9) | collective-permute-done | bytes 65568 | tf_op jit(solution)/shard_map/ppermute | solution.py:354
  104.2 4.0 %collective-permute-start.11 = (f32[2,4,8,128]{3,2,1,0:T(8,128)S(1)}, f32[2,4,8,128]{3,2,1,0:T(8,128)S(1)}, u32[]{:S(2)}, u32[]{:S(2)}) collective-permute-start(f32[2,4,8,128]{3,2,1,0:T(8,128)S(1)} %get-tuple-element.56.refs_0_), channel_id=1, source_target_pairs={{0,32},{64,0},{128,64},{192,128},{256,192},{320,256},{384,320},{44... | collective-permute-start | bytes 98312 | tf_op jit(solution)/shard_map/ppermute | solution.py:412
  110.1 2.1 %collective-permute-start.12 = (f32[2,104,128]{2,1,0:T(8,128)S(1)}, f32[2,104,128]{2,1,0:T(8,128)S(1)}, u32[]{:S(2)}, u32[]{:S(2)}) collective-permute-start(f32[2,104,128]{2,1,0:T(8,128)S(1)} %get-tuple-element.57), channel_id=1, source_target_pairs={{1,2},{2,1},{3,4},{4,3},{5,6},{6,5},{7,8},{8,7},{9,10},{10,9},{11,... | collective-permute-start | bytes 319496 | tf_op jit(solution)/shard_map/ppermute | solution.py:354
  114.1 4.1 %collective-permute-done.12.refs_2_ = f32[2,104,128]{2,1,0:T(8,128)S(1)} collective-permute-done((f32[2,104,128]{2,1,0:T(8,128)S(1)}, f32[2,104,128]{2,1,0:T(8,128)S(1)}, u32[]{:S(2)}, u32[]{:S(2)}) %collective-permute-start.12) | collective-permute-done | bytes 106528 | tf_op jit(solution)/shard_map/ppermute | solution.py:354
  118.7 3.8 %collective-permute-start.14 = (f32[2,4,8,128]{3,2,1,0:T(8,128)S(1)}, f32[2,4,8,128]{3,2,1,0:T(8,128)S(1)}, u32[]{:S(2)}, u32[]{:S(2)}) collective-permute-start(f32[2,4,8,128]{3,2,1,0:T(8,128)S(1)} %get-tuple-element.60.refs_0_), channel_id=1, source_target_pairs={{0,64},{64,128},{128,192},{192,256},{256,320},{320,384},{384,448},... | collective-permute-start | bytes 98312 | tf_op jit(solution)/shard_map/ppermute | solution.py:412
  122.5 2.1 %collective-permute-done.14.refs_1_ = f32[2,4,8,128]{3,2,1,0:T(8,128)S(1)} collective-permute-done((f32[2,4,8,128]{3,2,1,0:T(8,128)S(1)}, f32[2,4,8,128]{3,2,1,0:T(8,128)S(1)}, u32[]{:S(2)}, u32[]{:S(2)}) %collective-permute-start.14) | collective-permute-done | bytes 32800 | tf_op jit(solution)/shard_map/ppermute | solution.py:412
  124.6 2.2 %collective-permute-start.15 = (f32[2,104,128]{2,1,0:T(8,128)S(1)}, f32[2,104,128]{2,1,0:T(8,128)S(1)}, u32[]{:S(2)}, u32[]{:S(2)}) collective-permute-start(f32[2,104,128]{2,1,0:T(8,128)S(1)} %get-tuple-element.61), channel_id=1, source_target_pairs={{1,2},{2,1},{3,4},{4,3},{5,6},{6,5},{7,8},{8,7},{9,10},{10,9},{11,... | collective-permute-start | bytes 319496 | tf_op jit(solution)/shard_map/ppermute | solution.py:354
  128.7 4.0 %collective-permute-done.15.refs_2_ = f32[2,104,128]{2,1,0:T(8,128)S(1)} collective-permute-done((f32[2,104,128]{2,1,0:T(8,128)S(1)}, f32[2,104,128]{2,1,0:T(8,128)S(1)}, u32[]{:S(2)}, u32[]{:S(2)}) %collective-permute-start.15) | collective-permute-done | bytes 106528 | tf_op jit(solution)/shard_map/ppermute | solution.py:354
  133.2 6.6 %collective-permute-start.17 = (f32[2,4,8,128]{3,2,1,0:T(8,128)S(1)}, f32[2,4,8,128]{3,2,1,0:T(8,128)S(1)}, u32[]{:S(2)}, u32[]{:S(2)}) collective-permute-start(f32[2,4,8,128]{3,2,1,0:T(8,128)S(1)} %get-tuple-element.64.refs_0_), channel_id=1, source_target_pairs={{0,32},{64,0},{128,64},{192,128},{256,192},{320,256},{384,320},{44... | collective-permute-start | bytes 98312 | tf_op jit(solution)/shard_map/ppermute | solution.py:412
  145.3 4.3 %collective-permute-done.18.refs_2_ = f32[2,104,128]{2,1,0:T(8,128)S(1)} collective-permute-done((f32[2,104,128]{2,1,0:T(8,128)S(1)}, f32[2,104,128]{2,1,0:T(8,128)S(1)}, u32[]{:S(2)}, u32[]{:S(2)}) %collective-permute-start.18) | collective-permute-done | bytes 106528 | tf_op jit(solution)/shard_map/ppermute | solution.py:354
  150.1 26.5 %all_to_all.11.come_ref = f32[16,2,6,8,128]{4,3,2,1,0:T(8,128)S(1)} all-to-all(f32[16,2,6,8,128]{4,3,2,1,0:T(8,128)S(1)} %pad_maximum_fusion), channel_id=1, replica_groups=mesh['tm'=16,'space'=32] {'tm'}, dimensions={0} | all-to-all | bytes 1572864 | tf_op jit(solution)/shard_map/all_to_all | solution.py:425
  (45 shorter events, 25.2 us)
Async XLA Ops:
  0.2 1.4 copy-start
  1.6 1.0 copy-start.1
  2.8 19.1 %collective-permute-start = (f32[3,2,128,128]{3,2,1,0:T(8,128)S(1)}, f32[3,2,128,128]{3,2,1,0:T(8,128)S(1)}, u32[]{:S(2)}, u32[]{:S(2)}) collective-permute-start(f32[3,2,128,128]{3,2,1,0:T(8,128)S(1)} %get-tuple-element.38), channel_id=1, source_target_pairs={{1,2},{2,1},{3,4},{4,3},{5,6},{6,5},{7,8},{8,7},{9,10},{10,9},{11,... | collective-permute-start | bytes 1179656 | tf_op jit(solution)/shard_map/ppermute | solution.py:354
  14.2 7.8 %collective-permute-start.1 = (f32[3,2,128,128]{3,2,1,0:T(8,128)S(1)}, f32[3,2,128,128]{3,2,1,0:T(8,128)S(1)}, u32[]{:S(2)}, u32[]{:S(2)}) collective-permute-start(f32[3,2,128,128]{3,2,1,0:T(8,128)S(1)} %get-tuple-element.39), channel_id=1, source_target_pairs={{0,1},{1,0},{2,3},{3,2},{4,5},{5,4},{6,7},{7,6},{8,9},{9,8},{10,11... | collective-permute-start | bytes 1179656 | tf_op jit(solution)/shard_map/ppermute | solution.py:355
  17.4 15.0 %collective-permute-start.3 = (f32[2,2,128,128]{3,2,1,0:T(8,128)S(1)}, f32[2,2,128,128]{3,2,1,0:T(8,128)S(1)}, u32[]{:S(2)}, u32[]{:S(2)}) collective-permute-start(f32[2,2,128,128]{3,2,1,0:T(8,128)S(1)} %get-tuple-element.41), channel_id=1, source_target_pairs={{0,480},{32,0},{64,32},{96,64},{128,96},{160,128},{192,160},{224,1... | collective-permute-start | bytes 786440 | tf_op jit(solution)/shard_map/ppermute | solution.py:384
  22.0 13.5 %collective-permute-start.4 = (f32[2,2,128,128]{3,2,1,0:T(8,128)S(1)}, f32[2,2,128,128]{3,2,1,0:T(8,128)S(1)}, u32[]{:S(2)}, u32[]{:S(2)}) collective-permute-start(f32[2,2,128,128]{3,2,1,0:T(8,128)S(1)} %get-tuple-element.43), channel_id=1, source_target_pairs={{0,480},{32,0},{64,32},{96,64},{128,96},{160,128},{192,160},{224,1... | collective-permute-start | bytes 786440 | tf_op jit(solution)/shard_map/ppermute | solution.py:386
  24.7 23.4 %collective-permute-start.2 = (f32[2,4,128,128]{3,2,1,0:T(8,128)S(1)}, f32[2,4,128,128]{3,2,1,0:T(8,128)S(1)}, u32[]{:S(2)}, u32[]{:S(2)}) collective-permute-start(f32[2,4,128,128]{3,2,1,0:T(8,128)S(1)} %get-tuple-element.40), channel_id=1, source_target_pairs={{0,480},{32,0},{64,32},{96,64},{128,96},{160,128},{192,160},{224,1... | collective-permute-start | bytes 1572872 | tf_op jit(solution)/shard_map/ppermute | solution.py:387
  35.9 8.5 %collective-permute-start.5 = (f32[2,128,128]{2,1,0:T(8,128)S(1)}, f32[2,128,128]{2,1,0:T(8,128)S(1)}, u32[]{:S(2)}, u32[]{:S(2)}) collective-permute-start(f32[2,128,128]{2,1,0:T(8,128)S(1)} %get-tuple-element.45), channel_id=1, source_target_pairs={{1,2},{2,1},{3,4},{4,3},{5,6},{6,5},{7,8},{8,7},{9,10},{10,9},{11,... | collective-permute-start | bytes 393224 | tf_op jit(solution)/shard_map/ppermute | solution.py:354
  37.9 6.6 %collective-permute-start.6 = (f32[2,128,128]{2,1,0:T(8,128)S(1)}, f32[2,128,128]{2,1,0:T(8,128)S(1)}, u32[]{:S(2)}, u32[]{:S(2)}) collective-permute-start(f32[2,128,128]{2,1,0:T(8,128)S(1)} %get-tuple-element.46), channel_id=1, source_target_pairs={{0,1},{1,0},{2,3},{3,2},{4,5},{5,4},{6,7},{7,6},{8,9},{9,8},{10,11... | collective-permute-start | bytes 393224 | tf_op jit(solution)/shard_map/ppermute | solution.py:355
  48.6 12.4 %collective-permute-start.7 = (f32[2,128,128]{2,1,0:T(8,128)S(1)}, f32[2,128,128]{2,1,0:T(8,128)S(1)}, u32[]{:S(2)}, u32[]{:S(2)}) collective-permute-start(f32[2,128,128]{2,1,0:T(8,128)S(1)} %get-tuple-element.49), channel_id=1, source_target_pairs={{1,2},{2,1},{3,4},{4,3},{5,6},{6,5},{7,8},{8,7},{9,10},{10,9},{11,... | collective-permute-start | bytes 393224 | tf_op jit(solution)/shard_map/ppermute | solution.py:354
  58.4 3.2 %collective-permute-start.8 = (f32[2,128,128]{2,1,0:T(8,128)S(1)}, f32[2,128,128]{2,1,0:T(8,128)S(1)}, u32[]{:S(2)}, u32[]{:S(2)}) collective-permute-start(f32[2,128,128]{2,1,0:T(8,128)S(1)} %get-tuple-element.50), channel_id=1, source_target_pairs={{0,1},{1,0},{2,3},{3,2},{4,5},{5,4},{6,7},{7,6},{8,9},{9,8},{10,11... | collective-permute-start | bytes 393224 | tf_op jit(solution)/shard_map/ppermute | solution.py:355
  96.2 7.7 %collective-permute-start.9 = (f32[2,64,128]{2,1,0:T(8,128)S(1)}, f32[2,64,128]{2,1,0:T(8,128)S(1)}, u32[]{:S(2)}, u32[]{:S(2)}) collective-permute-start(f32[2,64,128]{2,1,0:T(8,128)S(1)} %get-tuple-element.53), channel_id=1, source_target_pairs={{1,2},{2,1},{3,4},{4,3},{5,6},{6,5},{7,8},{8,7},{9,10},{10,9},{11,... | collective-permute-start | bytes 196616 | tf_op jit(solution)/shard_map/ppermute | solution.py:354
  98.6 5.3 %collective-permute-start.10 = (f32[2,64,128]{2,1,0:T(8,128)S(1)}, f32[2,64,128]{2,1,0:T(8,128)S(1)}, u32[]{:S(2)}, u32[]{:S(2)}) collective-permute-start(f32[2,64,128]{2,1,0:T(8,128)S(1)} %get-tuple-element.54), channel_id=1, source_target_pairs={{0,1},{1,0},{2,3},{3,2},{4,5},{5,4},{6,7},{7,6},{8,9},{9,8},{10,11... | collective-permute-start | bytes 196616 | tf_op jit(solution)/shard_map/ppermute | solution.py:355
  104.2 5.8 %collective-permute-start.11 = (f32[2,4,8,128]{3,2,1,0:T(8,128)S(1)}, f32[2,4,8,128]{3,2,1,0:T(8,128)S(1)}, u32[]{:S(2)}, u32[]{:S(2)}) collective-permute-start(f32[2,4,8,128]{3,2,1,0:T(8,128)S(1)} %get-tuple-element.56.refs_0_), channel_id=1, source_target_pairs={{0,32},{64,0},{128,64},{192,128},{256,192},{320,256},{384,320},{44... | collective-permute-start | bytes 98312 | tf_op jit(solution)/shard_map/ppermute | solution.py:412
  110.1 8.1 %collective-permute-start.12 = (f32[2,104,128]{2,1,0:T(8,128)S(1)}, f32[2,104,128]{2,1,0:T(8,128)S(1)}, u32[]{:S(2)}, u32[]{:S(2)}) collective-permute-start(f32[2,104,128]{2,1,0:T(8,128)S(1)} %get-tuple-element.57), channel_id=1, source_target_pairs={{1,2},{2,1},{3,4},{4,3},{5,6},{6,5},{7,8},{8,7},{9,10},{10,9},{11,... | collective-permute-start | bytes 319496 | tf_op jit(solution)/shard_map/ppermute | solution.py:354
  112.2 6.0 %collective-permute-start.13 = (f32[2,104,128]{2,1,0:T(8,128)S(1)}, f32[2,104,128]{2,1,0:T(8,128)S(1)}, u32[]{:S(2)}, u32[]{:S(2)}) collective-permute-start(f32[2,104,128]{2,1,0:T(8,128)S(1)} %get-tuple-element.58), channel_id=1, source_target_pairs={{0,1},{1,0},{2,3},{3,2},{4,5},{5,4},{6,7},{7,6},{8,9},{9,8},{10,11... | collective-permute-start | bytes 319496 | tf_op jit(solution)/shard_map/ppermute | solution.py:355
  118.7 5.9 %collective-permute-start.14 = (f32[2,4,8,128]{3,2,1,0:T(8,128)S(1)}, f32[2,4,8,128]{3,2,1,0:T(8,128)S(1)}, u32[]{:S(2)}, u32[]{:S(2)}) collective-permute-start(f32[2,4,8,128]{3,2,1,0:T(8,128)S(1)} %get-tuple-element.60.refs_0_), channel_id=1, source_target_pairs={{0,64},{64,128},{128,192},{192,256},{256,320},{320,384},{384,448},... | collective-permute-start | bytes 98312 | tf_op jit(solution)/shard_map/ppermute | solution.py:412
  124.6 8.1 %collective-permute-start.15 = (f32[2,104,128]{2,1,0:T(8,128)S(1)}, f32[2,104,128]{2,1,0:T(8,128)S(1)}, u32[]{:S(2)}, u32[]{:S(2)}) collective-permute-start(f32[2,104,128]{2,1,0:T(8,128)S(1)} %get-tuple-element.61), channel_id=1, source_target_pairs={{1,2},{2,1},{3,4},{4,3},{5,6},{6,5},{7,8},{8,7},{9,10},{10,9},{11,... | collective-permute-start | bytes 319496 | tf_op jit(solution)/shard_map/ppermute | solution.py:354
  126.8 5.9 %collective-permute-start.16 = (f32[2,104,128]{2,1,0:T(8,128)S(1)}, f32[2,104,128]{2,1,0:T(8,128)S(1)}, u32[]{:S(2)}, u32[]{:S(2)}) collective-permute-start(f32[2,104,128]{2,1,0:T(8,128)S(1)} %get-tuple-element.62), channel_id=1, source_target_pairs={{0,1},{1,0},{2,3},{3,2},{4,5},{5,4},{6,7},{7,6},{8,9},{9,8},{10,11... | collective-permute-start | bytes 319496 | tf_op jit(solution)/shard_map/ppermute | solution.py:355
  133.2 8.2 %collective-permute-start.17 = (f32[2,4,8,128]{3,2,1,0:T(8,128)S(1)}, f32[2,4,8,128]{3,2,1,0:T(8,128)S(1)}, u32[]{:S(2)}, u32[]{:S(2)}) collective-permute-start(f32[2,4,8,128]{3,2,1,0:T(8,128)S(1)} %get-tuple-element.64.refs_0_), channel_id=1, source_target_pairs={{0,32},{64,0},{128,64},{192,128},{256,192},{320,256},{384,320},{44... | collective-permute-start | bytes 98312 | tf_op jit(solution)/shard_map/ppermute | solution.py:412
  141.4 8.1 %collective-permute-start.18 = (f32[2,104,128]{2,1,0:T(8,128)S(1)}, f32[2,104,128]{2,1,0:T(8,128)S(1)}, u32[]{:S(2)}, u32[]{:S(2)}) collective-permute-start(f32[2,104,128]{2,1,0:T(8,128)S(1)} %get-tuple-element.65), channel_id=1, source_target_pairs={{1,2},{2,1},{3,4},{4,3},{5,6},{6,5},{7,8},{8,7},{9,10},{10,9},{11,... | collective-permute-start | bytes 319496 | tf_op jit(solution)/shard_map/ppermute | solution.py:354
  143.4 6.2 %collective-permute-start.19 = (f32[2,104,128]{2,1,0:T(8,128)S(1)}, f32[2,104,128]{2,1,0:T(8,128)S(1)}, u32[]{:S(2)}, u32[]{:S(2)}) collective-permute-start(f32[2,104,128]{2,1,0:T(8,128)S(1)} %get-tuple-element.66), channel_id=1, source_target_pairs={{0,1},{1,0},{2,3},{3,2},{4,5},{5,4},{6,7},{7,6},{8,9},{9,8},{10,11... | collective-permute-start | bytes 319496 | tf_op jit(solution)/shard_map/ppermute | solution.py:355

commit v7 on v4

--- a/solution.py
+++ b/solution.py
@@ -108,21 +108,22 @@
     return sum(w[j] * states_ref[j, f, p] for j in range(3))
 
 
-def start_kernel(flags_ref, states_ref, first_ref, far_ref, near_ref, start_ref):
+def start_kernel(flags_ref, states_ref, first_edges_ref, far_ref, near_ref):
+    sides = (0, states_ref.shape[2] - 1)
+    for f in range(2):
+        for way in range(2):
+            put_edges(flags_ref, far_ref, near_ref, (way, f), *[combined(states_ref, way, f, p) for p in sides])
+        ends = [states_ref[2, f, p] for p in sides]
+        ends = [jnp.where(flag(flags_ref, last, x), first_edges_ref[f, e], x) for e, x in enumerate(ends)]
+        put_edges(flags_ref, far_ref, near_ref, (2, f), *ends)
+
+
+def old_kernel(flags_ref, states_ref, first_ref, part_ref, start_ref):
     depth = states_ref.shape[2]
-    for f in range(2):
-        for p in range(depth):
+    for p in range(depth):
+        for f in range(2):
             own = states_ref[2, f, p]
             start_ref[f, p] = jnp.where(flag(flags_ref, last, own), first_ref[f, p], own)
-        for way in range(2):
-            head, tail = combined(states_ref, way, f, 0), combined(states_ref, way, f, depth - 1)
-            put_edges(flags_ref, far_ref, near_ref, (way, f), head, tail)
-        put_edges(flags_ref, far_ref, near_ref, (2, f), start_ref[f, 0], start_ref[f, depth - 1])
-
-
-def old_kernel(states_ref, part_ref):
-    depth = states_ref.shape[2]
-    for p in range(depth):
         react = [reactions(states_ref[j, 0, p], states_ref[j, 1, p]) for j in range(3)]
         for way in range(2):
             for f in range(2):
@@ -363,9 +364,10 @@
 
     back_one = [(i, (i - 1) % count) for i in range(count)]
     message = shape(3, 2, rows, cols)
-    far, near, fine0 = call(start_kernel, [message, message, grid], flags, slab, first_start)
+    first_edges = first_start[:, :: depth - 1]
+    far, near = call(start_kernel, [message] * 2, flags, slab, first_edges)
     far, near = swapped(far, near)
-    (part,) = call(old_kernel, [shape(2, 2, depth, rows, cols)], slab)
+    part, fine0 = call(old_kernel, [shape(2, 2, depth, rows, cols), grid], flags, slab, first_start)
     old_first, old_second = call(sum_kernel, [grid] * 2, flags, part, far, near)
     old_first = lax.ppermute(old_first, "tm", back_one)
     old_second = lax.ppermute(old_second, "tm", back_one)

time: 176 us -> 176 us (level)
  no operation moved by 1% of the time
where the time goes in v7:
time: 176 us; the launch traced here: 175 us
  starting transfers between devices  65.6 us (37%)
  blocking collectives  64.7 us (37%)
  waiting for transfers between devices  35.5 us (20%)
  Pallas kernels  6.44 us (4%)
  local copies, waits for them, and re-layouts  2.61 us (1%)
    all_to_all x1, blocking collectives, local(): held = lax.all_to_all(send, 'tm', 0, 0, tiled=True)  35.9 us
    ppermute x7, starting transfers between devices, swapped(): lax.ppermute(near, 'space', [(i + j, i + 1 - j) for i in range(0, count,...  35.5 us
    all_to_all x1, blocking collectives, local(): back = lax.all_to_all(jnp.concatenate(ends), 'tm', 0, 0, tiled=True)  28.8 us
    ppermute x7, starting transfers between devices, swapped(): lax.ppermute(far, 'space', [((i + j) % count, (i + 1 - j) % count) for i...  13.8 us
    ppermute x3, waiting for transfers between devices, local(): state = [end[0], lax.ppermute(end[0], 'tm', route)]  12.9 us
    ppermute x1, waiting for transfers between devices, local(): old_first = lax.ppermute(old_first, 'tm', back_one)  9 us
    ppermute x1, starting transfers between devices, local(): old_first = lax.ppermute(old_first, 'tm', back_one)  6.94 us
    pallas_call x15, Pallas kernels, call(): pl.pallas_call(kernel, out_shape=tuple(out_shapes), in_specs=[pl.BlockSpe...  6.44 us
  transfers between devices with their start and end apart: 19, of which 12 were waited for; matrix products, arithmetic and copies ran while one was open for 0% of the time, Pallas kernels for 1%

profile of v7, /device:TPU:194, one launch (start us, length us, event | category | flops | bytes accessed | tf_op | source)
XLA Modules:
  0.0 175.3 jit_solution(16428371663944304014)
XLA Ops:
  2.8 1.9 %collective-permute-start = (f32[3,2,128,128]{3,2,1,0:T(8,128)S(1)}, f32[3,2,128,128]{3,2,1,0:T(8,128)S(1)}, u32[]{:S(2)}, u32[]{:S(2)}) collective-permute-start(f32[3,2,128,128]{3,2,1,0:T(8,128)S(1)} %get-tuple-element.37), channel_id=1, source_target_pairs={{1,2},{2,1},{3,4},{4,3},{5,6},{6,5},{7,8},{8,7},{9,10},{10,9},{11,... | collective-permute-start | bytes 1179656 | tf_op jit(solution)/shard_map/ppermute | solution.py:342
  4.7 5.6 %collective-permute-start.1 = (f32[3,2,128,128]{3,2,1,0:T(8,128)S(1)}, f32[3,2,128,128]{3,2,1,0:T(8,128)S(1)}, u32[]{:S(2)}, u32[]{:S(2)}) collective-permute-start(f32[3,2,128,128]{3,2,1,0:T(8,128)S(1)} %get-tuple-element.38), channel_id=1, source_target_pairs={{0,1},{1,0},{2,3},{3,2},{4,5},{5,4},{6,7},{7,6},{8,9},{9,8},{10,11... | collective-permute-start | bytes 1179656 | tf_op jit(solution)/shard_map/ppermute | solution.py:343
  11.8 4.3 %collective-permute-done.far_ref = f32[3,2,128,128]{3,2,1,0:T(8,128)S(1)} collective-permute-done((f32[3,2,128,128]{3,2,1,0:T(8,128)S(1)}, f32[3,2,128,128]{3,2,1,0:T(8,128)S(1)}, u32[]{:S(2)}, u32[]{:S(2)}) %collective-permute-start) | collective-permute-done | bytes 393248 | tf_op jit(solution)/shard_map/ppermute | solution.py:342
  16.2 6.9 %collective-permute-start.3 = (f32[2,4,128,128]{3,2,1,0:T(8,128)S(1)}, f32[2,4,128,128]{3,2,1,0:T(8,128)S(1)}, u32[]{:S(2)}, u32[]{:S(2)}) collective-permute-start(f32[2,4,128,128]{3,2,1,0:T(8,128)S(1)} %get-tuple-element.40), channel_id=1, source_target_pairs={{0,480},{32,0},{64,32},{96,64},{128,96},{160,128},{192,160},{224,1... | collective-permute-start | bytes 1572872 | tf_op jit(solution)/shard_map/ppermute | solution.py:372
  23.1 3.3 %collective-permute-start.2 = (f32[2,4,128,128]{3,2,1,0:T(8,128)S(1)}, f32[2,4,128,128]{3,2,1,0:T(8,128)S(1)}, u32[]{:S(2)}, u32[]{:S(2)}) collective-permute-start(f32[2,4,128,128]{3,2,1,0:T(8,128)S(1)} %get-tuple-element.39), channel_id=1, source_target_pairs={{0,480},{32,0},{64,32},{96,64},{128,96},{160,128},{192,160},{224,1... | collective-permute-start | bytes 1572872 | tf_op jit(solution)/shard_map/ppermute | solution.py:373
  26.5 9.0 %collective-permute-done.3.old_ref = f32[2,4,128,128]{3,2,1,0:T(8,128)S(1)} collective-permute-done((f32[2,4,128,128]{3,2,1,0:T(8,128)S(1)}, f32[2,4,128,128]{3,2,1,0:T(8,128)S(1)}, u32[]{:S(2)}, u32[]{:S(2)}) %collective-permute-start.3) | collective-permute-done | bytes 524320 | tf_op jit(solution)/shard_map/ppermute | solution.py:372
  35.9 1.9 %collective-permute-start.4 = (f32[2,128,128]{2,1,0:T(8,128)S(1)}, f32[2,128,128]{2,1,0:T(8,128)S(1)}, u32[]{:S(2)}, u32[]{:S(2)}) collective-permute-start(f32[2,128,128]{2,1,0:T(8,128)S(1)} %get-tuple-element.43), channel_id=1, source_target_pairs={{1,2},{2,1},{3,4},{4,3},{5,6},{6,5},{7,8},{8,7},{9,10},{10,9},{11,... | collective-permute-start | bytes 393224 | tf_op jit(solution)/shard_map/ppermute | solution.py:342
  37.9 3.6 %collective-permute-start.5 = (f32[2,128,128]{2,1,0:T(8,128)S(1)}, f32[2,128,128]{2,1,0:T(8,128)S(1)}, u32[]{:S(2)}, u32[]{:S(2)}) collective-permute-start(f32[2,128,128]{2,1,0:T(8,128)S(1)} %get-tuple-element.44), channel_id=1, source_target_pairs={{0,1},{1,0},{2,3},{3,2},{4,5},{5,4},{6,7},{7,6},{8,9},{9,8},{10,11... | collective-permute-start | bytes 393224 | tf_op jit(solution)/shard_map/ppermute | solution.py:343
  41.4 3.8 %collective-permute-done.2.old_ref = f32[2,4,128,128]{3,2,1,0:T(8,128)S(1)} collective-permute-done((f32[2,4,128,128]{3,2,1,0:T(8,128)S(1)}, f32[2,4,128,128]{3,2,1,0:T(8,128)S(1)}, u32[]{:S(2)}, u32[]{:S(2)}) %collective-permute-start.2) | collective-permute-done | bytes 524320 | tf_op jit(solution)/shard_map/ppermute | solution.py:373
  46.6 2.3 %collective-permute-start.6 = (f32[2,128,128]{2,1,0:T(8,128)S(1)}, f32[2,128,128]{2,1,0:T(8,128)S(1)}, u32[]{:S(2)}, u32[]{:S(2)}) collective-permute-start(f32[2,128,128]{2,1,0:T(8,128)S(1)} %get-tuple-element.47), channel_id=1, source_target_pairs={{1,2},{2,1},{3,4},{4,3},{5,6},{6,5},{7,8},{8,7},{9,10},{10,9},{11,... | collective-permute-start | bytes 393224 | tf_op jit(solution)/shard_map/ppermute | solution.py:342
  48.9 5.2 %collective-permute-start.7 = (f32[2,128,128]{2,1,0:T(8,128)S(1)}, f32[2,128,128]{2,1,0:T(8,128)S(1)}, u32[]{:S(2)}, u32[]{:S(2)}) collective-permute-start(f32[2,128,128]{2,1,0:T(8,128)S(1)} %get-tuple-element.48), channel_id=1, source_target_pairs={{0,1},{1,0},{2,3},{3,2},{4,5},{5,4},{6,7},{7,6},{8,9},{9,8},{10,11... | collective-permute-start | bytes 393224 | tf_op jit(solution)/shard_map/ppermute | solution.py:343
  55.8 35.9 %all_to_all.10 = f32[16,2,56,128]{3,2,1,0:T(8,128)S(1)} all-to-all(f32[16,2,56,128]{3,2,1,0:T(8,128)S(1)} %get-tuple-element.50), channel_id=1, replica_groups=mesh['tm'=16,'space'=32] {'tm'}, dimensions={0} | all-to-all | bytes 1835008 | tf_op jit(solution)/shard_map/all_to_all | solution.py:390
  91.7 1.9 %collective-permute-start.8 = (f32[2,64,128]{2,1,0:T(8,128)S(1)}, f32[2,64,128]{2,1,0:T(8,128)S(1)}, u32[]{:S(2)}, u32[]{:S(2)}) collective-permute-start(f32[2,64,128]{2,1,0:T(8,128)S(1)} %get-tuple-element.51), channel_id=1, source_target_pairs={{1,2},{2,1},{3,4},{4,3},{5,6},{6,5},{7,8},{8,7},{9,10},{10,9},{11,... | collective-permute-start | bytes 196616 | tf_op jit(solution)/shard_map/ppermute | solution.py:342
  93.7 5.7 %collective-permute-start.9 = (f32[2,64,128]{2,1,0:T(8,128)S(1)}, f32[2,64,128]{2,1,0:T(8,128)S(1)}, u32[]{:S(2)}, u32[]{:S(2)}) collective-permute-start(f32[2,64,128]{2,1,0:T(8,128)S(1)} %get-tuple-element.52), channel_id=1, source_target_pairs={{0,1},{1,0},{2,3},{3,2},{4,5},{5,4},{6,7},{7,6},{8,9},{9,8},{10,11... | collective-permute-start | bytes 196616 | tf_op jit(solution)/shard_map/ppermute | solution.py:343
  100.5 1.9 %collective-permute-start.10 = (f32[2,4,8,128]{3,2,1,0:T(8,128)S(1)}, f32[2,4,8,128]{3,2,1,0:T(8,128)S(1)}, u32[]{:S(2)}, u32[]{:S(2)}) collective-permute-start(f32[2,4,8,128]{3,2,1,0:T(8,128)S(1)} %get-tuple-element.54.refs_0_), channel_id=1, source_target_pairs={{0,32},{64,0},{128,64},{192,128},{256,192},{320,256},{384,320},{44... | collective-permute-start | bytes 98312 | tf_op jit(solution)/shard_map/ppermute | solution.py:398
  102.5 3.8 %collective-permute-done.10.refs_1_ = f32[2,4,8,128]{3,2,1,0:T(8,128)S(1)} collective-permute-done((f32[2,4,8,128]{3,2,1,0:T(8,128)S(1)}, f32[2,4,8,128]{3,2,1,0:T(8,128)S(1)}, u32[]{:S(2)}, u32[]{:S(2)}) %collective-permute-start.10) | collective-permute-done | bytes 32800 | tf_op jit(solution)/shard_map/ppermute | solution.py:398
  106.4 1.9 %collective-permute-start.11 = (f32[2,104,128]{2,1,0:T(8,128)S(1)}, f32[2,104,128]{2,1,0:T(8,128)S(1)}, u32[]{:S(2)}, u32[]{:S(2)}) collective-permute-start(f32[2,104,128]{2,1,0:T(8,128)S(1)} %get-tuple-element.55), channel_id=1, source_target_pairs={{1,2},{2,1},{3,4},{4,3},{5,6},{6,5},{7,8},{8,7},{9,10},{10,9},{11,... | collective-permute-start | bytes 319496 | tf_op jit(solution)/shard_map/ppermute | solution.py:342
  108.3 4.9 %collective-permute-start.12 = (f32[2,104,128]{2,1,0:T(8,128)S(1)}, f32[2,104,128]{2,1,0:T(8,128)S(1)}, u32[]{:S(2)}, u32[]{:S(2)}) collective-permute-start(f32[2,104,128]{2,1,0:T(8,128)S(1)} %get-tuple-element.56), channel_id=1, source_target_pairs={{0,1},{1,0},{2,3},{3,2},{4,5},{5,4},{6,7},{7,6},{8,9},{9,8},{10,11... | collective-permute-start | bytes 319496 | tf_op jit(solution)/shard_map/ppermute | solution.py:343
  114.6 2.2 %collective-permute-start.13 = (f32[2,4,8,128]{3,2,1,0:T(8,128)S(1)}, f32[2,4,8,128]{3,2,1,0:T(8,128)S(1)}, u32[]{:S(2)}, u32[]{:S(2)}) collective-permute-start(f32[2,4,8,128]{3,2,1,0:T(8,128)S(1)} %get-tuple-element.58.refs_0_), channel_id=1, source_target_pairs={{0,64},{64,128},{128,192},{192,256},{256,320},{320,384},{384,448},... | collective-permute-start | bytes 98312 | tf_op jit(solution)/shard_map/ppermute | solution.py:398
  116.8 5.2 %collective-permute-done.13.refs_1_ = f32[2,4,8,128]{3,2,1,0:T(8,128)S(1)} collective-permute-done((f32[2,4,8,128]{3,2,1,0:T(8,128)S(1)}, f32[2,4,8,128]{3,2,1,0:T(8,128)S(1)}, u32[]{:S(2)}, u32[]{:S(2)}) %collective-permute-start.13) | collective-permute-done | bytes 32800 | tf_op jit(solution)/shard_map/ppermute | solution.py:398
  123.9 5.3 %collective-permute-start.15 = (f32[2,104,128]{2,1,0:T(8,128)S(1)}, f32[2,104,128]{2,1,0:T(8,128)S(1)}, u32[]{:S(2)}, u32[]{:S(2)}) collective-permute-start(f32[2,104,128]{2,1,0:T(8,128)S(1)} %get-tuple-element.60), channel_id=1, source_target_pairs={{0,1},{1,0},{2,3},{3,2},{4,5},{5,4},{6,7},{7,6},{8,9},{9,8},{10,11... | collective-permute-start | bytes 319496 | tf_op jit(solution)/shard_map/ppermute | solution.py:343
  132.5 3.9 %collective-permute-done.16.refs_1_ = f32[2,4,8,128]{3,2,1,0:T(8,128)S(1)} collective-permute-done((f32[2,4,8,128]{3,2,1,0:T(8,128)S(1)}, f32[2,4,8,128]{3,2,1,0:T(8,128)S(1)}, u32[]{:S(2)}, u32[]{:S(2)}) %collective-permute-start.16) | collective-permute-done | bytes 32800 | tf_op jit(solution)/shard_map/ppermute | solution.py:398
  138.3 5.4 %collective-permute-start.18 = (f32[2,104,128]{2,1,0:T(8,128)S(1)}, f32[2,104,128]{2,1,0:T(8,128)S(1)}, u32[]{:S(2)}, u32[]{:S(2)}) collective-permute-start(f32[2,104,128]{2,1,0:T(8,128)S(1)} %get-tuple-element.64), channel_id=1, source_target_pairs={{0,1},{1,0},{2,3},{3,2},{4,5},{5,4},{6,7},{7,6},{8,9},{9,8},{10,11... | collective-permute-start | bytes 319496 | tf_op jit(solution)/shard_map/ppermute | solution.py:343
  145.1 28.8 %all_to_all.11.come_ref = f32[16,2,6,8,128]{4,3,2,1,0:T(8,128)S(1)} all-to-all(f32[16,2,6,8,128]{4,3,2,1,0:T(8,128)S(1)} %pad_maximum_fusion), channel_id=1, replica_groups=mesh['tm'=16,'space'=32] {'tm'}, dimensions={0} | all-to-all | bytes 1572864 | tf_op jit(solution)/shard_map/all_to_all | solution.py:411
  (44 shorter events, 20.4 us)
Async XLA Ops:
  0.0 10.3 %copy-start.1 = (f32[2,4,128,128]{3,2,1,0:T(8,128)S(1)}, f32[2,4,128,128]{3,2,1,0:T(8,128)}, u32[]{:S(2)}) copy-start(f32[2,4,128,128]{3,2,1,0:T(8,128)} %first_ref.1) | copy-start | bytes 1572868
  1.2 1.4 copy-start
  2.8 13.3 %collective-permute-start = (f32[3,2,128,128]{3,2,1,0:T(8,128)S(1)}, f32[3,2,128,128]{3,2,1,0:T(8,128)S(1)}, u32[]{:S(2)}, u32[]{:S(2)}) collective-permute-start(f32[3,2,128,128]{3,2,1,0:T(8,128)S(1)} %get-tuple-element.37), channel_id=1, source_target_pairs={{1,2},{2,1},{3,4},{4,3},{5,6},{6,5},{7,8},{8,7},{9,10},{10,9},{11,... | collective-permute-start | bytes 1179656 | tf_op jit(solution)/shard_map/ppermute | solution.py:342
  4.7 11.4 %collective-permute-start.1 = (f32[3,2,128,128]{3,2,1,0:T(8,128)S(1)}, f32[3,2,128,128]{3,2,1,0:T(8,128)S(1)}, u32[]{:S(2)}, u32[]{:S(2)}) collective-permute-start(f32[3,2,128,128]{3,2,1,0:T(8,128)S(1)} %get-tuple-element.38), channel_id=1, source_target_pairs={{0,1},{1,0},{2,3},{3,2},{4,5},{5,4},{6,7},{7,6},{8,9},{9,8},{10,11... | collective-permute-start | bytes 1179656 | tf_op jit(solution)/shard_map/ppermute | solution.py:343
  16.2 19.3 %collective-permute-start.3 = (f32[2,4,128,128]{3,2,1,0:T(8,128)S(1)}, f32[2,4,128,128]{3,2,1,0:T(8,128)S(1)}, u32[]{:S(2)}, u32[]{:S(2)}) collective-permute-start(f32[2,4,128,128]{3,2,1,0:T(8,128)S(1)} %get-tuple-element.40), channel_id=1, source_target_pairs={{0,480},{32,0},{64,32},{96,64},{128,96},{160,128},{192,160},{224,1... | collective-permute-start | bytes 1572872 | tf_op jit(solution)/shard_map/ppermute | solution.py:372
  23.1 22.1 %collective-permute-start.2 = (f32[2,4,128,128]{3,2,1,0:T(8,128)S(1)}, f32[2,4,128,128]{3,2,1,0:T(8,128)S(1)}, u32[]{:S(2)}, u32[]{:S(2)}) collective-permute-start(f32[2,4,128,128]{3,2,1,0:T(8,128)S(1)} %get-tuple-element.39), channel_id=1, source_target_pairs={{0,480},{32,0},{64,32},{96,64},{128,96},{160,128},{192,160},{224,1... | collective-permute-start | bytes 1572872 | tf_op jit(solution)/shard_map/ppermute | solution.py:373
  35.9 10.2 %collective-permute-start.4 = (f32[2,128,128]{2,1,0:T(8,128)S(1)}, f32[2,128,128]{2,1,0:T(8,128)S(1)}, u32[]{:S(2)}, u32[]{:S(2)}) collective-permute-start(f32[2,128,128]{2,1,0:T(8,128)S(1)} %get-tuple-element.43), channel_id=1, source_target_pairs={{1,2},{2,1},{3,4},{4,3},{5,6},{6,5},{7,8},{8,7},{9,10},{10,9},{11,... | collective-permute-start | bytes 393224 | tf_op jit(solution)/shard_map/ppermute | solution.py:342
  37.9 8.3 %collective-permute-start.5 = (f32[2,128,128]{2,1,0:T(8,128)S(1)}, f32[2,128,128]{2,1,0:T(8,128)S(1)}, u32[]{:S(2)}, u32[]{:S(2)}) collective-permute-start(f32[2,128,128]{2,1,0:T(8,128)S(1)} %get-tuple-element.44), channel_id=1, source_target_pairs={{0,1},{1,0},{2,3},{3,2},{4,5},{5,4},{6,7},{7,6},{8,9},{9,8},{10,11... | collective-permute-start | bytes 393224 | tf_op jit(solution)/shard_map/ppermute | solution.py:343
  46.6 7.5 %collective-permute-start.6 = (f32[2,128,128]{2,1,0:T(8,128)S(1)}, f32[2,128,128]{2,1,0:T(8,128)S(1)}, u32[]{:S(2)}, u32[]{:S(2)}) collective-permute-start(f32[2,128,128]{2,1,0:T(8,128)S(1)} %get-tuple-element.47), channel_id=1, source_target_pairs={{1,2},{2,1},{3,4},{4,3},{5,6},{6,5},{7,8},{8,7},{9,10},{10,9},{11,... | collective-permute-start | bytes 393224 | tf_op jit(solution)/shard_map/ppermute | solution.py:342
  48.9 6.2 %collective-permute-start.7 = (f32[2,128,128]{2,1,0:T(8,128)S(1)}, f32[2,128,128]{2,1,0:T(8,128)S(1)}, u32[]{:S(2)}, u32[]{:S(2)}) collective-permute-start(f32[2,128,128]{2,1,0:T(8,128)S(1)} %get-tuple-element.48), channel_id=1, source_target_pairs={{0,1},{1,0},{2,3},{3,2},{4,5},{5,4},{6,7},{7,6},{8,9},{9,8},{10,11... | collective-permute-start | bytes 393224 | tf_op jit(solution)/shard_map/ppermute | solution.py:343
  91.7 7.6 %collective-permute-start.8 = (f32[2,64,128]{2,1,0:T(8,128)S(1)}, f32[2,64,128]{2,1,0:T(8,128)S(1)}, u32[]{:S(2)}, u32[]{:S(2)}) collective-permute-start(f32[2,64,128]{2,1,0:T(8,128)S(1)} %get-tuple-element.51), channel_id=1, source_target_pairs={{1,2},{2,1},{3,4},{4,3},{5,6},{6,5},{7,8},{8,7},{9,10},{10,9},{11,... | collective-permute-start | bytes 196616 | tf_op jit(solution)/shard_map/ppermute | solution.py:342
  93.7 6.6 %collective-permute-start.9 = (f32[2,64,128]{2,1,0:T(8,128)S(1)}, f32[2,64,128]{2,1,0:T(8,128)S(1)}, u32[]{:S(2)}, u32[]{:S(2)}) collective-permute-start(f32[2,64,128]{2,1,0:T(8,128)S(1)} %get-tuple-element.52), channel_id=1, source_target_pairs={{0,1},{1,0},{2,3},{3,2},{4,5},{5,4},{6,7},{7,6},{8,9},{9,8},{10,11... | collective-permute-start | bytes 196616 | tf_op jit(solution)/shard_map/ppermute | solution.py:343
  100.5 5.8 %collective-permute-start.10 = (f32[2,4,8,128]{3,2,1,0:T(8,128)S(1)}, f32[2,4,8,128]{3,2,1,0:T(8,128)S(1)}, u32[]{:S(2)}, u32[]{:S(2)}) collective-permute-start(f32[2,4,8,128]{3,2,1,0:T(8,128)S(1)} %get-tuple-element.54.refs_0_), channel_id=1, source_target_pairs={{0,32},{64,0},{128,64},{192,128},{256,192},{320,256},{384,320},{44... | collective-permute-start | bytes 98312 | tf_op jit(solution)/shard_map/ppermute | solution.py:398
  106.4 6.8 %collective-permute-start.11 = (f32[2,104,128]{2,1,0:T(8,128)S(1)}, f32[2,104,128]{2,1,0:T(8,128)S(1)}, u32[]{:S(2)}, u32[]{:S(2)}) collective-permute-start(f32[2,104,128]{2,1,0:T(8,128)S(1)} %get-tuple-element.55), channel_id=1, source_target_pairs={{1,2},{2,1},{3,4},{4,3},{5,6},{6,5},{7,8},{8,7},{9,10},{10,9},{11,... | collective-permute-start | bytes 319496 | tf_op jit(solution)/shard_map/ppermute | solution.py:342
  108.3 5.8 %collective-permute-start.12 = (f32[2,104,128]{2,1,0:T(8,128)S(1)}, f32[2,104,128]{2,1,0:T(8,128)S(1)}, u32[]{:S(2)}, u32[]{:S(2)}) collective-permute-start(f32[2,104,128]{2,1,0:T(8,128)S(1)} %get-tuple-element.56), channel_id=1, source_target_pairs={{0,1},{1,0},{2,3},{3,2},{4,5},{5,4},{6,7},{7,6},{8,9},{9,8},{10,11... | collective-permute-start | bytes 319496 | tf_op jit(solution)/shard_map/ppermute | solution.py:343
  114.6 7.3 %collective-permute-start.13 = (f32[2,4,8,128]{3,2,1,0:T(8,128)S(1)}, f32[2,4,8,128]{3,2,1,0:T(8,128)S(1)}, u32[]{:S(2)}, u32[]{:S(2)}) collective-permute-start(f32[2,4,8,128]{3,2,1,0:T(8,128)S(1)} %get-tuple-element.58.refs_0_), channel_id=1, source_target_pairs={{0,64},{64,128},{128,192},{192,256},{256,320},{320,384},{384,448},... | collective-permute-start | bytes 98312 | tf_op jit(solution)/shard_map/ppermute | solution.py:398
  122.0 7.2 %collective-permute-start.14 = (f32[2,104,128]{2,1,0:T(8,128)S(1)}, f32[2,104,128]{2,1,0:T(8,128)S(1)}, u32[]{:S(2)}, u32[]{:S(2)}) collective-permute-start(f32[2,104,128]{2,1,0:T(8,128)S(1)} %get-tuple-element.59), channel_id=1, source_target_pairs={{1,2},{2,1},{3,4},{4,3},{5,6},{6,5},{7,8},{8,7},{9,10},{10,9},{11,... | collective-permute-start | bytes 319496 | tf_op jit(solution)/shard_map/ppermute | solution.py:342
  123.9 6.2 %collective-permute-start.15 = (f32[2,104,128]{2,1,0:T(8,128)S(1)}, f32[2,104,128]{2,1,0:T(8,128)S(1)}, u32[]{:S(2)}, u32[]{:S(2)}) collective-permute-start(f32[2,104,128]{2,1,0:T(8,128)S(1)} %get-tuple-element.60), channel_id=1, source_target_pairs={{0,1},{1,0},{2,3},{3,2},{4,5},{5,4},{6,7},{7,6},{8,9},{9,8},{10,11... | collective-permute-start | bytes 319496 | tf_op jit(solution)/shard_map/ppermute | solution.py:343
  130.5 5.8 %collective-permute-start.16 = (f32[2,4,8,128]{3,2,1,0:T(8,128)S(1)}, f32[2,4,8,128]{3,2,1,0:T(8,128)S(1)}, u32[]{:S(2)}, u32[]{:S(2)}) collective-permute-start(f32[2,4,8,128]{3,2,1,0:T(8,128)S(1)} %get-tuple-element.62.refs_0_), channel_id=1, source_target_pairs={{0,32},{64,0},{128,64},{192,128},{256,192},{320,256},{384,320},{44... | collective-permute-start | bytes 98312 | tf_op jit(solution)/shard_map/ppermute | solution.py:398
  136.4 7.3 %collective-permute-start.17 = (f32[2,104,128]{2,1,0:T(8,128)S(1)}, f32[2,104,128]{2,1,0:T(8,128)S(1)}, u32[]{:S(2)}, u32[]{:S(2)}) collective-permute-start(f32[2,104,128]{2,1,0:T(8,128)S(1)} %get-tuple-element.63), channel_id=1, source_target_pairs={{1,2},{2,1},{3,4},{4,3},{5,6},{6,5},{7,8},{8,7},{9,10},{10,9},{11,... | collective-permute-start | bytes 319496 | tf_op jit(solution)/shard_map/ppermute | solution.py:342
  138.3 6.3 %collective-permute-start.18 = (f32[2,104,128]{2,1,0:T(8,128)S(1)}, f32[2,104,128]{2,1,0:T(8,128)S(1)}, u32[]{:S(2)}, u32[]{:S(2)}) collective-permute-start(f32[2,104,128]{2,1,0:T(8,128)S(1)} %get-tuple-element.64), channel_id=1, source_target_pairs={{0,1},{1,0},{2,3},{3,2},{4,5},{5,4},{6,7},{7,6},{8,9},{9,8},{10,11... | collective-permute-start | bytes 319496 | tf_op jit(solution)/shard_map/ppermute | solution.py:343
